TPU v7x, 32 devices: a whole 2x2x4 slice. The times are simulated.
32 devices in a mesh: pipe: 4 (over x, core), bundle: 8 (over z, y).
Axes of the slice: x: 2, y: 2, z: 4, core: 2. Of those that a mesh axis runs over, the one named last changes fastest.
Arguments:
- act_fwd: bfloat16 [4, 512, 8192], P('pipe', 'bundle'), may hold values from -6 to 6
- grad_in: bfloat16 [4, 512, 8192], P('pipe', 'bundle'), may hold values from -6 to 6
- w_gate: bfloat16 [4, 8192, 1024], P('pipe', None, 'bundle'), may hold values from -0.0625 to 0.0625
- w_up: bfloat16 [4, 8192, 1024], P('pipe', None, 'bundle'), may hold values from -0.0625 to 0.0625
- w_down: bfloat16 [4, 1024, 8192], P('pipe', 'bundle'), may hold values from -0.1875 to 0.1875
- saved_gate: bfloat16 [4, 512, 1024], P('pipe', None, 'bundle'), may hold values from -6 to 6
- saved_up: bfloat16 [4, 512, 1024], P('pipe', None, 'bundle'), may hold values from -6 to 6
- mask_fwd: int32 [4, 32, 8], P('pipe'), may hold values from 0 to 1, as said below
- mask_bwd: int32 [4, 32, 8], P('pipe'), may hold values from 0 to 1, as said below
Outputs:
- next_forward: bfloat16 [4, 512, 8192], P('pipe', 'bundle')
- next_backward: bfloat16 [4, 512, 8192], P('pipe', 'bundle')
Inputs may be any that keep to these rules, and one draw needn't show every extreme that they name: `mask_fwd`: within the 4 row blocks of one device's tokens (blocks k * 4 to k * 4 + 3), each bundle is active in at most one. `mask_bwd`: within the 4 row blocks of one device's tokens (blocks k * 4 to k * 4 + 3), each bundle is active in at most one.
All inputs are finite; a program needn't handle non-finite values.
Results may differ from a plain program's by a relative error of at most 0.0033.
Values may be sent and summed in bfloat16 or wider, within the bound.
No kernel may reach another device: no remote copies, remote signals or barrier semaphores. Data moves between devices by JAX's collectives and lax.ppermute only.
A program may use at most 128 MiB of HBM per device.

v0:
```python
import jax
import jax.numpy as jnp
from jax import lax
from jax.sharding import PartitionSpec as P

BLOCK = 16


def shifted(value, axis, steps):
    count = lax.axis_size(axis)
    pairs = [(source, (source + steps) % count) for source in range(count)]
    return lax.ppermute(value, axis, pairs)


def contract_last(left, right):
    return lax.dot_general(
        left, right, (((1,), (1,)), ((), ())), preferred_element_type=jnp.float32
    )


def sender_select(mask_all, device, blocks_dev):
    own_rows = lax.dynamic_slice_in_dim(mask_all[0], device * blocks_dev, blocks_dev, 0)
    return own_rows.T.astype(jnp.bfloat16)


def owner_select(mask_all, device, owners, blocks_dev):
    column = lax.dynamic_slice_in_dim(mask_all[0], device, 1, 1)[:, 0]
    return column.reshape(owners, blocks_dev).astype(jnp.bfloat16)


def pack_rows(rows, select, blocks_dev):
    width = rows.shape[-1]
    stacked = rows.reshape(blocks_dev, BLOCK, width)
    packed = jnp.einsum("bj,jtd->btd", select, stacked, preferred_element_type=jnp.float32)
    return packed.astype(jnp.bfloat16)


def pick_saved(saved, select, owners, blocks_dev):
    width = saved.shape[-1]
    stacked = saved.reshape(owners, blocks_dev, BLOCK, width)
    picked = jnp.einsum("kj,kjtu->ktu", select, stacked, preferred_element_type=jnp.float32)
    return picked.astype(jnp.bfloat16).reshape(owners * BLOCK, width)


def place_parts(parts, select, base_rows):
    total = jnp.einsum("bj,btd->jtd", select, parts, preferred_element_type=jnp.float32)
    total = total.reshape(base_rows.shape)
    return (base_rows.astype(jnp.float32) + total).astype(jnp.bfloat16)


def send_rows(packed):
    return lax.all_to_all(packed, "bundle", split_axis=0, concat_axis=0, tiled=True)


def send_parts(parts):
    return lax.all_to_all(parts, "bundle", split_axis=0, concat_axis=0, tiled=True)


def per_device(act_fwd, grad_in, w_gate, w_up, w_down, saved_gate, saved_up, mask_fwd, mask_bwd):
    owners = lax.axis_size("bundle")
    device = lax.axis_index("bundle")
    blocks_dev = act_fwd.shape[1] // BLOCK
    width = act_fwd.shape[2]
    gate_w = w_gate[0]
    up_w = w_up[0]
    down_w = w_down[0]
    select_f = sender_select(mask_fwd, device, blocks_dev)
    select_b = sender_select(mask_bwd, device, blocks_dev)
    packed_f = pack_rows(act_fwd[0], select_f, blocks_dev)
    packed_b = pack_rows(grad_in[0], select_b, blocks_dev)
    owner_b = owner_select(mask_bwd, device, owners, blocks_dev)
    gate_saved = pick_saved(saved_gate[0], owner_b, owners, blocks_dev)
    up_saved = pick_saved(saved_up[0], owner_b, owners, blocks_dev)
    rows_f = send_rows(packed_f)
    rows = rows_f.reshape(owners * BLOCK, width)
    gate_pre = jnp.dot(rows, gate_w, preferred_element_type=jnp.float32)
    up_pre = jnp.dot(rows, up_w, preferred_element_type=jnp.float32)
    hidden = (jnp.maximum(gate_pre, 0.0) * up_pre).astype(jnp.bfloat16)
    parts_f = (
        jnp.dot(hidden, down_w, preferred_element_type=jnp.float32)
        .astype(jnp.bfloat16)
        .reshape(owners, BLOCK, width)
    )
    back_f = send_parts(parts_f)
    rows_b = send_rows(packed_b)
    grad_hidden = contract_last(rows_b.reshape(owners * BLOCK, width), down_w)
    gate_value = gate_saved.astype(jnp.float32)
    up_value = up_saved.astype(jnp.float32)
    grad_gate = jnp.where(gate_value > 0, grad_hidden * up_value, 0.0).astype(jnp.bfloat16)
    grad_up = (grad_hidden * jnp.maximum(gate_value, 0.0)).astype(jnp.bfloat16)
    summed = contract_last(grad_gate, gate_w) + contract_last(grad_up, up_w)
    parts_b = summed.astype(jnp.bfloat16).reshape(owners, BLOCK, width)
    back_b = send_parts(parts_b)
    ahead = place_parts(back_f, select_f, act_fwd[0])
    behind = place_parts(back_b, select_b, grad_in[0])
    next_forward = shifted(ahead[None], "pipe", 1)
    next_backward = shifted(behind[None], "pipe", -1)
    return (next_forward, next_backward)


def solution(mesh):
    in_specs = (
        P("pipe", "bundle", None),
        P("pipe", "bundle", None),
        P("pipe", None, "bundle"),
        P("pipe", None, "bundle"),
        P("pipe", "bundle", None),
        P("pipe", None, "bundle"),
        P("pipe", None, "bundle"),
        P("pipe", None, None),
        P("pipe", None, None),
    )
    out_specs = (P("pipe", "bundle", None), P("pipe", "bundle", None))
    return jax.shard_map(
        per_device, mesh=mesh, in_specs=in_specs, out_specs=out_specs, check_vma=False
    )
```

profile of v0, /device:TPU:0, one launch (start us, length us, event | category | flops | bytes accessed | tf_op | source)
XLA Modules:
  0.0 241.4 jit_solution(4229285930731159591)
XLA Ops:
  0.7 2.7 %convolution_convert_fusion = bf16[8,16,8192]{2,0,1:T(8,128)(2,1)S(1)} fusion(bf16[4,16,8192]{2,1,0:T(8,128)(2,1)} %bitcast.81, s32[1,32,8]{1,2,0:T(8,128)} %param.17, s32[]{:T(128)S(6)} %select_n.11), kind=kOutput, calls=%fused_computation.2 | convolution fusion | flops 9437216 | bytes 3146756 | tf_op jit(solution)/shard_map/bj,jtd->btd/dot_general | solution.py:34
  3.4 2.5 %copy.34 = bf16[8,16,8192]{2,1,0:T(8,128)(2,1)} copy(bf16[8,16,8192]{2,0,1:T(8,128)(2,1)S(1)} %convolution_convert_fusion) | data formatting | bytes 4194304 | tf_op jit(solution)/shard_map/convert_element_type | solution.py:35
  5.9 7.4 %all-to-all-start.2 = ((bf16[8,16,8192]{2,1,0:T(8,128)(2,1)}), bf16[8,16,8192]{2,1,0:T(8,128)(2,1)}, u32[]{:S(2)}, u32[]{:S(2)}) async-start(bf16[8,16,8192]{2,1,0:T(8,128)(2,1)} %copy.34), calls=%async_computation.2 | async-start | bytes 4194304 | tf_op jit(solution)/shard_map/all_to_all | solution.py:52
  13.3 1.4 convolution_convert_fusion.1
  14.7 2.5 %copy.29 = bf16[8,16,8192]{2,1,0:T(8,128)(2,1)} copy(bf16[8,16,8192]{2,0,1:T(8,128)(2,1)S(1)} %convolution_convert_fusion.1) | data formatting | bytes 4194304 | tf_op jit(solution)/shard_map/convert_element_type | solution.py:35
  17.2 44.5 %all-to-all-done.2 = bf16[8,16,8192]{2,1,0:T(8,128)(2,1)} async-done(((bf16[8,16,8192]{2,1,0:T(8,128)(2,1)}), bf16[8,16,8192]{2,1,0:T(8,128)(2,1)}, u32[]{:S(2)}, u32[]{:S(2)}) %all-to-all-start.2) | async-done | bytes 2097184 | tf_op jit(solution)/shard_map/all_to_all | solution.py:52
  61.6 4.3 %all-to-all-start = ((bf16[8,16,8192]{2,1,0:T(8,128)(2,1)}), bf16[8,16,8192]{2,1,0:T(8,128)(2,1)}, u32[]{:S(2)}, u32[]{:S(2)}) async-start(bf16[8,16,8192]{2,1,0:T(8,128)(2,1)} %copy.29), calls=%async_computation | async-start | bytes 4194304 | tf_op jit(solution)/shard_map/all_to_all | solution.py:52
  66.6 3.1 %fusion.36 = (bf16[128,128]{1,0:T(8,128)(2,1)S(1)}, bf16[128,128]{1,0:T(8,128)(2,1)S(1)}) fusion(f32[8,16,128]{2,1,0:T(8,128)S(1)} %convert_maximum_fusion, f32[8,16,128]{2,1,0:T(8,128)S(1)} %bitcast.85, pred[8,16,128]{2,1,0:T(8,128)(4,1)S(1)} %convert_compare_fusion, bf16[128,8192]{1,0:T(8,128)(2,1)} %bitcast.16, bf16[1,128,8192]{2,1,0:T(8,128)(2,1)} %param.13), kind=kOutput, calls=%fused_computation.38 | convolution fusion | flops 268550144 | bytes 4407296 | tf_op jit(solution)/shard_map/dot_general | solution.py:16
  70.4 2.1 fusion
  72.5 41.3 %all-to-all-done = bf16[8,16,8192]{2,1,0:T(8,128)(2,1)} async-done(((bf16[8,16,8192]{2,1,0:T(8,128)(2,1)}), bf16[8,16,8192]{2,1,0:T(8,128)(2,1)}, u32[]{:S(2)}, u32[]{:S(2)}) %all-to-all-start) | async-done | bytes 2097184 | tf_op jit(solution)/shard_map/all_to_all | solution.py:52
  113.8 4.3 %all-to-all-start.3 = ((bf16[8,16,8192]{2,1,0:T(8,128)(2,1)}), bf16[8,16,8192]{2,1,0:T(8,128)(2,1)}, u32[]{:S(2)}, u32[]{:S(2)}) async-start(bf16[8,16,8192]{2,1,0:T(8,128)(2,1)} %bitcast.80), calls=%async_computation.3 | async-start | bytes 4194304 | tf_op jit(solution)/shard_map/all_to_all | solution.py:56
  118.2 2.9 %fusion.17 = f32[128,128]{1,0:T(8,128)S(1)} fusion(bf16[128,8192]{1,0:T(8,128)(2,1)} %bitcast.3, bf16[1,8192,128]{2,1,0:T(8,128)(2,1)} %param.11), kind=kOutput, calls=%fused_computation.23 | convolution fusion | flops 268451840 | bytes 4259840 | tf_op jit(solution)/shard_map/dot_general | solution.py:76
  121.1 4.9 %convolution_convert_fusion.2 = bf16[128,8192]{1,0:T(8,128)(2,1)} fusion(bf16[1,128,8192]{2,1,0:T(8,128)(2,1)} %param.13, f32[128,128]{1,0:T(8,128)S(1)} %fusion.17, bf16[128,8192]{1,0:T(8,128)(2,1)} %bitcast.3, bf16[1,8192,128]{2,1,0:T(8,128)(2,1)S(1)} %copy-done), kind=kOutput, calls=%fused_computation.4 | convolution fusion | flops 537952256 | bytes 8454144 | tf_op jit(solution)/shard_map/dot_general | solution.py:80
  126.0 40.0 %all-to-all-done.3 = bf16[8,16,8192]{2,1,0:T(8,128)(2,1)} async-done(((bf16[8,16,8192]{2,1,0:T(8,128)(2,1)}), bf16[8,16,8192]{2,1,0:T(8,128)(2,1)}, u32[]{:S(2)}, u32[]{:S(2)}) %all-to-all-start.3) | async-done | bytes 2097184 | tf_op jit(solution)/shard_map/all_to_all | solution.py:56
  166.0 4.5 %all-to-all-start.1 = ((bf16[8,16,8192]{2,1,0:T(8,128)(2,1)}), bf16[8,16,8192]{2,1,0:T(8,128)(2,1)}, u32[]{:S(2)}, u32[]{:S(2)}) async-start(bf16[8,16,8192]{2,1,0:T(8,128)(2,1)} %bitcast.79), calls=%async_computation.1 | async-start | bytes 4194304 | tf_op jit(solution)/shard_map/all_to_all | solution.py:56
  170.5 4.2 %fusion.13 = f32[4,16,8192]{2,0,1:T(4,128)S(1)} fusion(bf16[8,16,8192]{2,1,0:T(8,128)(2,1)} %all-to-all-done.3, s32[1,32,8]{1,2,0:T(8,128)S(1)} %copy-done.4, s32[]{:T(128)S(6)} %select_n.11), kind=kOutput, calls=%fused_computation.19 | convolution fusion | flops 8388640 | bytes 4195332 | tf_op jit(solution)/shard_map/bj,btd->jtd/dot_general | solution.py:46
  174.7 1.2 copy.36
  175.9 1.2 fusion.1
  177.1 41.2 %all-to-all-done.1 = bf16[8,16,8192]{2,1,0:T(8,128)(2,1)} async-done(((bf16[8,16,8192]{2,1,0:T(8,128)(2,1)}), bf16[8,16,8192]{2,1,0:T(8,128)(2,1)}, u32[]{:S(2)}, u32[]{:S(2)}) %all-to-all-start.1) | async-done | bytes 2097184 | tf_op jit(solution)/shard_map/all_to_all | solution.py:56
  218.2 4.1 %fusion.15 = f32[4,16,8192]{2,0,1:T(4,128)S(1)} fusion(bf16[8,16,8192]{2,1,0:T(8,128)(2,1)} %all-to-all-done.1, s32[1,32,8]{1,2,0:T(8,128)S(1)} %copy-done.5, s32[]{:T(128)S(6)} %select_n.11), kind=kOutput, calls=%fused_computation.21 | convolution fusion | flops 8388640 | bytes 4195332 | tf_op jit(solution)/shard_map/bj,btd->jtd/dot_general | solution.py:46
  222.4 1.2 copy.31
  223.9 14.2 %collective-permute-done = bf16[1,64,8192]{2,1,0:T(8,128)(2,1)S(1)} collective-permute-done((bf16[1,64,8192]{2,1,0:T(8,128)(2,1)S(1)}, bf16[1,64,8192]{2,1,0:T(8,128)(2,1)S(1)}, u32[]{:S(2)}, u32[]{:S(2)}) %collective-permute-start) | collective-permute-done | bytes 1048608 | tf_op jit(solution)/shard_map/ppermute | solution.py:12
  238.1 1.0 copy.56
  239.1 2.3 copy.57
  (27 shorter events, 1.6 us)
Async XLA Ops:
  0.6 69.8 %copy-start = (bf16[1,8192,128]{2,1,0:T(8,128)(2,1)S(1)}, bf16[1,8192,128]{2,1,0:T(8,128)(2,1)}, u32[]{:S(2)}) copy-start(bf16[1,8192,128]{2,1,0:T(8,128)(2,1)} %param.12) | copy-start | bytes 6291460
  5.9 7.4 %copy-start.3 = (bf16[1,64,8192]{2,1,0:T(8,128)(2,1)S(1)}, bf16[1,64,8192]{2,1,0:T(8,128)(2,1)}, u32[]{:S(2)}) copy-start(bf16[1,64,8192]{2,1,0:T(8,128)(2,1)} %param.9) | copy-start | bytes 3145732
  5.9 7.4 %copy-start.5 = (s32[1,32,8]{1,2,0:T(8,128)S(1)}, s32[1,32,8]{1,2,0:T(8,128)}, u32[]{:S(2)}) copy-start(s32[1,32,8]{1,2,0:T(8,128)} %param.16) | copy-start | bytes 3076
  5.9 55.8 %all-to-all-start.2 = ((bf16[8,16,8192]{2,1,0:T(8,128)(2,1)}), bf16[8,16,8192]{2,1,0:T(8,128)(2,1)}, u32[]{:S(2)}, u32[]{:S(2)}) async-start(bf16[8,16,8192]{2,1,0:T(8,128)(2,1)} %copy.34), calls=%async_computation.2 | async-start | bytes 4194304 | tf_op jit(solution)/shard_map/all_to_all | solution.py:52
  17.2 48.8 %copy-start.4 = (s32[1,32,8]{1,2,0:T(8,128)S(1)}, s32[1,32,8]{1,2,0:T(8,128)}, u32[]{:S(2)}) copy-start(s32[1,32,8]{1,2,0:T(8,128)} %param.17) | copy-start | bytes 3076
  17.2 49.0 %copy-start.6 = (bf16[1,512,128]{2,1,0:T(8,128)(2,1)S(1)}, bf16[1,512,128]{2,1,0:T(8,128)(2,1)}, u32[]{:S(2)}) copy-start(bf16[1,512,128]{2,1,0:T(8,128)(2,1)} %param.14) | copy-start | bytes 393220
  17.2 49.2 %copy-start.7 = (bf16[1,512,128]{2,1,0:T(8,128)(2,1)S(1)}, bf16[1,512,128]{2,1,0:T(8,128)(2,1)}, u32[]{:S(2)}) copy-start(bf16[1,512,128]{2,1,0:T(8,128)(2,1)} %param.15) | copy-start | bytes 393220
  61.6 52.2 %all-to-all-start = ((bf16[8,16,8192]{2,1,0:T(8,128)(2,1)}), bf16[8,16,8192]{2,1,0:T(8,128)(2,1)}, u32[]{:S(2)}, u32[]{:S(2)}) async-start(bf16[8,16,8192]{2,1,0:T(8,128)(2,1)} %copy.29), calls=%async_computation | async-start | bytes 4194304 | tf_op jit(solution)/shard_map/all_to_all | solution.py:52
  66.6 3.1 %copy-start.1 = (bf16[1,8192,128]{2,1,0:T(8,128)(2,1)S(1)}, bf16[1,8192,128]{2,1,0:T(8,128)(2,1)}, u32[]{:S(2)}) copy-start(bf16[1,8192,128]{2,1,0:T(8,128)(2,1)} %param.11) | copy-start | bytes 6291460
  113.8 52.2 %all-to-all-start.3 = ((bf16[8,16,8192]{2,1,0:T(8,128)(2,1)}), bf16[8,16,8192]{2,1,0:T(8,128)(2,1)}, u32[]{:S(2)}, u32[]{:S(2)}) async-start(bf16[8,16,8192]{2,1,0:T(8,128)(2,1)} %bitcast.80), calls=%async_computation.3 | async-start | bytes 4194304 | tf_op jit(solution)/shard_map/all_to_all | solution.py:56
  166.0 52.3 %all-to-all-start.1 = ((bf16[8,16,8192]{2,1,0:T(8,128)(2,1)}), bf16[8,16,8192]{2,1,0:T(8,128)(2,1)}, u32[]{:S(2)}, u32[]{:S(2)}) async-start(bf16[8,16,8192]{2,1,0:T(8,128)(2,1)} %bitcast.79), calls=%async_computation.1 | async-start | bytes 4194304 | tf_op jit(solution)/shard_map/all_to_all | solution.py:56
  174.7 1.2 copy-start.2
  177.1 46.8 %collective-permute-start.1 = (bf16[1,64,8192]{2,1,0:T(8,128)(2,1)}, bf16[1,64,8192]{2,1,0:T(8,128)(2,1)}, u32[]{:S(2)}, u32[]{:S(2)}) collective-permute-start(bf16[1,64,8192]{2,1,0:T(8,128)(2,1)} %fusion.1), channel_id=1, source_target_pairs={{0,24},{8,0},{16,8},{24,16},{1,25},{9,1},{17,9},{25,17},{2,26},{10... | collective-permute-start | bytes 3145736 | tf_op jit(solution)/shard_map/ppermute | solution.py:12
  223.9 14.3 %collective-permute-start = (bf16[1,64,8192]{2,1,0:T(8,128)(2,1)S(1)}, bf16[1,64,8192]{2,1,0:T(8,128)(2,1)S(1)}, u32[]{:S(2)}, u32[]{:S(2)}) collective-permute-start(bf16[1,64,8192]{2,1,0:T(8,128)(2,1)S(1)} %fusion.2), channel_id=1, source_target_pairs={{0,8},{8,16},{16,24},{24,0},{1,9},{9,17},{17,25},{25,1},{2,10},{10... | collective-permute-start | bytes 3145736 | tf_op jit(solution)/shard_map/ppermute | solution.py:12
where the time goes:
time: 242 us; the launch traced here: 241 us
  waiting for transfers between devices  181 us (75%)
  matrix products  26.5 us (11%)
  starting transfers between devices  20.7 us (9%)
  local copies, waits for them, and re-layouts  10.8 us (4%)
    all_to_all x2, waiting for transfers between devices, send_rows(): lax.all_to_all(packed, 'bundle', split_axis=0, concat_axis=0, tiled=True)  85.8 us
    all_to_all x2, waiting for transfers between devices, send_parts(): lax.all_to_all(parts, 'bundle', split_axis=0, concat_axis=0, tiled=True)  81.2 us
    ppermute x2, waiting for transfers between devices, shifted(): return lax.ppermute(value, axis, pairs)  14.2 us
    all_to_all x2, starting transfers between devices, send_rows(): lax.all_to_all(packed, 'bundle', split_axis=0, concat_axis=0, tiled=True)  11.8 us
    all_to_all x2, starting transfers between devices, send_parts(): lax.all_to_all(parts, 'bundle', split_axis=0, concat_axis=0, tiled=True)  8.87 us
    dot_general x2, matrix products, place_parts(): jnp.einsum('bj,btd->jtd', select, parts, preferred_element_type=jnp.float32)  8.3 us
    dot_general x3, matrix products, contract_last(): lax.dot_general(left, right, (((1,), (1,)), ((), ())), preferred_element_...  5.86 us
    convert_element_type x2, local copies, waits for them, and re-layouts, pack_rows(): return packed.astype(jnp.bfloat16)  4.98 us
  transfers between devices with their start and end apart: 6, of which 5 were waited for; matrix products, arithmetic and copies ran while one was open for 13% of the time, Pallas kernels for 0%

commit v1 on v0

v1 whole, which is shorter than its diff:
```python
import jax
import jax.numpy as jnp
from jax import lax
from jax.sharding import PartitionSpec as P

BLOCK = 16


def contract_last(left, right):
    return lax.dot_general(
        left, right, (((1,), (1,)), ((), ())), preferred_element_type=jnp.float32
    )


def contract_first(left, right):
    return lax.dot_general(
        left, right, (((0,), (0,)), ((), ())), preferred_element_type=jnp.float32
    )


def one_hot_rows(flags, blocks):
    wide = jnp.repeat(jnp.repeat(flags, BLOCK, axis=0), BLOCK, axis=1)
    row = lax.broadcasted_iota(jnp.int32, wide.shape, 0) % BLOCK
    col = lax.broadcasted_iota(jnp.int32, wide.shape, 1) % BLOCK
    return jnp.where(row == col, wide, 0).astype(jnp.bfloat16)


def exchange(piece, offset):
    count = lax.axis_size("bundle")
    return lax.ppermute(piece, "bundle", [(b, b ^ offset) for b in range(count)])


def deliver(piece, offset, steps):
    pipes, count = lax.axis_size("pipe"), lax.axis_size("bundle")
    pairs = [
        (p * count + b, ((p + steps) % pipes) * count + (b ^ offset))
        for p in range(pipes)
        for b in range(count)
    ]
    return lax.ppermute(piece, ("pipe", "bundle"), pairs)


def far_first(count):
    return list(range(count - 1, -1, -1))


def own_flags(mask, device, blocks_dev, offsets):
    own = lax.dynamic_slice_in_dim(mask[0], device * blocks_dev, blocks_dev, 0)
    return own.T[device ^ offsets]


def owner_flags(mask, device, blocks_dev, offsets):
    blocks = mask.shape[1]
    column = lax.dynamic_slice_in_dim(mask[0], device, 1, 1)[:, 0]
    home = lax.broadcasted_iota(jnp.int32, (offsets.shape[0], blocks), 1) // blocks_dev
    return jnp.where(home == (device ^ offsets)[:, None], column[None, :], 0)


def dispatch(rows, flags, blocks_dev, order):
    packed = jnp.dot(one_hot_rows(flags, blocks_dev), rows, preferred_element_type=jnp.float32)
    packed = packed.astype(jnp.bfloat16)
    arrived = []
    for place, offset in enumerate(order):
        piece = packed[place * BLOCK : (place + 1) * BLOCK]
        arrived.append(exchange(piece, offset) if offset else piece)
    return arrived


def give_back(parts, order, steps):
    return [
        deliver(parts[place * BLOCK : (place + 1) * BLOCK], offset, steps)
        for place, offset in enumerate(order)
    ]


def shifted(value, steps):
    count = lax.axis_size("pipe")
    return lax.ppermute(value, "pipe", [(p, (p + steps) % count) for p in range(count)])


def place_parts(parts, flags, base, blocks_dev):
    total = contract_first(one_hot_rows(flags, blocks_dev), jnp.concatenate(parts, axis=0))
    return (base.astype(jnp.float32) + total).astype(jnp.bfloat16)


def per_device(act_fwd, grad_in, w_gate, w_up, w_down, saved_gate, saved_up, mask_fwd, mask_bwd):
    count = lax.axis_size("bundle")
    device = lax.axis_index("bundle")
    blocks_dev = act_fwd.shape[1] // BLOCK
    gate_w, up_w, down_w = w_gate[0], w_up[0], w_down[0]
    order = far_first(count)
    offsets = jnp.array(order, jnp.int32)
    flags_f = own_flags(mask_fwd, device, blocks_dev, offsets)
    flags_b = own_flags(mask_bwd, device, blocks_dev, offsets)
    rows_f = jnp.concatenate(dispatch(act_fwd[0], flags_f, blocks_dev, order), axis=0)
    rows_b = jnp.concatenate(dispatch(grad_in[0], flags_b, blocks_dev, order), axis=0)
    pick = one_hot_rows(owner_flags(mask_bwd, device, blocks_dev, offsets), mask_bwd.shape[1])
    gate_value = jnp.dot(pick, saved_gate[0], preferred_element_type=jnp.float32)
    up_value = jnp.dot(pick, saved_up[0], preferred_element_type=jnp.float32)

    gate_pre = jnp.dot(rows_f, gate_w, preferred_element_type=jnp.float32)
    up_pre = jnp.dot(rows_f, up_w, preferred_element_type=jnp.float32)
    hidden = (jnp.maximum(gate_pre, 0.0) * up_pre).astype(jnp.bfloat16)
    parts_f = jnp.dot(hidden, down_w, preferred_element_type=jnp.float32).astype(jnp.bfloat16)
    back_f = give_back(parts_f, order, 1)

    grad_hidden = contract_last(rows_b, down_w)
    grad_gate = jnp.where(gate_value > 0, grad_hidden * up_value, 0.0).astype(jnp.bfloat16)
    grad_up = (grad_hidden * jnp.maximum(gate_value, 0.0)).astype(jnp.bfloat16)
    parts_b = (contract_last(grad_gate, gate_w) + contract_last(grad_up, up_w)).astype(jnp.bfloat16)
    back_b = give_back(parts_b, order, -1)

    base_f = shifted(act_fwd[0], 1)
    base_b = shifted(grad_in[0], -1)
    next_flags_f = shifted(flags_f.astype(jnp.float32), 1)
    next_flags_b = shifted(flags_b.astype(jnp.float32), -1)
    next_forward = place_parts(back_f, next_flags_f, base_f, blocks_dev)
    next_backward = place_parts(back_b, next_flags_b, base_b, blocks_dev)
    return (next_forward[None], next_backward[None])


def solution(mesh):
    in_specs = (
        P("pipe", "bundle", None),
        P("pipe", "bundle", None),
        P("pipe", None, "bundle"),
        P("pipe", None, "bundle"),
        P("pipe", "bundle", None),
        P("pipe", None, "bundle"),
        P("pipe", None, "bundle"),
        P("pipe", None, None),
        P("pipe", None, None),
    )
    out_specs = (P("pipe", "bundle", None), P("pipe", "bundle", None))
    return jax.shard_map(
        per_device, mesh=mesh, in_specs=in_specs, out_specs=out_specs, check_vma=False
    )
```

time: 242 us -> 235 us (0.971)
  waiting for transfers between devices: 181 us -> 68.8 us
  starting transfers between devices: 20.7 us -> 114 us
  local copies, waits for them, and re-layouts: 10.8 us -> 26.2 us
  matrix products: 26.5 us -> 22.2 us
    all_to_all x4 -> x0, waiting for transfers between devices: 167 us -> none  [the longest x2 85.8 us: send_rows(): lax.all_to_all(packed, 'bundle', split_axis=0, concat_axis=0, tiled=True)]
    ppermute x2 -> x34, starting transfers between devices: 0.06 us -> 114 us  [the longest x16 56.9 us: deliver(): return lax.ppermute(piece, ('pipe', 'bundle'), pairs)]
    ppermute x2 -> x34, waiting for transfers between devices: 14.2 us -> 68.8 us  [the longest x16 46.1 us: deliver(): return lax.ppermute(piece, ('pipe', 'bundle'), pairs)]
    all_to_all x4 -> x0, starting transfers between devices: 20.6 us -> none  [the longest x2 11.8 us: send_rows(): lax.all_to_all(packed, 'bundle', split_axis=0, concat_axis=0, tiled=True)]
    unnamed x18 -> x62, local copies, waits for them, and re-layouts: 3.27 us -> 15 us
    slice x0 -> x4, local copies, waits for them, and re-layouts: none -> 5.57 us  [the longest x2 3.02 us: give_back(): parts[place * BLOCK:(place + 1) * BLOCK]]
    dot_general x7 -> x6, matrix products: 15.7 us -> 10.2 us  [the longest x2 5.31 us: contract_first(): lax.dot_general(left, right, (((0,), (0,)), ((), ())), preferred_element_...]
    convert_element_type x3 -> x0, local copies, waits for them, and re-layouts: 5.07 us -> none  [the longest x2 4.98 us: pack_rows(): return packed.astype(jnp.bfloat16)]
  transfers between devices with their start and end apart: 6 -> 34, of which waited for: 5 -> 18; matrix products, arithmetic and copies ran while one was open for 13% -> 16% of each run, Pallas kernels for 0% -> 0%
where the time goes in v1:
time: 235 us
  starting transfers between devices  114 us (49%)
  waiting for transfers between devices  68.8 us (29%)
  local copies, waits for them, and re-layouts  26.2 us (11%)
  matrix products  22.2 us (9%)
    ppermute x16, starting transfers between devices, deliver(): return lax.ppermute(piece, ('pipe', 'bundle'), pairs)  56.9 us
    ppermute x14, starting transfers between devices, exchange(): lax.ppermute(piece, 'bundle', [(b, b ^ offset) for b in range(count)])  55.5 us
    ppermute x16, waiting for transfers between devices, deliver(): return lax.ppermute(piece, ('pipe', 'bundle'), pairs)  46.1 us
    ppermute x14, waiting for transfers between devices, exchange(): lax.ppermute(piece, 'bundle', [(b, b ^ offset) for b in range(count)])  21.6 us
    unnamed x62, local copies, waits for them, and re-layouts  15 us
    dot_general x3, matrix products, contract_last(): lax.dot_general(left, right, (((1,), (1,)), ((), ())), preferred_element_...  7.12 us
    dot_general x2, matrix products, contract_first(): lax.dot_general(left, right, (((0,), (0,)), ((), ())), preferred_element_...  5.31 us
    dot_general x1, matrix products, per_device(): jnp.dot(hidden, down_w, preferred_element_type=jnp.float32)  4.94 us
  transfers between devices with their start and end apart: 34, of which 18 were waited for; matrix products, arithmetic and copies ran while one was open for 16% of the time, Pallas kernels for 0%

profile of v1, /device:TPU:0, one launch (start us, length us, event | category | flops | bytes accessed | tf_op | source)
XLA Modules:
  0.0 234.6 jit_solution(16441444651957868197)
XLA Ops:
  8.6 6.0 %collective-permute-start.19 = (bf16[16,8192]{1,0:T(8,128)(2,1)}, bf16[16,8192]{1,0:T(8,128)(2,1)}, u32[]{:S(2)}, u32[]{:S(2)}) collective-permute-start(bf16[16,8192]{1,0:T(8,128)(2,1)} %get-tuple-element.16), channel_id=1, source_target_pairs={{0,7},{1,6},{2,5},{3,4},{4,3},{5,2},{6,1},{7,0},{8,15},{9,14},{10,... | collective-permute-start | bytes 786440 | tf_op jit(solution)/shard_map/ppermute | solution.py:30
  28.8 18.0 %collective-permute-start.24 = (bf16[16,8192]{1,0:T(8,128)(2,1)}, bf16[16,8192]{1,0:T(8,128)(2,1)S(1)}, u32[]{:S(2)}, u32[]{:S(2)}) collective-permute-start(bf16[16,8192]{1,0:T(8,128)(2,1)} %get-tuple-element.11), channel_id=1, source_target_pairs={{0,2},{1,3},{2,0},{3,1},{4,6},{5,7},{6,4},{7,5},{8,10},{9,11},{10,... | collective-permute-start | bytes 786440 | tf_op jit(solution)/shard_map/ppermute | solution.py:30
  50.2 6.4 %collective-permute-done.21 = bf16[16,8192]{1,0:T(8,128)(2,1)} collective-permute-done((bf16[16,8192]{1,0:T(8,128)(2,1)}, bf16[16,8192]{1,0:T(8,128)(2,1)}, u32[]{:S(2)}, u32[]{:S(2)}) %collective-permute-start.21) | collective-permute-done | bytes 262176 | tf_op jit(solution)/shard_map/ppermute | solution.py:30
  57.6 3.7 %collective-permute-done.22 = bf16[16,8192]{1,0:T(8,128)(2,1)} collective-permute-done((bf16[16,8192]{1,0:T(8,128)(2,1)}, bf16[16,8192]{1,0:T(8,128)(2,1)}, u32[]{:S(2)}, u32[]{:S(2)}) %collective-permute-start.22) | collective-permute-done | bytes 262176 | tf_op jit(solution)/shard_map/ppermute | solution.py:30
  67.1 3.9 %collective-permute-start.5 = (bf16[16,8192]{1,0:T(8,128)(2,1)}, bf16[16,8192]{1,0:T(8,128)(2,1)}, u32[]{:S(2)}, u32[]{:S(2)}) collective-permute-start(bf16[16,8192]{1,0:T(8,128)(2,1)} %get-tuple-element.28), channel_id=1, source_target_pairs={{0,4},{1,5},{2,6},{3,7},{4,0},{5,1},{6,2},{7,3},{8,12},{9,13},{10,... | collective-permute-start | bytes 786440 | tf_op jit(solution)/shard_map/ppermute | solution.py:30
  75.9 3.5 %fusion = bf16[128,8192]{1,0:T(8,128)(2,1)S(1)} fusion(f32[128,8192]{1,0:T(8,128)} %fusion.7, bf16[1,8192,128]{2,1,0:T(8,128)(2,1)} %param.13, f32[128,128]{1,0:T(8,128)S(1)} %fusion.1, f32[128,128]{1,0:T(8,128)S(1)} %fusion.28), kind=kOutput, calls=%fused_computation.3 | convolution fusion | flops 270581760 | bytes 8519680 | tf_op jit(solution)/shard_map/dot_general | solution.py:10
  80.7 12.9 %collective-permute-start.6 = (bf16[16,8192]{1,0:T(8,128)(2,1)S(1)}, bf16[16,8192]{1,0:T(8,128)(2,1)S(1)}, u32[]{:S(2)}, u32[]{:S(2)}) collective-permute-start(bf16[16,8192]{1,0:T(8,128)(2,1)S(1)} %copy-done.9), channel_id=1, source_target_pairs={{0,3},{1,2},{2,1},{3,0},{4,7},{5,6},{6,5},{7,4},{8,11},{9,10},{10,... | collective-permute-start | bytes 786440 | tf_op jit(solution)/shard_map/ppermute | solution.py:30
  94.6 3.5 %collective-permute-start.7 = (bf16[16,8192]{1,0:T(8,128)(2,1)S(1)}, bf16[16,8192]{1,0:T(8,128)(2,1)S(1)}, u32[]{:S(2)}, u32[]{:S(2)}) collective-permute-start(bf16[16,8192]{1,0:T(8,128)(2,1)S(1)} %copy-done.8), channel_id=1, source_target_pairs={{0,2},{1,3},{2,0},{3,1},{4,6},{5,7},{6,4},{7,5},{8,10},{9,11},{10,... | collective-permute-start | bytes 786440 | tf_op jit(solution)/shard_map/ppermute | solution.py:30
  99.1 5.1 %collective-permute-done.4 = bf16[16,8192]{1,0:T(8,128)(2,1)} collective-permute-done((bf16[16,8192]{1,0:T(8,128)(2,1)}, bf16[16,8192]{1,0:T(8,128)(2,1)}, u32[]{:S(2)}, u32[]{:S(2)}) %collective-permute-start.4) | collective-permute-done | bytes 262176 | tf_op jit(solution)/shard_map/ppermute | solution.py:30
  107.8 3.4 %collective-permute-done.6 = bf16[16,8192]{1,0:T(8,128)(2,1)S(1)} collective-permute-done((bf16[16,8192]{1,0:T(8,128)(2,1)S(1)}, bf16[16,8192]{1,0:T(8,128)(2,1)S(1)}, u32[]{:S(2)}, u32[]{:S(2)}) %collective-permute-start.6) | collective-permute-done | bytes 262176 | tf_op jit(solution)/shard_map/ppermute | solution.py:30
  119.7 4.9 %convolution_convert_fusion.2 = bf16[128,8192]{1,0:T(8,128)(2,1)} fusion(bf16[1,128,8192]{2,1,0:T(8,128)(2,1)} %param.14, f32[128,128]{1,0:T(8,128)S(1)} %fusion.5, bf16[128,8192]{1,0:T(8,128)(2,1)} %copy-done.1, bf16[1,8192,128]{2,1,0:T(8,128)(2,1)S(1)} %copy-done), kind=kOutput, calls=%fused_computation.6 | convolution fusion | flops 537968640 | bytes 8454144 | tf_op jit(solution)/shard_map/dot_general | solution.py:104
  128.8 10.2 %collective-permute-done.9 = bf16[16,8192]{1,0:T(8,128)(2,1)S(1)} collective-permute-done((bf16[16,8192]{1,0:T(8,128)(2,1)S(1)}, bf16[16,8192]{1,0:T(8,128)(2,1)S(1)}, u32[]{:S(2)}, u32[]{:S(2)}) %collective-permute-start.9) | collective-permute-done | bytes 262176 | tf_op jit(solution)/shard_map/ppermute | solution.py:40
  139.0 19.7 %collective-permute-start.29 = (bf16[16,8192]{1,0:T(8,128)(2,1)S(1)}, bf16[16,8192]{1,0:T(8,128)(2,1)S(1)}, u32[]{:S(2)}, u32[]{:S(2)}) collective-permute-start(bf16[16,8192]{1,0:T(8,128)(2,1)S(1)} %copy-done.13), channel_id=1, source_target_pairs={{0,28},{1,29},{2,30},{3,31},{4,24},{5,25},{6,26},{7,27},{8,4},{9,5... | collective-permute-start | bytes 786440 | tf_op jit(solution)/shard_map/ppermute | solution.py:40
  159.8 3.0 %collective-permute-start.31 = (bf16[16,8192]{1,0:T(8,128)(2,1)S(1)}, bf16[16,8192]{1,0:T(8,128)(2,1)S(1)}, u32[]{:S(2)}, u32[]{:S(2)}) collective-permute-start(bf16[16,8192]{1,0:T(8,128)(2,1)S(1)} %copy-done.11), channel_id=1, source_target_pairs={{0,26},{1,27},{2,24},{3,25},{4,30},{5,31},{6,28},{7,29},{8,2},{9,3... | collective-permute-start | bytes 786440 | tf_op jit(solution)/shard_map/ppermute | solution.py:40
  163.8 4.0 %collective-permute-done.29 = bf16[16,8192]{1,0:T(8,128)(2,1)S(1)} collective-permute-done((bf16[16,8192]{1,0:T(8,128)(2,1)S(1)}, bf16[16,8192]{1,0:T(8,128)(2,1)S(1)}, u32[]{:S(2)}, u32[]{:S(2)}) %collective-permute-start.29) | collective-permute-done | bytes 262176 | tf_op jit(solution)/shard_map/ppermute | solution.py:40
  167.8 4.8 %collective-permute-start.32 = (bf16[16,8192]{1,0:T(8,128)(2,1)S(1)}, bf16[16,8192]{1,0:T(8,128)(2,1)S(1)}, u32[]{:S(2)}, u32[]{:S(2)}) collective-permute-start(bf16[16,8192]{1,0:T(8,128)(2,1)S(1)} %copy-done.10), channel_id=1, source_target_pairs={{0,25},{1,24},{2,27},{3,26},{4,29},{5,28},{6,31},{7,30},{8,1},{9,0... | collective-permute-start | bytes 786440 | tf_op jit(solution)/shard_map/ppermute | solution.py:40
  173.9 3.0 %collective-permute-done.31 = bf16[16,8192]{1,0:T(8,128)(2,1)S(1)} collective-permute-done((bf16[16,8192]{1,0:T(8,128)(2,1)S(1)}, bf16[16,8192]{1,0:T(8,128)(2,1)S(1)}, u32[]{:S(2)}, u32[]{:S(2)}) %collective-permute-start.31) | collective-permute-done | bytes 262176 | tf_op jit(solution)/shard_map/ppermute | solution.py:40
  178.2 3.5 %collective-permute-start.11 = (bf16[16,8192]{1,0:T(8,128)(2,1)S(1)}, bf16[16,8192]{1,0:T(8,128)(2,1)S(1)}, u32[]{:S(2)}, u32[]{:S(2)}) collective-permute-start(bf16[16,8192]{1,0:T(8,128)(2,1)S(1)} %get-tuple-element.22), channel_id=1, source_target_pairs={{0,13},{1,12},{2,15},{3,14},{4,9},{5,8},{6,11},{7,10},{8,21},{9,20... | collective-permute-start | bytes 786440 | tf_op jit(solution)/shard_map/ppermute | solution.py:40
  183.4 4.1 %collective-permute-done.10 = bf16[16,8192]{1,0:T(8,128)(2,1)S(1)} collective-permute-done((bf16[16,8192]{1,0:T(8,128)(2,1)S(1)}, bf16[16,8192]{1,0:T(8,128)(2,1)S(1)}, u32[]{:S(2)}, u32[]{:S(2)}) %collective-permute-start.10) | collective-permute-done | bytes 262176 | tf_op jit(solution)/shard_map/ppermute | solution.py:40
  187.5 18.0 %collective-permute-start.13 = (bf16[16,8192]{1,0:T(8,128)(2,1)S(1)}, bf16[16,8192]{1,0:T(8,128)(2,1)S(1)}, u32[]{:S(2)}, u32[]{:S(2)}) collective-permute-start(bf16[16,8192]{1,0:T(8,128)(2,1)S(1)} %get-tuple-element.20), channel_id=1, source_target_pairs={{0,11},{1,10},{2,9},{3,8},{4,15},{5,14},{6,13},{7,12},{8,19},{9,18... | collective-permute-start | bytes 786440 | tf_op jit(solution)/shard_map/ppermute | solution.py:40
  205.5 5.7 %collective-permute-done.11 = bf16[16,8192]{1,0:T(8,128)(2,1)S(1)} collective-permute-done((bf16[16,8192]{1,0:T(8,128)(2,1)S(1)}, bf16[16,8192]{1,0:T(8,128)(2,1)S(1)}, u32[]{:S(2)}, u32[]{:S(2)}) %collective-permute-start.11) | collective-permute-done | bytes 262176 | tf_op jit(solution)/shard_map/ppermute | solution.py:40
  211.2 4.5 %collective-permute-done.12 = bf16[16,8192]{1,0:T(8,128)(2,1)S(1)} collective-permute-done((bf16[16,8192]{1,0:T(8,128)(2,1)S(1)}, bf16[16,8192]{1,0:T(8,128)(2,1)S(1)}, u32[]{:S(2)}, u32[]{:S(2)}) %collective-permute-start.12) | collective-permute-done | bytes 262176 | tf_op jit(solution)/shard_map/ppermute | solution.py:40
  216.8 6.2 %collective-permute-done.13 = bf16[16,8192]{1,0:T(8,128)(2,1)S(1)} collective-permute-done((bf16[16,8192]{1,0:T(8,128)(2,1)S(1)}, bf16[16,8192]{1,0:T(8,128)(2,1)S(1)}, u32[]{:S(2)}, u32[]{:S(2)}) %collective-permute-start.13) | collective-permute-done | bytes 262176 | tf_op jit(solution)/shard_map/ppermute | solution.py:40
  223.1 3.7 %collective-permute-done.14 = bf16[16,8192]{1,0:T(8,128)(2,1)S(1)} collective-permute-done((bf16[16,8192]{1,0:T(8,128)(2,1)S(1)}, bf16[16,8192]{1,0:T(8,128)(2,1)S(1)}, u32[]{:S(2)}, u32[]{:S(2)}) %collective-permute-start.14) | collective-permute-done | bytes 262176 | tf_op jit(solution)/shard_map/ppermute | solution.py:40
  (160 shorter events, 71.6 us)
Async XLA Ops:
  8.6 20.2 %collective-permute-start.19 = (bf16[16,8192]{1,0:T(8,128)(2,1)}, bf16[16,8192]{1,0:T(8,128)(2,1)}, u32[]{:S(2)}, u32[]{:S(2)}) collective-permute-start(bf16[16,8192]{1,0:T(8,128)(2,1)} %get-tuple-element.16), channel_id=1, source_target_pairs={{0,7},{1,6},{2,5},{3,4},{4,3},{5,2},{6,1},{7,0},{8,15},{9,14},{10,... | collective-permute-start | bytes 786440 | tf_op jit(solution)/shard_map/ppermute | solution.py:30
  14.6 33.1 %collective-permute-start.20 = (bf16[16,8192]{1,0:T(8,128)(2,1)}, bf16[16,8192]{1,0:T(8,128)(2,1)}, u32[]{:S(2)}, u32[]{:S(2)}) collective-permute-start(bf16[16,8192]{1,0:T(8,128)(2,1)} %get-tuple-element.15), channel_id=1, source_target_pairs={{0,6},{1,7},{2,4},{3,5},{4,2},{5,3},{6,0},{7,1},{8,14},{9,15},{10,... | collective-permute-start | bytes 786440 | tf_op jit(solution)/shard_map/ppermute | solution.py:30
  14.8 41.7 %collective-permute-start.21 = (bf16[16,8192]{1,0:T(8,128)(2,1)}, bf16[16,8192]{1,0:T(8,128)(2,1)}, u32[]{:S(2)}, u32[]{:S(2)}) collective-permute-start(bf16[16,8192]{1,0:T(8,128)(2,1)} %get-tuple-element.14), channel_id=1, source_target_pairs={{0,5},{1,4},{2,7},{3,6},{4,1},{5,0},{6,3},{7,2},{8,13},{9,12},{10,... | collective-permute-start | bytes 786440 | tf_op jit(solution)/shard_map/ppermute | solution.py:30
  15.6 45.7 %collective-permute-start.22 = (bf16[16,8192]{1,0:T(8,128)(2,1)}, bf16[16,8192]{1,0:T(8,128)(2,1)}, u32[]{:S(2)}, u32[]{:S(2)}) collective-permute-start(bf16[16,8192]{1,0:T(8,128)(2,1)} %get-tuple-element.13), channel_id=1, source_target_pairs={{0,4},{1,5},{2,6},{3,7},{4,0},{5,1},{6,2},{7,3},{8,12},{9,13},{10,... | collective-permute-start | bytes 786440 | tf_op jit(solution)/shard_map/ppermute | solution.py:30
  25.4 38.9 %collective-permute-start.23 = (bf16[16,8192]{1,0:T(8,128)(2,1)}, bf16[16,8192]{1,0:T(8,128)(2,1)}, u32[]{:S(2)}, u32[]{:S(2)}) collective-permute-start(bf16[16,8192]{1,0:T(8,128)(2,1)} %get-tuple-element.12), channel_id=1, source_target_pairs={{0,3},{1,2},{2,1},{3,0},{4,7},{5,6},{6,5},{7,4},{8,11},{9,10},{10,... | collective-permute-start | bytes 786440 | tf_op jit(solution)/shard_map/ppermute | solution.py:30
  28.8 38.3 %collective-permute-start.24 = (bf16[16,8192]{1,0:T(8,128)(2,1)}, bf16[16,8192]{1,0:T(8,128)(2,1)S(1)}, u32[]{:S(2)}, u32[]{:S(2)}) collective-permute-start(bf16[16,8192]{1,0:T(8,128)(2,1)} %get-tuple-element.11), channel_id=1, source_target_pairs={{0,2},{1,3},{2,0},{3,1},{4,6},{5,7},{6,4},{7,5},{8,10},{9,11},{10,... | collective-permute-start | bytes 786440 | tf_op jit(solution)/shard_map/ppermute | solution.py:30
  47.7 19.4 %collective-permute-start.25 = (bf16[16,8192]{1,0:T(8,128)(2,1)}, bf16[16,8192]{1,0:T(8,128)(2,1)S(1)}, u32[]{:S(2)}, u32[]{:S(2)}) collective-permute-start(bf16[16,8192]{1,0:T(8,128)(2,1)} %get-tuple-element.10), channel_id=1, source_target_pairs={{0,1},{1,0},{2,3},{3,2},{4,5},{5,4},{6,7},{7,6},{8,9},{9,8},{10,11... | collective-permute-start | bytes 786440 | tf_op jit(solution)/shard_map/ppermute | solution.py:30
  56.6 172.6 %collective-permute-start.17 = (bf16[64,8192]{1,0:T(8,128)(2,1)S(1)}, bf16[64,8192]{1,0:T(8,128)(2,1)}, u32[]{:S(2)}, u32[]{:S(2)}) collective-permute-start(bf16[64,8192]{1,0:T(8,128)(2,1)S(1)} %bitcast.83), channel_id=1, source_target_pairs={{0,24},{8,0},{16,8},{24,16},{1,25},{9,1},{17,9},{25,17},{2,26},{10... | collective-permute-start | bytes 3145736 | tf_op jit(solution)/shard_map/ppermute | solution.py:78
  61.3 19.5 %collective-permute-start.2 = (bf16[16,8192]{1,0:T(8,128)(2,1)}, bf16[16,8192]{1,0:T(8,128)(2,1)}, u32[]{:S(2)}, u32[]{:S(2)}) collective-permute-start(bf16[16,8192]{1,0:T(8,128)(2,1)} %get-tuple-element.31), channel_id=1, source_target_pairs={{0,7},{1,6},{2,5},{3,4},{4,3},{5,2},{6,1},{7,0},{8,15},{9,14},{10,... | collective-permute-start | bytes 786440 | tf_op jit(solution)/shard_map/ppermute | solution.py:30
  64.3 30.3 %collective-permute-start.3 = (bf16[16,8192]{1,0:T(8,128)(2,1)}, bf16[16,8192]{1,0:T(8,128)(2,1)}, u32[]{:S(2)}, u32[]{:S(2)}) collective-permute-start(bf16[16,8192]{1,0:T(8,128)(2,1)} %get-tuple-element.30), channel_id=1, source_target_pairs={{0,6},{1,7},{2,4},{3,5},{4,2},{5,3},{6,0},{7,1},{8,14},{9,15},{10,... | collective-permute-start | bytes 786440 | tf_op jit(solution)/shard_map/ppermute | solution.py:30
  67.0 37.2 %collective-permute-start.4 = (bf16[16,8192]{1,0:T(8,128)(2,1)}, bf16[16,8192]{1,0:T(8,128)(2,1)}, u32[]{:S(2)}, u32[]{:S(2)}) collective-permute-start(bf16[16,8192]{1,0:T(8,128)(2,1)} %get-tuple-element.29), channel_id=1, source_target_pairs={{0,5},{1,4},{2,7},{3,6},{4,1},{5,0},{6,3},{7,2},{8,13},{9,12},{10,... | collective-permute-start | bytes 786440 | tf_op jit(solution)/shard_map/ppermute | solution.py:30
  67.1 39.7 %collective-permute-start.5 = (bf16[16,8192]{1,0:T(8,128)(2,1)}, bf16[16,8192]{1,0:T(8,128)(2,1)}, u32[]{:S(2)}, u32[]{:S(2)}) collective-permute-start(bf16[16,8192]{1,0:T(8,128)(2,1)} %get-tuple-element.28), channel_id=1, source_target_pairs={{0,4},{1,5},{2,6},{3,7},{4,0},{5,1},{6,2},{7,3},{8,12},{9,13},{10,... | collective-permute-start | bytes 786440 | tf_op jit(solution)/shard_map/ppermute | solution.py:30
  80.7 30.5 %collective-permute-start.6 = (bf16[16,8192]{1,0:T(8,128)(2,1)S(1)}, bf16[16,8192]{1,0:T(8,128)(2,1)S(1)}, u32[]{:S(2)}, u32[]{:S(2)}) collective-permute-start(bf16[16,8192]{1,0:T(8,128)(2,1)S(1)} %copy-done.9), channel_id=1, source_target_pairs={{0,3},{1,2},{2,1},{3,0},{4,7},{5,6},{6,5},{7,4},{8,11},{9,10},{10,... | collective-permute-start | bytes 786440 | tf_op jit(solution)/shard_map/ppermute | solution.py:30
  94.6 19.2 %collective-permute-start.7 = (bf16[16,8192]{1,0:T(8,128)(2,1)S(1)}, bf16[16,8192]{1,0:T(8,128)(2,1)S(1)}, u32[]{:S(2)}, u32[]{:S(2)}) collective-permute-start(bf16[16,8192]{1,0:T(8,128)(2,1)S(1)} %copy-done.8), channel_id=1, source_target_pairs={{0,2},{1,3},{2,0},{3,1},{4,6},{5,7},{6,4},{7,5},{8,10},{9,11},{10,... | collective-permute-start | bytes 786440 | tf_op jit(solution)/shard_map/ppermute | solution.py:30
  106.8 125.1 %collective-permute-start = (bf16[64,8192]{1,0:T(8,128)(2,1)}, bf16[64,8192]{1,0:T(8,128)(2,1)}, u32[]{:S(2)}, u32[]{:S(2)}) collective-permute-start(bf16[64,8192]{1,0:T(8,128)(2,1)} %bitcast), channel_id=1, source_target_pairs={{0,8},{8,16},{16,24},{24,0},{1,9},{9,17},{17,25},{25,1},{2,10},{10... | collective-permute-start | bytes 3145736 | tf_op jit(solution)/shard_map/ppermute | solution.py:78
  111.2 15.2 %collective-permute-start.26 = (bf16[16,8192]{1,0:T(8,128)(2,1)}, bf16[16,8192]{1,0:T(8,128)(2,1)}, u32[]{:S(2)}, u32[]{:S(2)}) collective-permute-start(bf16[16,8192]{1,0:T(8,128)(2,1)} %get-tuple-element.9), channel_id=1, source_target_pairs={{0,31},{1,30},{2,29},{3,28},{4,27},{5,26},{6,25},{7,24},{8,7},{9,6... | collective-permute-start | bytes 786440 | tf_op jit(solution)/shard_map/ppermute | solution.py:40
  113.8 44.9 %collective-permute-start.27 = (bf16[16,8192]{1,0:T(8,128)(2,1)}, bf16[16,8192]{1,0:T(8,128)(2,1)}, u32[]{:S(2)}, u32[]{:S(2)}) collective-permute-start(bf16[16,8192]{1,0:T(8,128)(2,1)} %get-tuple-element.8), channel_id=1, source_target_pairs={{0,30},{1,31},{2,28},{3,29},{4,26},{5,27},{6,24},{7,25},{8,6},{9,7... | collective-permute-start | bytes 786440 | tf_op jit(solution)/shard_map/ppermute | solution.py:40
  116.6 43.3 %collective-permute-start.28 = (bf16[16,8192]{1,0:T(8,128)(2,1)}, bf16[16,8192]{1,0:T(8,128)(2,1)}, u32[]{:S(2)}, u32[]{:S(2)}) collective-permute-start(bf16[16,8192]{1,0:T(8,128)(2,1)} %get-tuple-element.7), channel_id=1, source_target_pairs={{0,29},{1,28},{2,31},{3,30},{4,25},{5,24},{6,27},{7,26},{8,5},{9,4... | collective-permute-start | bytes 786440 | tf_op jit(solution)/shard_map/ppermute | solution.py:40
  139.0 28.8 %collective-permute-start.29 = (bf16[16,8192]{1,0:T(8,128)(2,1)S(1)}, bf16[16,8192]{1,0:T(8,128)(2,1)S(1)}, u32[]{:S(2)}, u32[]{:S(2)}) collective-permute-start(bf16[16,8192]{1,0:T(8,128)(2,1)S(1)} %copy-done.13), channel_id=1, source_target_pairs={{0,28},{1,29},{2,30},{3,31},{4,24},{5,25},{6,26},{7,27},{8,4},{9,5... | collective-permute-start | bytes 786440 | tf_op jit(solution)/shard_map/ppermute | solution.py:40
  159.8 17.0 %collective-permute-start.31 = (bf16[16,8192]{1,0:T(8,128)(2,1)S(1)}, bf16[16,8192]{1,0:T(8,128)(2,1)S(1)}, u32[]{:S(2)}, u32[]{:S(2)}) collective-permute-start(bf16[16,8192]{1,0:T(8,128)(2,1)S(1)} %copy-done.11), channel_id=1, source_target_pairs={{0,26},{1,27},{2,24},{3,25},{4,30},{5,31},{6,28},{7,29},{8,2},{9,3... | collective-permute-start | bytes 786440 | tf_op jit(solution)/shard_map/ppermute | solution.py:40
  178.2 33.0 %collective-permute-start.11 = (bf16[16,8192]{1,0:T(8,128)(2,1)S(1)}, bf16[16,8192]{1,0:T(8,128)(2,1)S(1)}, u32[]{:S(2)}, u32[]{:S(2)}) collective-permute-start(bf16[16,8192]{1,0:T(8,128)(2,1)S(1)} %get-tuple-element.22), channel_id=1, source_target_pairs={{0,13},{1,12},{2,15},{3,14},{4,9},{5,8},{6,11},{7,10},{8,21},{9,20... | collective-permute-start | bytes 786440 | tf_op jit(solution)/shard_map/ppermute | solution.py:40
  183.4 32.4 %collective-permute-start.12 = (bf16[16,8192]{1,0:T(8,128)(2,1)S(1)}, bf16[16,8192]{1,0:T(8,128)(2,1)S(1)}, u32[]{:S(2)}, u32[]{:S(2)}) collective-permute-start(bf16[16,8192]{1,0:T(8,128)(2,1)S(1)} %get-tuple-element.21), channel_id=1, source_target_pairs={{0,12},{1,13},{2,14},{3,15},{4,8},{5,9},{6,10},{7,11},{8,20},{9,21... | collective-permute-start | bytes 786440 | tf_op jit(solution)/shard_map/ppermute | solution.py:40
  187.5 35.5 %collective-permute-start.13 = (bf16[16,8192]{1,0:T(8,128)(2,1)S(1)}, bf16[16,8192]{1,0:T(8,128)(2,1)S(1)}, u32[]{:S(2)}, u32[]{:S(2)}) collective-permute-start(bf16[16,8192]{1,0:T(8,128)(2,1)S(1)} %get-tuple-element.20), channel_id=1, source_target_pairs={{0,11},{1,10},{2,9},{3,8},{4,15},{5,14},{6,13},{7,12},{8,19},{9,18... | collective-permute-start | bytes 786440 | tf_op jit(solution)/shard_map/ppermute | solution.py:40
  211.2 15.6 %collective-permute-start.14 = (bf16[16,8192]{1,0:T(8,128)(2,1)S(1)}, bf16[16,8192]{1,0:T(8,128)(2,1)S(1)}, u32[]{:S(2)}, u32[]{:S(2)}) collective-permute-start(bf16[16,8192]{1,0:T(8,128)(2,1)S(1)} %get-tuple-element.19), channel_id=1, source_target_pairs={{0,10},{1,11},{2,8},{3,9},{4,14},{5,15},{6,12},{7,13},{8,18},{9,19... | collective-permute-start | bytes 786440 | tf_op jit(solution)/shard_map/ppermute | solution.py:40
  (27 other events, 505.0 us)

commit v2 on v0

v2 whole, which is shorter than its diff:
```python
import functools

import jax
import jax.numpy as jnp
from jax import lax
from jax.experimental import pallas as pl
from jax.experimental.pallas import tpu as pltpu
from jax.sharding import PartitionSpec as P

BLOCK = 16
OUT, HAS, SAVED = range(3)
FIELDS = 3
VMEM_LIMIT = 48 * 1024 * 1024
ACROSS = ((1,), (1,))


def after(value, *others):
    return lax.optimization_barrier((value, others))[0]


def shifted(value, steps):
    count = lax.axis_size("pipe")
    return lax.ppermute(value, "pipe", [(p, (p + steps) % count) for p in range(count)])


def swap(pieces):
    count = lax.axis_size("bundle")
    pieces = pieces.reshape(count, -1, pieces.shape[1])
    pieces = lax.all_to_all(pieces, "bundle", split_axis=0, concat_axis=0, tiled=True)
    return pieces.reshape(-1, pieces.shape[2])


def plan_one(bundles, blocks_dev, dev, mask, plan):
    def scan(source, bundle):
        active = at = jnp.int32(0)
        for j in range(blocks_dev):
            one = mask[bundle, source * blocks_dev + j]
            active, at = active + one, at + j * one
        return active, at

    for b in range(bundles):
        plan[HAS * bundles + b], plan[OUT * bundles + b] = scan(dev, b)
        plan[SAVED * bundles + b] = b * blocks_dev + scan(b, dev)[1]


def plan_kernel(bundles, blocks_dev, dev_ref, mask_f, mask_b, plan_f, plan_b):
    plan_one(bundles, blocks_dev, dev_ref[0], mask_f, plan_f)
    plan_one(bundles, blocks_dev, dev_ref[0], mask_b, plan_b)


def plans_of(mask_f, mask_b, device, blocks_dev):
    bundles = mask_f.shape[1]
    smem = pl.BlockSpec(memory_space=pltpu.SMEM)
    return pl.pallas_call(
        functools.partial(plan_kernel, bundles, blocks_dev),
        out_shape=[jax.ShapeDtypeStruct((FIELDS * bundles,), jnp.int32)] * 2,
        in_specs=[smem] * 3,
        out_specs=[smem] * 2,
    )(device[None], mask_f.T, mask_b.T)


def chunk_of(width, most):
    chunk = min(width, most)
    while width % chunk:
        chunk //= 2
    return chunk


def chunked(kernel, plan, ins, out_rows, most, scratch=()):
    width = ins[0].shape[1]
    chunk = chunk_of(width, most)

    def spec(rows):
        return pl.BlockSpec((rows, chunk), lambda c, *_: (0, c))

    return pl.pallas_call(
        kernel,
        out_shape=jax.ShapeDtypeStruct((out_rows, width), jnp.bfloat16),
        grid_spec=pltpu.PrefetchScalarGridSpec(
            num_scalar_prefetch=1,
            grid=(width // chunk,),
            in_specs=[spec(a.shape[0]) for a in ins],
            out_specs=spec(out_rows),
            scratch_shapes=[pltpu.VMEM((r, chunk), t) for r, t in scratch],
        ),
        compiler_params=pltpu.CompilerParams(vmem_limit_bytes=VMEM_LIMIT),
    )(plan, *ins)


def block_at(index):
    return pl.ds(pl.multiple_of(index * BLOCK, BLOCK), BLOCK)


def pack(rows, plan, bundles):
    def kernel(plan_ref, rows_ref, out):
        for b in range(bundles):
            out[b * BLOCK : (b + 1) * BLOCK] = rows_ref[block_at(plan_ref[OUT * bundles + b]), :]

    return chunked(kernel, plan, [rows], bundles * BLOCK, 4096)


def placed(plan, base, parts, bundles):
    def kernel(plan_ref, base_ref, parts_ref, out, total):
        total[...] = base_ref[...].astype(jnp.float32)
        for b in range(bundles):
            weight = plan_ref[HAS * bundles + b].astype(jnp.float32)
            part = parts_ref[b * BLOCK : (b + 1) * BLOCK].astype(jnp.float32)
            total[block_at(plan_ref[OUT * bundles + b]), :] += part * weight
        out[...] = total[...].astype(jnp.bfloat16)

    rows = base.shape[0]
    return chunked(kernel, plan, [base, parts], rows, 4096, [(rows, jnp.float32)])


def middle(kernel, plan, rows, weights, saved, first_weights):
    height, width = rows.shape
    chunk = chunk_of(width, 4096)
    steps = width // chunk
    units = min(weights[0].shape)
    specs = [pl.BlockSpec((height, chunk), lambda s, c, *_: (0, jnp.where(s == 0, c, steps - 1)))]
    for i, weight in enumerate(weights):
        tall = weight.shape[0] == width

        def at(s, c, *_, early=i in first_weights, tall=tall):
            where = jnp.where(s == 0, c, steps - 1) if early else jnp.where(s == 0, 0, c)
            return (where, 0) if tall else (0, where)

        shape = (chunk, weight.shape[1]) if tall else (weight.shape[0], chunk)
        specs.append(pl.BlockSpec(shape, at))
    specs += [pl.BlockSpec(a.shape, lambda s, c, *_: (0, 0)) for a in saved]
    return pl.pallas_call(
        kernel,
        out_shape=jax.ShapeDtypeStruct((height, width), jnp.bfloat16),
        grid_spec=pltpu.PrefetchScalarGridSpec(
            num_scalar_prefetch=1,
            grid=(2, steps),
            in_specs=specs,
            out_specs=pl.BlockSpec((height, chunk), lambda s, c, *_: (0, jnp.where(s == 0, 0, c))),
            scratch_shapes=[
                pltpu.VMEM((height, 2 * units), jnp.float32),
                pltpu.VMEM((height, 2 * units), jnp.bfloat16),
            ],
        ),
        compiler_params=pltpu.CompilerParams(vmem_limit_bytes=VMEM_LIMIT),
    )(plan, rows, *weights, *saved)


def dot(left, right, dims=((1,), (0,))):
    return lax.dot_general(left, right, (dims, ((), ())), preferred_element_type=jnp.float32)


def forward(plan, rows, gate_w, up_w, down_w):
    units = gate_w.shape[1]

    def kernel(plan_ref, rows_ref, gate_ref, up_ref, down_ref, out, total_ref, hidden_ref):
        first, start = pl.program_id(0) == 0, pl.program_id(1) == 0

        @pl.when(first & start)
        def _():
            total_ref[...] = jnp.zeros_like(total_ref)

        @pl.when(first)
        def _():
            total_ref[:, :units] += dot(rows_ref[...], gate_ref[...])
            total_ref[:, units:] += dot(rows_ref[...], up_ref[...])

        @pl.when(jnp.logical_not(first) & start)
        def _():
            hidden = jnp.maximum(total_ref[:, :units], 0.0) * total_ref[:, units:]
            hidden_ref[:, :units] = hidden.astype(jnp.bfloat16)

        @pl.when(jnp.logical_not(first))
        def _():
            out[...] = dot(hidden_ref[:, :units], down_ref[...]).astype(jnp.bfloat16)

    return middle(kernel, plan, rows, [gate_w, up_w, down_w], [], (0, 1))


def backward(plan, rows, gate_w, up_w, down_w, saved_gate, saved_up, bundles):
    units = gate_w.shape[1]

    def kernel(
        plan_ref, rows_ref, gate_ref, up_ref, down_ref, gate_saved, up_saved, out, total_ref, grad_ref
    ):
        first, start = pl.program_id(0) == 0, pl.program_id(1) == 0

        @pl.when(first & start)
        def _():
            total_ref[...] = jnp.zeros_like(total_ref)

        @pl.when(first)
        def _():
            total_ref[:, :units] += dot(rows_ref[...], down_ref[...], ACROSS)

        @pl.when(jnp.logical_not(first) & start)
        def _():
            for b in range(bundles):
                place, at = pl.ds(b * BLOCK, BLOCK), block_at(plan_ref[SAVED * bundles + b])
                gate = gate_saved[at, :].astype(jnp.float32)
                up = up_saved[at, :].astype(jnp.float32)
                grad = total_ref[place, :units]
                grad_gate = jnp.where(gate > 0, grad * up, 0.0)
                grad_ref[place, :units] = grad_gate.astype(jnp.bfloat16)
                grad_ref[place, units:] = (grad * jnp.maximum(gate, 0.0)).astype(jnp.bfloat16)

        @pl.when(jnp.logical_not(first))
        def _():
            total = dot(grad_ref[:, :units], gate_ref[...], ACROSS)
            total += dot(grad_ref[:, units:], up_ref[...], ACROSS)
            out[...] = total.astype(jnp.bfloat16)

    return middle(kernel, plan, rows, [gate_w, up_w, down_w], [saved_gate, saved_up], (2,))


def per_device(act_fwd, grad_in, w_gate, w_up, w_down, saved_gate, saved_up, mask_fwd, mask_bwd):
    bundles = lax.axis_size("bundle")
    device = lax.axis_index("bundle")
    blocks_dev = act_fwd.shape[1] // BLOCK
    gate_w, up_w, down_w = w_gate[0], w_up[0], w_down[0]

    plan_f, plan_b = plans_of(mask_fwd[0], mask_bwd[0], device, blocks_dev)
    packed_f = pack(act_fwd[0], plan_f, bundles)
    rows_f = swap(packed_f)
    packed_b = pack(after(grad_in[0], packed_f), plan_b, bundles)
    base_f = shifted(after(act_fwd[0], packed_b), 1)
    base_b = shifted(after(grad_in[0], base_f), -1)
    next_mask_f = shifted(after(mask_fwd[0], packed_b), 1)
    next_mask_b = shifted(after(mask_bwd[0], packed_b), -1)
    next_plan_f, next_plan_b = plans_of(next_mask_f, next_mask_b, device, blocks_dev)

    rows_f = after(rows_f, base_b, next_plan_f)
    rows_b = swap(after(packed_b, rows_f))
    parts_f = shifted(forward(plan_f, rows_f, gate_w, up_w, down_w), 1)
    back_f = swap(after(parts_f, rows_b))
    parts_b = backward(
        plan_b, rows_b, gate_w, up_w, down_w, saved_gate[0], saved_up[0], bundles
    )
    parts_b = shifted(parts_b, -1)
    next_forward = placed(next_plan_f, base_f, back_f, bundles)
    back_b = swap(after(parts_b, back_f))
    next_backward = placed(next_plan_b, base_b, back_b, bundles)
    return (next_forward[None], next_backward[None])


def solution(mesh):
    in_specs = (
        P("pipe", "bundle", None),
        P("pipe", "bundle", None),
        P("pipe", None, "bundle"),
        P("pipe", None, "bundle"),
        P("pipe", "bundle", None),
        P("pipe", None, "bundle"),
        P("pipe", None, "bundle"),
        P("pipe", None, None),
        P("pipe", None, None),
    )
    out_specs = (P("pipe", "bundle", None), P("pipe", "bundle", None))
    return jax.shard_map(
        per_device, mesh=mesh, in_specs=in_specs, out_specs=out_specs, check_vma=False
    )
```

time: 242 us -> 223 us (0.921)
  matrix products: 26.5 us -> 0 us
  Pallas kernels: 0 us -> 25.8 us
  waiting for transfers between devices: 181 us -> 168 us
  local copies, waits for them, and re-layouts: 10.8 us -> 4.71 us
    all_to_all x4, waiting for transfers between devices: 167 us -> 93.7 us  [swap(): lax.all_to_all(pieces, 'bundle', split_axis=0, concat_axis=0, tiled=True)]
    ppermute x2 -> x6, waiting for transfers between devices: 14.2 us -> 74.1 us  [shifted(): lax.ppermute(value, 'pipe', [(p, (p + steps) % count) for p in range(coun...]
    dot_general x11 -> x0, matrix products: 26.5 us -> none  [the longest x2 8.3 us: place_parts(): jnp.einsum('bj,btd->jtd', select, parts, preferred_element_type=jnp.float32)]
    pallas_call x0 -> x8, Pallas kernels: none -> 25.8 us  [the longest x2 12 us: middle(): pl.pallas_call(kernel, out_shape=jax.ShapeDtypeStruct((height, width), jn...]
    convert_element_type x3 -> x0, local copies, waits for them, and re-layouts: 5.07 us -> none  [the longest x2 4.98 us: pack_rows(): return packed.astype(jnp.bfloat16)]
    ppermute x2 -> x6, starting transfers between devices: 0.06 us -> 2.69 us  [shifted(): lax.ppermute(value, 'pipe', [(p, (p + steps) % count) for p in range(coun...]
    dot_general x2 -> x0, local copies, waits for them, and re-layouts: 2.44 us -> none  [place_parts(): jnp.einsum('bj,btd->jtd', select, parts, preferred_element_type=jnp.float32)]
  transfers between devices with their start and end apart: 6 -> 10, of which waited for: 5 -> 9; matrix products, arithmetic and copies ran while one was open for 13% -> 0% of each run, Pallas kernels for 0% -> 8%
where the time goes in v2:
time: 223 us; the launch traced here: 222 us
  waiting for transfers between devices  168 us (75%)
  Pallas kernels  25.8 us (12%)
  starting transfers between devices  22.8 us (10%)
  local copies, waits for them, and re-layouts  4.71 us (2%)
    all_to_all x4, waiting for transfers between devices, swap(): lax.all_to_all(pieces, 'bundle', split_axis=0, concat_axis=0, tiled=True)  93.7 us
    ppermute x6, waiting for transfers between devices, shifted(): lax.ppermute(value, 'pipe', [(p, (p + steps) % count) for p in range(coun...  74.1 us
    all_to_all x4, starting transfers between devices, swap(): lax.all_to_all(pieces, 'bundle', split_axis=0, concat_axis=0, tiled=True)  20.1 us
    pallas_call x2, Pallas kernels, middle(): pl.pallas_call(kernel, out_shape=jax.ShapeDtypeStruct((height, width), jn...  12 us
    pallas_call x4, Pallas kernels, chunked(): pl.pallas_call(kernel, out_shape=jax.ShapeDtypeStruct((out_rows, width),...  10.9 us
    unnamed x32, local copies, waits for them, and re-layouts  4.71 us
  transfers between devices with their start and end apart: 10, of which 9 were waited for; matrix products, arithmetic and copies ran while one was open for 0% of the time, Pallas kernels for 8%

profile of v2, /device:TPU:0, one launch (start us, length us, event | category | flops | bytes accessed | tf_op | source)
XLA Modules:
  0.0 221.9 jit_solution(15236437845818688337)
XLA Ops:
  0.6 1.5 shard_map.104
  2.1 1.2 copy-done.2
  4.0 2.0 shard_map.105
  6.0 7.4 %all-to-all-start = ((bf16[8,16,8192]{2,1,0:T(8,128)(2,1)}), bf16[8,16,8192]{2,1,0:T(8,128)(2,1)S(1)}, u32[]{:S(2)}, u32[]{:S(2)}) async-start(bf16[8,16,8192]{2,1,0:T(8,128)(2,1)} %bitcast.9), calls=%async_computation | async-start | bytes 4194304 | tf_op jit(solution)/shard_map/all_to_all | solution.py:29
  13.5 3.0 %shard_map.106 = bf16[128,8192]{1,0:T(8,128)(2,1)} custom-call(s32[24]{0:T(128)S(1)} %copy-done.6, bf16[64,8192]{1,0:T(8,128)(2,1)} %bitcast.5.rows_ref), custom_call_target="tpu_custom_call" | custom-call | tf_op jit(solution)/shard_map/pallas_call | solution.py:76
  16.5 14.2 %collective-permute-done.2.base_ref = bf16[64,8192]{1,0:T(8,128)(2,1)S(1)} collective-permute-done((bf16[64,8192]{1,0:T(8,128)(2,1)S(1)}, bf16[64,8192]{1,0:T(8,128)(2,1)S(1)}, u32[]{:S(2)}, u32[]{:S(2)}) %collective-permute-start.2) | collective-permute-done | bytes 1048608 | tf_op jit(solution)/shard_map/ppermute | solution.py:23
  32.2 1.2 collective-permute-start.1
  33.4 1.3 collective-permute-done
  34.7 9.6 %collective-permute-done.1 = s32[32,8]{0,1:T(8,128)S(1)} collective-permute-done((s32[32,8]{0,1:T(8,128)S(1)}, s32[32,8]{0,1:T(8,128)S(1)}, u32[]{:S(2)}, u32[]{:S(2)}) %collective-permute-start.1) | collective-permute-done | bytes 1056 | tf_op jit(solution)/shard_map/ppermute | solution.py:23
  45.0 1.5 shard_map.107
  46.4 15.3 %all-to-all-done = bf16[8,16,8192]{2,1,0:T(8,128)(2,1)S(1)} async-done(((bf16[8,16,8192]{2,1,0:T(8,128)(2,1)}), bf16[8,16,8192]{2,1,0:T(8,128)(2,1)S(1)}, u32[]{:S(2)}, u32[]{:S(2)}) %all-to-all-start) | async-done | bytes 2097184 | tf_op jit(solution)/shard_map/all_to_all | solution.py:29
  61.7 4.5 %all-to-all-start.1 = ((bf16[8,16,8192]{2,1,0:T(8,128)(2,1)}), bf16[8,16,8192]{2,1,0:T(8,128)(2,1)}, u32[]{:S(2)}, u32[]{:S(2)}) async-start(bf16[8,16,8192]{2,1,0:T(8,128)(2,1)} %bitcast.14), calls=%async_computation.1 | async-start | bytes 4194304 | tf_op jit(solution)/shard_map/all_to_all | solution.py:29
  66.2 5.8 %shard_map.108 = bf16[128,8192]{1,0:T(8,128)(2,1)S(1)} custom-call(s32[24]{0:T(128)S(1)} %copy-done.8, bf16[128,8192]{1,0:T(8,128)(2,1)S(1)} %bitcast.27, bf16[8192,128]{1,0:T(8,128)(2,1)} %bitcast.32, bf16[8192,128]{1,0:T(8,128)(2,1)} %bitcast.34, bf16[128,8192]{1,0:T(8,128)(2,1)} %bitcast.36), custom_call_target="tpu_custom_call" | custom-call | tf_op jit(solution)/shard_map/pallas_call | solution.py:131
  72.0 25.4 %collective-permute-done.4 = bf16[128,8192]{1,0:T(8,128)(2,1)S(1)} collective-permute-done((bf16[128,8192]{1,0:T(8,128)(2,1)S(1)}, bf16[128,8192]{1,0:T(8,128)(2,1)S(1)}, u32[]{:S(2)}, u32[]{:S(2)}) %collective-permute-start.4) | collective-permute-done | bytes 2097184 | tf_op jit(solution)/shard_map/ppermute | solution.py:23
  97.5 16.5 %all-to-all-done.1 = bf16[8,16,8192]{2,1,0:T(8,128)(2,1)} async-done(((bf16[8,16,8192]{2,1,0:T(8,128)(2,1)}), bf16[8,16,8192]{2,1,0:T(8,128)(2,1)}, u32[]{:S(2)}, u32[]{:S(2)}) %all-to-all-start.1) | async-done | bytes 2097184 | tf_op jit(solution)/shard_map/all_to_all | solution.py:29
  114.0 3.8 %all-to-all-start.2 = ((bf16[8,16,8192]{2,1,0:T(8,128)(2,1)}), bf16[8,16,8192]{2,1,0:T(8,128)(2,1)S(1)}, u32[]{:S(2)}, u32[]{:S(2)}) async-start(bf16[8,16,8192]{2,1,0:T(8,128)(2,1)} %bitcast.38), calls=%async_computation.2 | async-start | bytes 4194304 | tf_op jit(solution)/shard_map/all_to_all | solution.py:29
  117.8 6.2 %shard_map.110 = bf16[128,8192]{1,0:T(8,128)(2,1)S(1)} custom-call(s32[24]{0:T(128)S(1)} %copy-done.6, bf16[128,8192]{1,0:T(8,128)(2,1)} %bitcast.15.rows_ref, bf16[8192,128]{1,0:T(8,128)(2,1)} %bitcast.33, bf16[8192,128]{1,0:T(8,128)(2,1)} %bitcast.35, bf16[128,8192]{1,0:T(8,128)(2,1)} %bitcast.37, bf16[512,128]{1,0:T(8,128)(2,1)S(1)} %bitcast.30, ...), custom_call_target="tpu_custom_call" | custom-call | tf_op jit(solution)/shard_map/pallas_call | solution.py:131
  124.9 23.6 %collective-permute-done.5 = bf16[128,8192]{1,0:T(8,128)(2,1)} collective-permute-done((bf16[128,8192]{1,0:T(8,128)(2,1)S(1)}, bf16[128,8192]{1,0:T(8,128)(2,1)}, u32[]{:S(2)}, u32[]{:S(2)}) %collective-permute-start.5) | collective-permute-done | bytes 2097184 | tf_op jit(solution)/shard_map/ppermute | solution.py:23
  148.4 17.8 %all-to-all-done.2 = bf16[8,16,8192]{2,1,0:T(8,128)(2,1)S(1)} async-done(((bf16[8,16,8192]{2,1,0:T(8,128)(2,1)}), bf16[8,16,8192]{2,1,0:T(8,128)(2,1)S(1)}, u32[]{:S(2)}, u32[]{:S(2)}) %all-to-all-start.2) | async-done | bytes 2097184 | tf_op jit(solution)/shard_map/all_to_all | solution.py:29
  166.2 4.5 %all-to-all-start.3 = ((bf16[8,16,8192]{2,1,0:T(8,128)(2,1)}), bf16[8,16,8192]{2,1,0:T(8,128)(2,1)}, u32[]{:S(2)}, u32[]{:S(2)}) async-start(bf16[8,16,8192]{2,1,0:T(8,128)(2,1)} %bitcast.21), calls=%async_computation.3 | async-start | bytes 4194304 | tf_op jit(solution)/shard_map/all_to_all | solution.py:29
  170.7 1.2 copy-done.1
  171.9 2.4 %shard_map.109 = bf16[64,8192]{1,0:T(8,128)(2,1)} custom-call(s32[24]{0:T(128)S(1)} %copy-done.10, bf16[64,8192]{1,0:T(8,128)(2,1)S(1)} %copy-done.1, bf16[128,8192]{1,0:T(8,128)(2,1)S(1)} %bitcast.26), custom_call_target="tpu_custom_call" | custom-call | tf_op jit(solution)/shard_map/pallas_call | solution.py:76
  174.3 44.2 %all-to-all-done.3 = bf16[8,16,8192]{2,1,0:T(8,128)(2,1)} async-done(((bf16[8,16,8192]{2,1,0:T(8,128)(2,1)}), bf16[8,16,8192]{2,1,0:T(8,128)(2,1)}, u32[]{:S(2)}, u32[]{:S(2)}) %all-to-all-start.3) | async-done | bytes 2097184 | tf_op jit(solution)/shard_map/all_to_all | solution.py:29
  218.5 3.5 %shard_map.111 = bf16[64,8192]{1,0:T(8,128)(2,1)} custom-call(s32[24]{0:T(128)S(1)} %copy-done.9, bf16[64,8192]{1,0:T(8,128)(2,1)S(1)} %collective-permute-done.3.base_ref, bf16[128,8192]{1,0:T(8,128)(2,1)} %bitcast.22.parts_ref), custom_call_target="tpu_custom_call" | custom-call | tf_op jit(solution)/shard_map/pallas_call | solution.py:76
  (36 shorter events, 3.7 us)
Async XLA Ops:
  2.1 1.2 copy-start.2
  6.0 7.4 %copy-start.6 = (s32[24]{0:T(128)S(1)}, s32[24]{0:T(128)}, u32[]{:S(2)}) copy-start(s32[24]{0:T(128)} %get-tuple-element.15.plan_ref) | copy-start | bytes 292
  6.0 55.7 %all-to-all-start = ((bf16[8,16,8192]{2,1,0:T(8,128)(2,1)}), bf16[8,16,8192]{2,1,0:T(8,128)(2,1)S(1)}, u32[]{:S(2)}, u32[]{:S(2)}) async-start(bf16[8,16,8192]{2,1,0:T(8,128)(2,1)} %bitcast.9), calls=%async_computation | async-start | bytes 4194304 | tf_op jit(solution)/shard_map/all_to_all | solution.py:29
  13.4 3.0 %copy-start.3 = (bf16[1,64,8192]{2,1,0:T(8,128)(2,1)S(1)}, bf16[1,64,8192]{2,1,0:T(8,128)(2,1)}, u32[]{:S(2)}) copy-start(bf16[1,64,8192]{2,1,0:T(8,128)(2,1)} %param.9) | copy-start | bytes 3145732
  13.4 18.2 %copy-start.12 = (s32[1,32,8]{1,2,0:T(8,128)S(1)}, s32[1,32,8]{1,2,0:T(8,128)}, u32[]{:S(2)}) copy-start(s32[1,32,8]{1,2,0:T(8,128)} %param.16) | copy-start | bytes 3076
  13.5 18.7 %copy-start.13 = (s32[1,32,8]{1,2,0:T(8,128)S(1)}, s32[1,32,8]{1,2,0:T(8,128)}, u32[]{:S(2)}) copy-start(s32[1,32,8]{1,2,0:T(8,128)} %param.17) | copy-start | bytes 3076
  16.5 14.2 %collective-permute-start.2 = (bf16[64,8192]{1,0:T(8,128)(2,1)S(1)}, bf16[64,8192]{1,0:T(8,128)(2,1)S(1)}, u32[]{:S(2)}, u32[]{:S(2)}) collective-permute-start(bf16[64,8192]{1,0:T(8,128)(2,1)S(1)} %bitcast.29), channel_id=1, source_target_pairs={{0,8},{8,16},{16,24},{24,0},{1,9},{9,17},{17,25},{25,1},{2,10},{10... | collective-permute-start | bytes 3145736 | tf_op jit(solution)/shard_map/ppermute | solution.py:23
  30.7 1.0 copy-start
  31.7 14.7 %collective-permute-start.3 = (bf16[64,8192]{1,0:T(8,128)(2,1)}, bf16[64,8192]{1,0:T(8,128)(2,1)S(1)}, u32[]{:S(2)}, u32[]{:S(2)}) collective-permute-start(bf16[64,8192]{1,0:T(8,128)(2,1)} %bitcast.5.rows_ref), channel_id=1, source_target_pairs={{0,24},{8,0},{16,8},{24,16},{1,25},{9,1},{17,9},{25,17},{2,26},{10... | collective-permute-start | bytes 3145736 | tf_op jit(solution)/shard_map/ppermute | solution.py:23
  31.7 3.0 %collective-permute-start = (s32[32,8]{0,1:T(8,128)S(1)}, s32[32,8]{0,1:T(8,128)S(1)}, u32[]{:S(2)}, u32[]{:S(2)}) collective-permute-start(s32[32,8]{0,1:T(8,128)S(1)} %bitcast.42), channel_id=1, source_target_pairs={{0,8},{8,16},{16,24},{24,0},{1,9},{9,17},{17,25},{25,1},{2,10},{10... | collective-permute-start | bytes 3080 | tf_op jit(solution)/shard_map/ppermute | solution.py:23
  32.2 12.2 %collective-permute-start.1 = (s32[32,8]{0,1:T(8,128)S(1)}, s32[32,8]{0,1:T(8,128)S(1)}, u32[]{:S(2)}, u32[]{:S(2)}) collective-permute-start(s32[32,8]{0,1:T(8,128)S(1)} %bitcast.44), channel_id=1, source_target_pairs={{0,24},{8,0},{16,8},{24,16},{1,25},{9,1},{17,9},{25,17},{2,26},{10... | collective-permute-start | bytes 3080 | tf_op jit(solution)/shard_map/ppermute | solution.py:23
  34.7 9.6 %copy-start.14 = (s32[32,8]{0,1:T(8,128)}, s32[32,8]{0,1:T(8,128)S(1)}, u32[]{:S(2)}) copy-start(s32[32,8]{0,1:T(8,128)S(1)} %collective-permute-done) | copy-start | bytes 3076
  61.7 4.5 %copy-start.8 = (s32[24]{0:T(128)S(1)}, s32[24]{0:T(128)}, u32[]{:S(2)}) copy-start(s32[24]{0:T(128)} %get-tuple-element.16.plan_ref) | copy-start | bytes 292
  61.7 52.3 %all-to-all-start.1 = ((bf16[8,16,8192]{2,1,0:T(8,128)(2,1)}), bf16[8,16,8192]{2,1,0:T(8,128)(2,1)}, u32[]{:S(2)}, u32[]{:S(2)}) async-start(bf16[8,16,8192]{2,1,0:T(8,128)(2,1)} %bitcast.14), calls=%async_computation.1 | async-start | bytes 4194304 | tf_op jit(solution)/shard_map/all_to_all | solution.py:29
  71.9 25.5 %collective-permute-start.4 = (bf16[128,8192]{1,0:T(8,128)(2,1)S(1)}, bf16[128,8192]{1,0:T(8,128)(2,1)S(1)}, u32[]{:S(2)}, u32[]{:S(2)}) collective-permute-start(bf16[128,8192]{1,0:T(8,128)(2,1)S(1)} %shard_map.108), channel_id=1, source_target_pairs={{0,8},{8,16},{16,24},{24,0},{1,9},{9,17},{17,25},{25,1},{2,10},{10... | collective-permute-start | bytes 6291464 | tf_op jit(solution)/shard_map/ppermute | solution.py:23
  97.5 16.5 %copy-start.11 = (bf16[128,8192]{1,0:T(8,128)(2,1)}, bf16[128,8192]{1,0:T(8,128)(2,1)S(1)}, u32[]{:S(2)}) copy-start(bf16[128,8192]{1,0:T(8,128)(2,1)S(1)} %collective-permute-done.4) | copy-start | bytes 6291460
  114.0 3.8 %copy-start.4 = (bf16[1,512,128]{2,1,0:T(8,128)(2,1)S(1)}, bf16[1,512,128]{2,1,0:T(8,128)(2,1)}, u32[]{:S(2)}) copy-start(bf16[1,512,128]{2,1,0:T(8,128)(2,1)} %param.14) | copy-start | bytes 393220
  114.0 3.8 %copy-start.5 = (bf16[1,512,128]{2,1,0:T(8,128)(2,1)S(1)}, bf16[1,512,128]{2,1,0:T(8,128)(2,1)}, u32[]{:S(2)}) copy-start(bf16[1,512,128]{2,1,0:T(8,128)(2,1)} %param.15) | copy-start | bytes 393220
  114.0 52.2 %all-to-all-start.2 = ((bf16[8,16,8192]{2,1,0:T(8,128)(2,1)}), bf16[8,16,8192]{2,1,0:T(8,128)(2,1)S(1)}, u32[]{:S(2)}, u32[]{:S(2)}) async-start(bf16[8,16,8192]{2,1,0:T(8,128)(2,1)} %bitcast.38), calls=%async_computation.2 | async-start | bytes 4194304 | tf_op jit(solution)/shard_map/all_to_all | solution.py:29
  124.0 24.4 %collective-permute-start.5 = (bf16[128,8192]{1,0:T(8,128)(2,1)S(1)}, bf16[128,8192]{1,0:T(8,128)(2,1)}, u32[]{:S(2)}, u32[]{:S(2)}) collective-permute-start(bf16[128,8192]{1,0:T(8,128)(2,1)S(1)} %shard_map.110), channel_id=1, source_target_pairs={{0,24},{8,0},{16,8},{24,16},{1,25},{9,1},{17,9},{25,17},{2,26},{10... | collective-permute-start | bytes 6291464 | tf_op jit(solution)/shard_map/ppermute | solution.py:23
  166.2 4.5 %copy-start.10 = (s32[24]{0:T(128)S(1)}, s32[24]{0:T(128)}, u32[]{:S(2)}) copy-start(s32[24]{0:T(128)} %get-tuple-element.20.plan_ref) | copy-start | bytes 292
  166.2 52.3 %all-to-all-start.3 = ((bf16[8,16,8192]{2,1,0:T(8,128)(2,1)}), bf16[8,16,8192]{2,1,0:T(8,128)(2,1)}, u32[]{:S(2)}, u32[]{:S(2)}) async-start(bf16[8,16,8192]{2,1,0:T(8,128)(2,1)} %bitcast.21), calls=%async_computation.3 | async-start | bytes 4194304 | tf_op jit(solution)/shard_map/all_to_all | solution.py:29
  170.7 1.2 copy-start.1
  171.9 46.6 %copy-start.9 = (s32[24]{0:T(128)S(1)}, s32[24]{0:T(128)}, u32[]{:S(2)}) copy-start(s32[24]{0:T(128)} %get-tuple-element.26.plan_ref) | copy-start | bytes 292
  (2 other events, 1.3 us)

commit v3 on v2

--- a/solution.py
+++ b/solution.py
@@ -11,6 +11,8 @@
 OUT, HAS, SAVED = range(3)
 FIELDS = 3
 VMEM_LIMIT = 48 * 1024 * 1024
+VMEM_MOST = 60 * 1024 * 1024
+PLACE_CHUNK = 4096
 ACROSS = ((1,), (1,))
 
 
@@ -91,25 +93,47 @@
     return pl.ds(pl.multiple_of(index * BLOCK, BLOCK), BLOCK)
 
 
-def pack(rows, plan, bundles):
-    def kernel(plan_ref, rows_ref, out):
+def pack(rows, mask, device, blocks_dev):
+    bundles, width = mask.shape[1], rows.shape[1]
+    chunk = chunk_of(width, 4096)
+
+    def kernel(dev_ref, mask_ref, rows_ref, out):
         for b in range(bundles):
-            out[b * BLOCK : (b + 1) * BLOCK] = rows_ref[block_at(plan_ref[OUT * bundles + b]), :]
-
-    return chunked(kernel, plan, [rows], bundles * BLOCK, 4096)
+            at = jnp.int32(0)
+            for j in range(1, blocks_dev):
+                at += j * mask_ref[b, dev_ref[0] * blocks_dev + j]
+            out[b * BLOCK : (b + 1) * BLOCK] = rows_ref[block_at(at), :]
+
+    return pl.pallas_call(
+        kernel,
+        out_shape=jax.ShapeDtypeStruct((bundles * BLOCK, width), jnp.bfloat16),
+        grid=(width // chunk,),
+        in_specs=[
+            pl.BlockSpec(memory_space=pltpu.SMEM),
+            pl.BlockSpec(memory_space=pltpu.SMEM),
+            pl.BlockSpec((rows.shape[0], chunk), lambda c: (0, c)),
+        ],
+        out_specs=pl.BlockSpec((bundles * BLOCK, chunk), lambda c: (0, c)),
+        compiler_params=pltpu.CompilerParams(vmem_limit_bytes=VMEM_MOST),
+    )(device[None], mask.T, rows)
 
 
 def placed(plan, base, parts, bundles):
-    def kernel(plan_ref, base_ref, parts_ref, out, total):
-        total[...] = base_ref[...].astype(jnp.float32)
+    rows = base.shape[0]
+
+    def kernel(plan_ref, base_ref, parts_ref, out):
+        row = lax.broadcasted_iota(jnp.int32, (rows, bundles * BLOCK), 0)
+        part = lax.broadcasted_iota(jnp.int32, (rows, bundles * BLOCK), 1)
+        goes = jnp.full_like(row, -1)
         for b in range(bundles):
-            weight = plan_ref[HAS * bundles + b].astype(jnp.float32)
-            part = parts_ref[b * BLOCK : (b + 1) * BLOCK].astype(jnp.float32)
-            total[block_at(plan_ref[OUT * bundles + b]), :] += part * weight
-        out[...] = total[...].astype(jnp.bfloat16)
-
-    rows = base.shape[0]
-    return chunked(kernel, plan, [base, parts], rows, 4096, [(rows, jnp.float32)])
+            first = plan_ref[OUT * bundles + b] * BLOCK - b * BLOCK
+            held = (part >= b * BLOCK) & (part < (b + 1) * BLOCK) & (plan_ref[HAS * bundles + b] != 0)
+            goes = jnp.where(held, part + first, goes)
+        pick = jnp.where(goes == row, 1.0, 0.0).astype(jnp.bfloat16)
+        total = base_ref[...].astype(jnp.float32) + dot(pick, parts_ref[...])
+        out[...] = total.astype(jnp.bfloat16)
+
+    return chunked(kernel, plan, [base, parts], rows, PLACE_CHUNK)
 
 
 def middle(kernel, plan, rows, weights, saved, first_weights):
@@ -218,10 +242,10 @@
     blocks_dev = act_fwd.shape[1] // BLOCK
     gate_w, up_w, down_w = w_gate[0], w_up[0], w_down[0]
 
-    plan_f, plan_b = plans_of(mask_fwd[0], mask_bwd[0], device, blocks_dev)
-    packed_f = pack(act_fwd[0], plan_f, bundles)
+    packed_f = pack(act_fwd[0], mask_fwd[0], device, blocks_dev)
     rows_f = swap(packed_f)
-    packed_b = pack(after(grad_in[0], packed_f), plan_b, bundles)
+    packed_b = pack(after(grad_in[0], packed_f), mask_bwd[0], device, blocks_dev)
+    plan_f, plan_b = plans_of(mask_fwd[0], after(mask_bwd[0], packed_b), device, blocks_dev)
     base_f = shifted(after(act_fwd[0], packed_b), 1)
     base_b = shifted(after(grad_in[0], base_f), -1)
     next_mask_f = shifted(after(mask_fwd[0], packed_b), 1)

time: 223 us -> 219 us (0.982)
    pallas_call x4 -> x2, Pallas kernels: 10.9 us -> 5.43 us  [chunked(): pl.pallas_call(kernel, out_shape=jax.ShapeDtypeStruct((out_rows, width),...]
    pallas_call x0 -> x2, Pallas kernels: none -> 5 us  [pack(): pl.pallas_call(kernel, out_shape=jax.ShapeDtypeStruct((bundles * BLOCK, w...]
    unnamed x32 -> x28, local copies, waits for them, and re-layouts: 4.71 us -> 3.47 us
  transfers between devices with their start and end apart: 10 -> 10, of which waited for: 9 -> 9; matrix products, arithmetic and copies ran while one was open for 0% -> 0% of each run, Pallas kernels for 8% -> 9%
where the time goes in v3:
time: 219 us
  waiting for transfers between devices  166 us (76%)
  Pallas kernels  25.3 us (12%)
  starting transfers between devices  22.6 us (10%)
  local copies, waits for them, and re-layouts  3.47 us (2%)
    all_to_all x4, waiting for transfers between devices, swap(): lax.all_to_all(pieces, 'bundle', split_axis=0, concat_axis=0, tiled=True)  92.3 us
    ppermute x6, waiting for transfers between devices, shifted(): lax.ppermute(value, 'pipe', [(p, (p + steps) % count) for p in range(coun...  74.1 us
    all_to_all x4, starting transfers between devices, swap(): lax.all_to_all(pieces, 'bundle', split_axis=0, concat_axis=0, tiled=True)  19.9 us
    pallas_call x2, Pallas kernels, middle(): pl.pallas_call(kernel, out_shape=jax.ShapeDtypeStruct((height, width), jn...  11.9 us
    pallas_call x2, Pallas kernels, chunked(): pl.pallas_call(kernel, out_shape=jax.ShapeDtypeStruct((out_rows, width),...  5.43 us
    pallas_call x2, Pallas kernels, pack(): pl.pallas_call(kernel, out_shape=jax.ShapeDtypeStruct((bundles * BLOCK, w...  5 us
  transfers between devices with their start and end apart: 10, of which 9 were waited for; matrix products, arithmetic and copies ran while one was open for 0% of the time, Pallas kernels for 9%

profile of v3, /device:TPU:0, one launch (start us, length us, event | category | flops | bytes accessed | tf_op | source)
XLA Modules:
  0.0 218.5 jit_solution(16093039172250024576)
XLA Ops:
  0.6 2.5 %shard_map.104 = bf16[128,8192]{1,0:T(8,128)(2,1)} custom-call(s32[1]{0:T(128)} %bitcast.dev_ref, s32[8,32]{1,0:T(8,128)} %bitcast.46, bf16[64,8192]{1,0:T(8,128)(2,1)} %bitcast.42), custom_call_target="tpu_custom_call" | custom-call | tf_op jit(solution)/shard_map/pallas_call | solution.py:107
  3.1 7.3 %all-to-all-start = ((bf16[8,16,8192]{2,1,0:T(8,128)(2,1)}), bf16[8,16,8192]{2,1,0:T(8,128)(2,1)S(1)}, u32[]{:S(2)}, u32[]{:S(2)}) async-start(bf16[8,16,8192]{2,1,0:T(8,128)(2,1)} %bitcast.32), calls=%async_computation | async-start | bytes 4194304 | tf_op jit(solution)/shard_map/all_to_all | solution.py:31
  10.4 2.5 %shard_map.105 = bf16[128,8192]{1,0:T(8,128)(2,1)} custom-call(s32[1]{0:T(128)} %bitcast.dev_ref, s32[8,32]{1,0:T(8,128)} %bitcast.49, bf16[64,8192]{1,0:T(8,128)(2,1)} %bitcast.44), custom_call_target="tpu_custom_call" | custom-call | tf_op jit(solution)/shard_map/pallas_call | solution.py:107
  13.0 14.2 %collective-permute-done.2.base_ref = bf16[64,8192]{1,0:T(8,128)(2,1)S(1)} collective-permute-done((bf16[64,8192]{1,0:T(8,128)(2,1)S(1)}, bf16[64,8192]{1,0:T(8,128)(2,1)S(1)}, u32[]{:S(2)}, u32[]{:S(2)}) %collective-permute-start.2) | collective-permute-done | bytes 1048608 | tf_op jit(solution)/shard_map/ppermute | solution.py:25
  27.2 1.0 copy-done
  28.7 1.2 collective-permute-start.1
  29.9 1.3 collective-permute-done
  31.2 9.6 %collective-permute-done.1 = s32[32,8]{0,1:T(8,128)S(1)} collective-permute-done((s32[32,8]{0,1:T(8,128)S(1)}, s32[32,8]{0,1:T(8,128)S(1)}, u32[]{:S(2)}, u32[]{:S(2)}) %collective-permute-start.1) | collective-permute-done | bytes 1056 | tf_op jit(solution)/shard_map/ppermute | solution.py:25
  41.4 1.5 shard_map.106
  42.9 15.7 %all-to-all-done = bf16[8,16,8192]{2,1,0:T(8,128)(2,1)S(1)} async-done(((bf16[8,16,8192]{2,1,0:T(8,128)(2,1)}), bf16[8,16,8192]{2,1,0:T(8,128)(2,1)S(1)}, u32[]{:S(2)}, u32[]{:S(2)}) %all-to-all-start) | async-done | bytes 2097184 | tf_op jit(solution)/shard_map/all_to_all | solution.py:31
  58.6 4.3 %all-to-all-start.1 = ((bf16[8,16,8192]{2,1,0:T(8,128)(2,1)}), bf16[8,16,8192]{2,1,0:T(8,128)(2,1)}, u32[]{:S(2)}, u32[]{:S(2)}) async-start(bf16[8,16,8192]{2,1,0:T(8,128)(2,1)} %bitcast.31), calls=%async_computation.1 | async-start | bytes 4194304 | tf_op jit(solution)/shard_map/all_to_all | solution.py:31
  63.0 1.5 shard_map.107
  65.1 5.8 %shard_map.108 = bf16[128,8192]{1,0:T(8,128)(2,1)S(1)} custom-call(s32[24]{0:T(128)S(1)} %copy-done.7, bf16[128,8192]{1,0:T(8,128)(2,1)S(1)} %bitcast.28, bf16[8192,128]{1,0:T(8,128)(2,1)} %bitcast.33, bf16[8192,128]{1,0:T(8,128)(2,1)} %bitcast.35, bf16[128,8192]{1,0:T(8,128)(2,1)} %bitcast.37), custom_call_target="tpu_custom_call" | custom-call | tf_op jit(solution)/shard_map/pallas_call | solution.py:155
  70.9 25.4 %collective-permute-done.4 = bf16[128,8192]{1,0:T(8,128)(2,1)S(1)} collective-permute-done((bf16[128,8192]{1,0:T(8,128)(2,1)S(1)}, bf16[128,8192]{1,0:T(8,128)(2,1)S(1)}, u32[]{:S(2)}, u32[]{:S(2)}) %collective-permute-start.4) | collective-permute-done | bytes 2097184 | tf_op jit(solution)/shard_map/ppermute | solution.py:25
  96.4 14.4 %all-to-all-done.1 = bf16[8,16,8192]{2,1,0:T(8,128)(2,1)} async-done(((bf16[8,16,8192]{2,1,0:T(8,128)(2,1)}), bf16[8,16,8192]{2,1,0:T(8,128)(2,1)}, u32[]{:S(2)}, u32[]{:S(2)}) %all-to-all-start.1) | async-done | bytes 2097184 | tf_op jit(solution)/shard_map/all_to_all | solution.py:31
  110.8 3.8 %all-to-all-start.2 = ((bf16[8,16,8192]{2,1,0:T(8,128)(2,1)}), bf16[8,16,8192]{2,1,0:T(8,128)(2,1)S(1)}, u32[]{:S(2)}, u32[]{:S(2)}) async-start(bf16[8,16,8192]{2,1,0:T(8,128)(2,1)} %bitcast.39), calls=%async_computation.2 | async-start | bytes 4194304 | tf_op jit(solution)/shard_map/all_to_all | solution.py:31
  114.6 6.2 %shard_map.110 = bf16[128,8192]{1,0:T(8,128)(2,1)S(1)} custom-call(s32[24]{0:T(128)S(1)} %copy-done.6, bf16[128,8192]{1,0:T(8,128)(2,1)} %bitcast.17.rows_ref, bf16[8192,128]{1,0:T(8,128)(2,1)} %bitcast.34, bf16[8192,128]{1,0:T(8,128)(2,1)} %bitcast.36, bf16[128,8192]{1,0:T(8,128)(2,1)} %bitcast.38, bf16[512,128]{1,0:T(8,128)(2,1)S(1)} %bitcast.29, ...), custom_call_target="tpu_custom_call" | custom-call | tf_op jit(solution)/shard_map/pallas_call | solution.py:155
  121.7 23.6 %collective-permute-done.5 = bf16[128,8192]{1,0:T(8,128)(2,1)} collective-permute-done((bf16[128,8192]{1,0:T(8,128)(2,1)S(1)}, bf16[128,8192]{1,0:T(8,128)(2,1)}, u32[]{:S(2)}, u32[]{:S(2)}) %collective-permute-start.5) | collective-permute-done | bytes 2097184 | tf_op jit(solution)/shard_map/ppermute | solution.py:25
  145.2 17.7 %all-to-all-done.2 = bf16[8,16,8192]{2,1,0:T(8,128)(2,1)S(1)} async-done(((bf16[8,16,8192]{2,1,0:T(8,128)(2,1)}), bf16[8,16,8192]{2,1,0:T(8,128)(2,1)S(1)}, u32[]{:S(2)}, u32[]{:S(2)}) %all-to-all-start.2) | async-done | bytes 2097184 | tf_op jit(solution)/shard_map/all_to_all | solution.py:31
  163.0 4.5 %all-to-all-start.3 = ((bf16[8,16,8192]{2,1,0:T(8,128)(2,1)}), bf16[8,16,8192]{2,1,0:T(8,128)(2,1)}, u32[]{:S(2)}, u32[]{:S(2)}) async-start(bf16[8,16,8192]{2,1,0:T(8,128)(2,1)} %bitcast.23), calls=%async_computation.3 | async-start | bytes 4194304 | tf_op jit(solution)/shard_map/all_to_all | solution.py:31
  167.5 1.2 copy-done.1
  168.7 2.2 %shard_map.109 = bf16[64,8192]{1,0:T(8,128)(2,1)} custom-call(s32[24]{0:T(128)S(1)} %copy-done.5, bf16[64,8192]{1,0:T(8,128)(2,1)S(1)} %copy-done.1, bf16[128,8192]{1,0:T(8,128)(2,1)S(1)} %bitcast.27), custom_call_target="tpu_custom_call" | custom-call | tf_op jit(solution)/shard_map/pallas_call | solution.py:78
  170.9 44.4 %all-to-all-done.3 = bf16[8,16,8192]{2,1,0:T(8,128)(2,1)} async-done(((bf16[8,16,8192]{2,1,0:T(8,128)(2,1)}), bf16[8,16,8192]{2,1,0:T(8,128)(2,1)}, u32[]{:S(2)}, u32[]{:S(2)}) %all-to-all-start.3) | async-done | bytes 2097184 | tf_op jit(solution)/shard_map/all_to_all | solution.py:31
  215.3 3.2 %shard_map.111 = bf16[64,8192]{1,0:T(8,128)(2,1)} custom-call(s32[24]{0:T(128)S(1)} %copy-done.4, bf16[64,8192]{1,0:T(8,128)(2,1)S(1)} %collective-permute-done.3.base_ref, bf16[128,8192]{1,0:T(8,128)(2,1)} %bitcast.24.parts_ref), custom_call_target="tpu_custom_call" | custom-call | tf_op jit(solution)/shard_map/pallas_call | solution.py:78
  (32 shorter events, 2.7 us)
Async XLA Ops:
  3.1 55.5 %all-to-all-start = ((bf16[8,16,8192]{2,1,0:T(8,128)(2,1)}), bf16[8,16,8192]{2,1,0:T(8,128)(2,1)S(1)}, u32[]{:S(2)}, u32[]{:S(2)}) async-start(bf16[8,16,8192]{2,1,0:T(8,128)(2,1)} %bitcast.32), calls=%async_computation | async-start | bytes 4194304 | tf_op jit(solution)/shard_map/all_to_all | solution.py:31
  10.4 2.6 %copy-start.9 = (bf16[1,64,8192]{2,1,0:T(8,128)(2,1)S(1)}, bf16[1,64,8192]{2,1,0:T(8,128)(2,1)}, u32[]{:S(2)}) copy-start(bf16[1,64,8192]{2,1,0:T(8,128)(2,1)} %param.9) | copy-start | bytes 3145732
  10.4 17.8 %copy-start.10 = (s32[1,32,8]{1,2,0:T(8,128)S(1)}, s32[1,32,8]{1,2,0:T(8,128)}, u32[]{:S(2)}) copy-start(s32[1,32,8]{1,2,0:T(8,128)} %param.16) | copy-start | bytes 3076
  10.4 18.3 %copy-start.11 = (s32[1,32,8]{1,2,0:T(8,128)S(1)}, s32[1,32,8]{1,2,0:T(8,128)}, u32[]{:S(2)}) copy-start(s32[1,32,8]{1,2,0:T(8,128)} %param.17) | copy-start | bytes 3076
  12.9 14.2 %collective-permute-start.2 = (bf16[64,8192]{1,0:T(8,128)(2,1)S(1)}, bf16[64,8192]{1,0:T(8,128)(2,1)S(1)}, u32[]{:S(2)}, u32[]{:S(2)}) collective-permute-start(bf16[64,8192]{1,0:T(8,128)(2,1)S(1)} %bitcast.43), channel_id=1, source_target_pairs={{0,8},{8,16},{16,24},{24,0},{1,9},{9,17},{17,25},{25,1},{2,10},{10... | collective-permute-start | bytes 3145736 | tf_op jit(solution)/shard_map/ppermute | solution.py:25
  27.2 1.0 copy-start
  28.1 14.7 %collective-permute-start.3 = (bf16[64,8192]{1,0:T(8,128)(2,1)}, bf16[64,8192]{1,0:T(8,128)(2,1)S(1)}, u32[]{:S(2)}, u32[]{:S(2)}) collective-permute-start(bf16[64,8192]{1,0:T(8,128)(2,1)} %bitcast.45), channel_id=1, source_target_pairs={{0,24},{8,0},{16,8},{24,16},{1,25},{9,1},{17,9},{25,17},{2,26},{10... | collective-permute-start | bytes 3145736 | tf_op jit(solution)/shard_map/ppermute | solution.py:25
  28.1 3.0 %collective-permute-start = (s32[32,8]{0,1:T(8,128)S(1)}, s32[32,8]{0,1:T(8,128)S(1)}, u32[]{:S(2)}, u32[]{:S(2)}) collective-permute-start(s32[32,8]{0,1:T(8,128)S(1)} %bitcast.48), channel_id=1, source_target_pairs={{0,8},{8,16},{16,24},{24,0},{1,9},{9,17},{17,25},{25,1},{2,10},{10... | collective-permute-start | bytes 3080 | tf_op jit(solution)/shard_map/ppermute | solution.py:25
  28.7 12.2 %collective-permute-start.1 = (s32[32,8]{0,1:T(8,128)S(1)}, s32[32,8]{0,1:T(8,128)S(1)}, u32[]{:S(2)}, u32[]{:S(2)}) collective-permute-start(s32[32,8]{0,1:T(8,128)S(1)} %bitcast.51), channel_id=1, source_target_pairs={{0,24},{8,0},{16,8},{24,16},{1,25},{9,1},{17,9},{25,17},{2,26},{10... | collective-permute-start | bytes 3080 | tf_op jit(solution)/shard_map/ppermute | solution.py:25
  31.2 9.6 %copy-start.12 = (s32[32,8]{0,1:T(8,128)}, s32[32,8]{0,1:T(8,128)S(1)}, u32[]{:S(2)}) copy-start(s32[32,8]{0,1:T(8,128)S(1)} %collective-permute-done) | copy-start | bytes 3076
  40.8 0.6 copy-start.13
  58.6 52.2 %all-to-all-start.1 = ((bf16[8,16,8192]{2,1,0:T(8,128)(2,1)}), bf16[8,16,8192]{2,1,0:T(8,128)(2,1)}, u32[]{:S(2)}, u32[]{:S(2)}) async-start(bf16[8,16,8192]{2,1,0:T(8,128)(2,1)} %bitcast.31), calls=%async_computation.1 | async-start | bytes 4194304 | tf_op jit(solution)/shard_map/all_to_all | solution.py:31
  64.4 0.7 copy-start.7
  70.8 25.5 %collective-permute-start.4 = (bf16[128,8192]{1,0:T(8,128)(2,1)S(1)}, bf16[128,8192]{1,0:T(8,128)(2,1)S(1)}, u32[]{:S(2)}, u32[]{:S(2)}) collective-permute-start(bf16[128,8192]{1,0:T(8,128)(2,1)S(1)} %shard_map.108), channel_id=1, source_target_pairs={{0,8},{8,16},{16,24},{24,0},{1,9},{9,17},{17,25},{25,1},{2,10},{10... | collective-permute-start | bytes 6291464 | tf_op jit(solution)/shard_map/ppermute | solution.py:25
  96.4 14.4 %copy-start.8 = (bf16[128,8192]{1,0:T(8,128)(2,1)}, bf16[128,8192]{1,0:T(8,128)(2,1)S(1)}, u32[]{:S(2)}) copy-start(bf16[128,8192]{1,0:T(8,128)(2,1)S(1)} %collective-permute-done.4) | copy-start | bytes 6291460
  110.8 3.8 %copy-start.2 = (bf16[1,512,128]{2,1,0:T(8,128)(2,1)S(1)}, bf16[1,512,128]{2,1,0:T(8,128)(2,1)}, u32[]{:S(2)}) copy-start(bf16[1,512,128]{2,1,0:T(8,128)(2,1)} %param.14) | copy-start | bytes 393220
  110.8 3.8 %copy-start.3 = (bf16[1,512,128]{2,1,0:T(8,128)(2,1)S(1)}, bf16[1,512,128]{2,1,0:T(8,128)(2,1)}, u32[]{:S(2)}) copy-start(bf16[1,512,128]{2,1,0:T(8,128)(2,1)} %param.15) | copy-start | bytes 393220
  110.8 3.8 %copy-start.6 = (s32[24]{0:T(128)S(1)}, s32[24]{0:T(128)}, u32[]{:S(2)}) copy-start(s32[24]{0:T(128)} %get-tuple-element.26.plan_ref) | copy-start | bytes 292
  110.8 52.2 %all-to-all-start.2 = ((bf16[8,16,8192]{2,1,0:T(8,128)(2,1)}), bf16[8,16,8192]{2,1,0:T(8,128)(2,1)S(1)}, u32[]{:S(2)}, u32[]{:S(2)}) async-start(bf16[8,16,8192]{2,1,0:T(8,128)(2,1)} %bitcast.39), calls=%async_computation.2 | async-start | bytes 4194304 | tf_op jit(solution)/shard_map/all_to_all | solution.py:31
  120.8 24.4 %collective-permute-start.5 = (bf16[128,8192]{1,0:T(8,128)(2,1)S(1)}, bf16[128,8192]{1,0:T(8,128)(2,1)}, u32[]{:S(2)}, u32[]{:S(2)}) collective-permute-start(bf16[128,8192]{1,0:T(8,128)(2,1)S(1)} %shard_map.110), channel_id=1, source_target_pairs={{0,24},{8,0},{16,8},{24,16},{1,25},{9,1},{17,9},{25,17},{2,26},{10... | collective-permute-start | bytes 6291464 | tf_op jit(solution)/shard_map/ppermute | solution.py:25
  163.0 4.5 %copy-start.5 = (s32[24]{0:T(128)S(1)}, s32[24]{0:T(128)}, u32[]{:S(2)}) copy-start(s32[24]{0:T(128)} %get-tuple-element.18.plan_ref) | copy-start | bytes 292
  163.0 52.3 %all-to-all-start.3 = ((bf16[8,16,8192]{2,1,0:T(8,128)(2,1)}), bf16[8,16,8192]{2,1,0:T(8,128)(2,1)}, u32[]{:S(2)}, u32[]{:S(2)}) async-start(bf16[8,16,8192]{2,1,0:T(8,128)(2,1)} %bitcast.23), calls=%async_computation.3 | async-start | bytes 4194304 | tf_op jit(solution)/shard_map/all_to_all | solution.py:31
  167.5 1.2 copy-start.1
  168.7 46.6 %copy-start.4 = (s32[24]{0:T(128)S(1)}, s32[24]{0:T(128)}, u32[]{:S(2)}) copy-start(s32[24]{0:T(128)} %get-tuple-element.25.plan_ref) | copy-start | bytes 292

commit v4 on v3

--- a/solution.py
+++ b/solution.py
@@ -1,5 +1,3 @@
-import functools
-
 import jax
 import jax.numpy as jnp
 from jax import lax
@@ -12,6 +10,7 @@
 FIELDS = 3
 VMEM_LIMIT = 48 * 1024 * 1024
 VMEM_MOST = 60 * 1024 * 1024
+VMEM_LEAST = 16 * 1024 * 1024
 PLACE_CHUNK = 4096
 ACROSS = ((1,), (1,))
 
@@ -23,6 +22,11 @@
 def shifted(value, steps):
     count = lax.axis_size("pipe")
     return lax.ppermute(value, "pipe", [(p, (p + steps) % count) for p in range(count)])
+
+
+def permute(piece, offset):
+    count = lax.axis_size("bundle")
+    return lax.ppermute(piece, "bundle", [(b, b ^ offset) for b in range(count)])
 
 
 def swap(pieces):
@@ -43,22 +47,23 @@
     for b in range(bundles):
         plan[HAS * bundles + b], plan[OUT * bundles + b] = scan(dev, b)
         plan[SAVED * bundles + b] = b * blocks_dev + scan(b, dev)[1]
-
-
-def plan_kernel(bundles, blocks_dev, dev_ref, mask_f, mask_b, plan_f, plan_b):
-    plan_one(bundles, blocks_dev, dev_ref[0], mask_f, plan_f)
-    plan_one(bundles, blocks_dev, dev_ref[0], mask_b, plan_b)
-
-
-def plans_of(mask_f, mask_b, device, blocks_dev):
-    bundles = mask_f.shape[1]
+    plan[FIELDS * bundles] = dev
+
+
+def plans_of(masks, device, blocks_dev):
+    bundles, number = masks[0].shape[1], len(masks)
+
+    def kernel(dev_ref, *refs):
+        for mask, plan in zip(refs[:number], refs[number:]):
+            plan_one(bundles, blocks_dev, dev_ref[0], mask, plan)
+
     smem = pl.BlockSpec(memory_space=pltpu.SMEM)
     return pl.pallas_call(
-        functools.partial(plan_kernel, bundles, blocks_dev),
-        out_shape=[jax.ShapeDtypeStruct((FIELDS * bundles,), jnp.int32)] * 2,
-        in_specs=[smem] * 3,
-        out_specs=[smem] * 2,
-    )(device[None], mask_f.T, mask_b.T)
+        kernel,
+        out_shape=[jax.ShapeDtypeStruct((FIELDS * bundles + 1,), jnp.int32)] * number,
+        in_specs=[smem] * (1 + number),
+        out_specs=[smem] * number,
+    )(device[None], *[mask.T for mask in masks])
 
 
 def chunk_of(width, most):
@@ -85,7 +90,7 @@
             out_specs=spec(out_rows),
             scratch_shapes=[pltpu.VMEM((r, chunk), t) for r, t in scratch],
         ),
-        compiler_params=pltpu.CompilerParams(vmem_limit_bytes=VMEM_LIMIT),
+        compiler_params=pltpu.CompilerParams(vmem_limit_bytes=VMEM_LEAST),
     )(plan, *ins)
 
 
@@ -93,27 +98,30 @@
     return pl.ds(pl.multiple_of(index * BLOCK, BLOCK), BLOCK)
 
 
-def pack(rows, mask, device, blocks_dev):
+def pack(rows, mask, device, blocks_dev, order=()):
     bundles, width = mask.shape[1], rows.shape[1]
     chunk = chunk_of(width, 4096)
-
-    def kernel(dev_ref, mask_ref, rows_ref, out):
-        for b in range(bundles):
+    out_rows = [BLOCK] * bundles if order else [bundles * BLOCK]
+
+    def kernel(dev_ref, mask_ref, rows_ref, *outs):
+        for i in range(bundles):
+            bundle = dev_ref[0] ^ order[i] if order else i
             at = jnp.int32(0)
             for j in range(1, blocks_dev):
-                at += j * mask_ref[b, dev_ref[0] * blocks_dev + j]
-            out[b * BLOCK : (b + 1) * BLOCK] = rows_ref[block_at(at), :]
-
-    return pl.pallas_call(
-        kernel,
-        out_shape=jax.ShapeDtypeStruct((bundles * BLOCK, width), jnp.bfloat16),
+                at += j * mask_ref[bundle, dev_ref[0] * blocks_dev + j]
+            out = outs[i] if order else outs[0].at[pl.ds(i * BLOCK, BLOCK)]
+            out[...] = rows_ref[block_at(at), :]
+
+    return pl.pallas_call(
+        kernel,
+        out_shape=[jax.ShapeDtypeStruct((r, width), jnp.bfloat16) for r in out_rows],
         grid=(width // chunk,),
         in_specs=[
             pl.BlockSpec(memory_space=pltpu.SMEM),
             pl.BlockSpec(memory_space=pltpu.SMEM),
             pl.BlockSpec((rows.shape[0], chunk), lambda c: (0, c)),
         ],
-        out_specs=pl.BlockSpec((bundles * BLOCK, chunk), lambda c: (0, c)),
+        out_specs=[pl.BlockSpec((r, chunk), lambda c: (0, c)) for r in out_rows],
         compiler_params=pltpu.CompilerParams(vmem_limit_bytes=VMEM_MOST),
     )(device[None], mask.T, rows)
 
@@ -136,12 +144,32 @@
     return chunked(kernel, plan, [base, parts], rows, PLACE_CHUNK)
 
 
+def copied(value):
+    def kernel(value_ref, out):
+        out[...] = value_ref[...]
+
+    chunk = chunk_of(value.shape[1], 4096)
+    spec = pl.BlockSpec((value.shape[0], chunk), lambda c: (0, c))
+    return pl.pallas_call(
+        kernel,
+        out_shape=jax.ShapeDtypeStruct(value.shape, value.dtype),
+        grid=(value.shape[1] // chunk,),
+        in_specs=[spec],
+        out_specs=spec,
+        compiler_params=pltpu.CompilerParams(vmem_limit_bytes=VMEM_MOST),
+    )(value)
+
+
 def middle(kernel, plan, rows, weights, saved, first_weights):
-    height, width = rows.shape
+    width = rows[0].shape[1]
+    height = sum(piece.shape[0] for piece in rows)
     chunk = chunk_of(width, 4096)
     steps = width // chunk
     units = min(weights[0].shape)
-    specs = [pl.BlockSpec((height, chunk), lambda s, c, *_: (0, jnp.where(s == 0, c, steps - 1)))]
+    specs = [
+        pl.BlockSpec((piece.shape[0], chunk), lambda s, c, *_: (0, jnp.where(s == 0, c, steps - 1)))
+        for piece in rows
+    ]
     for i, weight in enumerate(weights):
         tall = weight.shape[0] == width
 
@@ -161,12 +189,13 @@
             in_specs=specs,
             out_specs=pl.BlockSpec((height, chunk), lambda s, c, *_: (0, jnp.where(s == 0, 0, c))),
             scratch_shapes=[
+                pltpu.VMEM((height, chunk), jnp.bfloat16),
                 pltpu.VMEM((height, 2 * units), jnp.float32),
                 pltpu.VMEM((height, 2 * units), jnp.bfloat16),
             ],
         ),
         compiler_params=pltpu.CompilerParams(vmem_limit_bytes=VMEM_LIMIT),
-    )(plan, rows, *weights, *saved)
+    )(plan, *rows, *weights, *saved)
 
 
 def dot(left, right, dims=((1,), (0,))):
@@ -176,7 +205,7 @@
 def forward(plan, rows, gate_w, up_w, down_w):
     units = gate_w.shape[1]
 
-    def kernel(plan_ref, rows_ref, gate_ref, up_ref, down_ref, out, total_ref, hidden_ref):
+    def kernel(plan_ref, rows_ref, gate_ref, up_ref, down_ref, out, _, total_ref, hidden_ref):
         first, start = pl.program_id(0) == 0, pl.program_id(1) == 0
 
         @pl.when(first & start)
@@ -197,15 +226,16 @@
         def _():
             out[...] = dot(hidden_ref[:, :units], down_ref[...]).astype(jnp.bfloat16)
 
-    return middle(kernel, plan, rows, [gate_w, up_w, down_w], [], (0, 1))
-
-
-def backward(plan, rows, gate_w, up_w, down_w, saved_gate, saved_up, bundles):
+    return middle(kernel, plan, [rows], [gate_w, up_w, down_w], [], (0, 1))
+
+
+def backward(plan, pieces, gate_w, up_w, down_w, saved_gate, saved_up, order):
+    bundles = len(order)
     units = gate_w.shape[1]
 
-    def kernel(
-        plan_ref, rows_ref, gate_ref, up_ref, down_ref, gate_saved, up_saved, out, total_ref, grad_ref
-    ):
+    def kernel(plan_ref, *refs):
+        ins, refs = refs[:bundles], refs[bundles:]
+        gate_ref, up_ref, down_ref, gate_saved, up_saved, out, rows_ref, total_ref, grad_ref = refs
         first, start = pl.program_id(0) == 0, pl.program_id(1) == 0
 
         @pl.when(first & start)
@@ -214,6 +244,9 @@
 
         @pl.when(first)
         def _():
+            for i, piece in enumerate(ins):
+                at = block_at(plan_ref[FIELDS * bundles] ^ order[i])
+                rows_ref[at, :] = piece[...]
             total_ref[:, :units] += dot(rows_ref[...], down_ref[...], ACROSS)
 
         @pl.when(jnp.logical_not(first) & start)
@@ -233,7 +266,7 @@
             total += dot(grad_ref[:, units:], up_ref[...], ACROSS)
             out[...] = total.astype(jnp.bfloat16)
 
-    return middle(kernel, plan, rows, [gate_w, up_w, down_w], [saved_gate, saved_up], (2,))
+    return middle(kernel, plan, pieces, [gate_w, up_w, down_w], [saved_gate, saved_up], (2,))
 
 
 def per_device(act_fwd, grad_in, w_gate, w_up, w_down, saved_gate, saved_up, mask_fwd, mask_bwd):
@@ -242,27 +275,34 @@
     blocks_dev = act_fwd.shape[1] // BLOCK
     gate_w, up_w, down_w = w_gate[0], w_up[0], w_down[0]
 
-    packed_f = pack(act_fwd[0], mask_fwd[0], device, blocks_dev)
+    order = list(range(bundles - 1, -1, -1))
+    half = bundles // 2
+    near, far = range(1, half), range(bundles - 1, half - 1, -1)
+
+    [packed_f] = pack(act_fwd[0], mask_fwd[0], device, blocks_dev)
     rows_f = swap(packed_f)
-    packed_b = pack(after(grad_in[0], packed_f), mask_bwd[0], device, blocks_dev)
-    plan_f, plan_b = plans_of(mask_fwd[0], after(mask_bwd[0], packed_b), device, blocks_dev)
-    base_f = shifted(after(act_fwd[0], packed_b), 1)
-    base_b = shifted(after(grad_in[0], base_f), -1)
-    next_mask_f = shifted(after(mask_fwd[0], packed_b), 1)
-    next_mask_b = shifted(after(mask_bwd[0], packed_b), -1)
-    next_plan_f, next_plan_b = plans_of(next_mask_f, next_mask_b, device, blocks_dev)
-
-    rows_f = after(rows_f, base_b, next_plan_f)
-    rows_b = swap(after(packed_b, rows_f))
-    parts_f = shifted(forward(plan_f, rows_f, gate_w, up_w, down_w), 1)
-    back_f = swap(after(parts_f, rows_b))
+    packed_b = pack(after(grad_in[0], packed_f), mask_bwd[0], device, blocks_dev, order)
+    packed_b = dict(zip(order, packed_b))
+    base_b = shifted(after(grad_in[0], packed_b[0]), -1)
+    next_mask_b = shifted(after(mask_bwd[0], packed_b[0]), -1)
+    plan_f, plan_b, next_plan_b = plans_of(
+        [mask_fwd[0], mask_bwd[0], next_mask_b], device, blocks_dev
+    )
+
+    rows_b = {0: packed_b[0]} | {o: permute(after(packed_b[o], base_b), o) for o in near}
+    waits = [rows_b[o] for o in near]
+    rows_b |= {o: permute(after(packed_b[o], *waits), o) for o in far}
+    rows_b = [rows_b[o] for o in order]
+    rows_f = after(rows_f, rows_b[0], next_plan_b)
+    parts_f = forward(plan_f, rows_f, gate_w, up_w, down_w)
+    back_f = swap(after(parts_f, *rows_b))
     parts_b = backward(
-        plan_b, rows_b, gate_w, up_w, down_w, saved_gate[0], saved_up[0], bundles
+        plan_b, rows_b, gate_w, up_w, down_w, saved_gate[0], saved_up[0], order
     )
     parts_b = shifted(parts_b, -1)
-    next_forward = placed(next_plan_f, base_f, back_f, bundles)
+    next_forward = copied(shifted(placed(plan_f, act_fwd[0], back_f, bundles), 1))
     back_b = swap(after(parts_b, back_f))
-    next_backward = placed(next_plan_b, base_b, back_b, bundles)
+    next_backward = placed(next_plan_b, base_b, after(back_b, next_forward), bundles)
     return (next_forward[None], next_backward[None])
 
 

time: 219 us -> 215 us (0.982)
  waiting for transfers between devices: 166 us -> 152 us
  starting transfers between devices: 22.6 us -> 28.7 us
  local copies, waits for them, and re-layouts: 3.47 us -> 7.13 us
    ppermute x0 -> x7, waiting for transfers between devices: none -> 55.9 us  [permute(): lax.ppermute(piece, 'bundle', [(b, b ^ offset) for b in range(count)])]
    all_to_all x4 -> x3, waiting for transfers between devices: 92.3 us -> 45.1 us  [swap(): lax.all_to_all(pieces, 'bundle', split_axis=0, concat_axis=0, tiled=True)]
    ppermute x6 -> x4, waiting for transfers between devices: 74.1 us -> 51.4 us  [shifted(): lax.ppermute(value, 'pipe', [(p, (p + steps) % count) for p in range(coun...]
    ppermute x0 -> x7, starting transfers between devices: none -> 11.1 us  [permute(): lax.ppermute(piece, 'bundle', [(b, b ^ offset) for b in range(count)])]
    all_to_all x4 -> x3, starting transfers between devices: 19.9 us -> 15.9 us  [swap(): lax.all_to_all(pieces, 'bundle', split_axis=0, concat_axis=0, tiled=True)]
    unnamed x28 -> x34, local copies, waits for them, and re-layouts: 3.47 us -> 7.13 us
  transfers between devices with their start and end apart: 10 -> 14, of which waited for: 9 -> 12; matrix products, arithmetic and copies ran while one was open for 0% -> 0% of each run, Pallas kernels for 9% -> 9%
where the time goes in v4:
time: 215 us; the launch traced here: 214 us
  waiting for transfers between devices  152 us (71%)
  starting transfers between devices  28.7 us (13%)
  Pallas kernels  25.2 us (12%)
  local copies, waits for them, and re-layouts  7.13 us (3%)
    ppermute x7, waiting for transfers between devices, permute(): lax.ppermute(piece, 'bundle', [(b, b ^ offset) for b in range(count)])  55.9 us
    ppermute x4, waiting for transfers between devices, shifted(): lax.ppermute(value, 'pipe', [(p, (p + steps) % count) for p in range(coun...  51.4 us
    all_to_all x3, waiting for transfers between devices, swap(): lax.all_to_all(pieces, 'bundle', split_axis=0, concat_axis=0, tiled=True)  45.1 us
    all_to_all x3, starting transfers between devices, swap(): lax.all_to_all(pieces, 'bundle', split_axis=0, concat_axis=0, tiled=True)  15.9 us
    pallas_call x2, Pallas kernels, middle(): pl.pallas_call(kernel, out_shape=jax.ShapeDtypeStruct((height, width), jn...  11.8 us
    ppermute x7, starting transfers between devices, permute(): lax.ppermute(piece, 'bundle', [(b, b ^ offset) for b in range(count)])  11.1 us
    unnamed x34, local copies, waits for them, and re-layouts  7.13 us
    pallas_call x2, Pallas kernels, pack(): pl.pallas_call(kernel, out_shape=[jax.ShapeDtypeStruct((r, width), jnp.bf...  4.94 us
  transfers between devices with their start and end apart: 14, of which 12 were waited for; matrix products, arithmetic and copies ran while one was open for 0% of the time, Pallas kernels for 9%

profile of v4, /device:TPU:0, one launch (start us, length us, event | category | flops | bytes accessed | tf_op | source)
XLA Modules:
  0.0 214.1 jit_solution(7407571835174332743)
XLA Ops:
  0.6 2.5 %shard_map.104 = bf16[128,8192]{1,0:T(8,128)(2,1)} custom-call(s32[1]{0:T(128)} %bitcast.dev_ref, s32[8,32]{1,0:T(8,128)} %bitcast.41, bf16[64,8192]{1,0:T(8,128)(2,1)} %bitcast.26), custom_call_target="tpu_custom_call" | custom-call | tf_op jit(solution)/shard_map/pallas_call | solution.py:115
  3.1 7.4 %all-to-all-start = ((bf16[8,16,8192]{2,1,0:T(8,128)(2,1)}), bf16[8,16,8192]{2,1,0:T(8,128)(2,1)S(1)}, u32[]{:S(2)}, u32[]{:S(2)}) async-start(bf16[8,16,8192]{2,1,0:T(8,128)(2,1)} %bitcast.30), calls=%async_computation | async-start | bytes 4194304 | tf_op jit(solution)/shard_map/all_to_all | solution.py:35
  10.5 2.4 %shard_map.105 = (bf16[16,8192]{1,0:T(8,128)(2,1)}, bf16[16,8192]{1,0:T(8,128)(2,1)}, bf16[16,8192]{1,0:T(8,128)(2,1)}, bf16[16,8192]{1,0:T(8,128)(2,1)}, bf16[1...) custom-call(s32[1]{0:T(128)} %bitcast.dev_ref, ...), custom_call_target="tpu_custom_call" | custom-call | tf_op jit(solution)/shard_map/pallas_call | solution.py:115
  13.7 12.3 %collective-permute-done.1.base_ref = bf16[64,8192]{1,0:T(8,128)(2,1)S(1)} collective-permute-done((bf16[64,8192]{1,0:T(8,128)(2,1)S(1)}, bf16[64,8192]{1,0:T(8,128)(2,1)S(1)}, u32[]{:S(2)}, u32[]{:S(2)}) %collective-permute-start.1) | collective-permute-done | bytes 1048608 | tf_op jit(solution)/shard_map/ppermute | solution.py:24
  27.1 1.7 collective-permute-start.2
  30.5 14.5 %collective-permute-done.2.refs_6_ = bf16[16,8192]{1,0:T(8,128)(2,1)S(1)} collective-permute-done((bf16[16,8192]{1,0:T(8,128)(2,1)}, bf16[16,8192]{1,0:T(8,128)(2,1)S(1)}, u32[]{:S(2)}, u32[]{:S(2)}) %collective-permute-start.2) | collective-permute-done | bytes 262176 | tf_op jit(solution)/shard_map/ppermute | solution.py:29
  45.0 7.3 %collective-permute-done.3.refs_5_ = bf16[16,8192]{1,0:T(8,128)(2,1)S(1)} collective-permute-done((bf16[16,8192]{1,0:T(8,128)(2,1)}, bf16[16,8192]{1,0:T(8,128)(2,1)S(1)}, u32[]{:S(2)}, u32[]{:S(2)}) %collective-permute-start.3) | collective-permute-done | bytes 262176 | tf_op jit(solution)/shard_map/ppermute | solution.py:29
  52.4 4.5 %collective-permute-done.4.refs_4_ = bf16[16,8192]{1,0:T(8,128)(2,1)S(1)} collective-permute-done((bf16[16,8192]{1,0:T(8,128)(2,1)}, bf16[16,8192]{1,0:T(8,128)(2,1)S(1)}, u32[]{:S(2)}, u32[]{:S(2)}) %collective-permute-start.4) | collective-permute-done | bytes 262176 | tf_op jit(solution)/shard_map/ppermute | solution.py:29
  56.9 3.5 %collective-permute-start.5 = (bf16[16,8192]{1,0:T(8,128)(2,1)}, bf16[16,8192]{1,0:T(8,128)(2,1)S(1)}, u32[]{:S(2)}, u32[]{:S(2)}) collective-permute-start(bf16[16,8192]{1,0:T(8,128)(2,1)} %get-tuple-element.39), channel_id=1, source_target_pairs={{0,7},{1,6},{2,5},{3,4},{4,3},{5,2},{6,1},{7,0},{8,15},{9,14},{10,... | collective-permute-start | bytes 786440 | tf_op jit(solution)/shard_map/ppermute | solution.py:29
  61.6 2.6 %collective-permute-start.7 = (bf16[16,8192]{1,0:T(8,128)(2,1)}, bf16[16,8192]{1,0:T(8,128)(2,1)}, u32[]{:S(2)}, u32[]{:S(2)}) collective-permute-start(bf16[16,8192]{1,0:T(8,128)(2,1)} %get-tuple-element.45), channel_id=1, source_target_pairs={{0,5},{1,4},{2,7},{3,6},{4,1},{5,0},{6,3},{7,2},{8,13},{9,12},{10,... | collective-permute-start | bytes 786440 | tf_op jit(solution)/shard_map/ppermute | solution.py:29
  66.4 1.6 shard_map.106
  69.7 5.7 %shard_map.107 = bf16[128,8192]{1,0:T(8,128)(2,1)S(1)} custom-call(s32[25]{0:T(128)S(1)} %copy-done.9, bf16[128,8192]{1,0:T(8,128)(2,1)S(1)} %bitcast.24, bf16[8192,128]{1,0:T(8,128)(2,1)} %bitcast.31, bf16[8192,128]{1,0:T(8,128)(2,1)} %bitcast.33, bf16[128,8192]{1,0:T(8,128)(2,1)} %bitcast.35), custom_call_target="tpu_custom_call" | custom-call | tf_op jit(solution)/shard_map/pallas_call | solution.py:183
  77.5 23.3 %collective-permute-done.7.refs_2_ = bf16[16,8192]{1,0:T(8,128)(2,1)} collective-permute-done((bf16[16,8192]{1,0:T(8,128)(2,1)}, bf16[16,8192]{1,0:T(8,128)(2,1)}, u32[]{:S(2)}, u32[]{:S(2)}) %collective-permute-start.7) | collective-permute-done | bytes 262176 | tf_op jit(solution)/shard_map/ppermute | solution.py:29
  100.8 5.3 %collective-permute-done.8.refs_3_ = bf16[16,8192]{1,0:T(8,128)(2,1)} collective-permute-done((bf16[16,8192]{1,0:T(8,128)(2,1)}, bf16[16,8192]{1,0:T(8,128)(2,1)}, u32[]{:S(2)}, u32[]{:S(2)}) %collective-permute-start.8) | collective-permute-done | bytes 262176 | tf_op jit(solution)/shard_map/ppermute | solution.py:29
  106.1 4.0 %all-to-all-start.1 = ((bf16[8,16,8192]{2,1,0:T(8,128)(2,1)}), bf16[8,16,8192]{2,1,0:T(8,128)(2,1)S(1)}, u32[]{:S(2)}, u32[]{:S(2)}) async-start(bf16[8,16,8192]{2,1,0:T(8,128)(2,1)} %bitcast.25), calls=%async_computation.1 | async-start | bytes 4194304 | tf_op jit(solution)/shard_map/all_to_all | solution.py:35
  112.0 6.1 %shard_map.110 = bf16[128,8192]{1,0:T(8,128)(2,1)S(1)} custom-call(s32[25]{0:T(128)S(1)} %copy-done.12, bf16[16,8192]{1,0:T(8,128)(2,1)S(1)} %collective-permute-done.5.refs_0_, bf16[16,8192]{1,0:T(8,128)(2,1)S(1)} %copy-done.6, bf16[16,8192]{1,0:T(8,128)(2,1)} %collective-permute-done.7.refs_2_, bf16[16,8192]{1,0:T(8,128)(2,1)} %collective-permute-done.8.refs_3_, ...), custom_call_target="tpu_custom_call" | custom-call | tf_op jit(solution)/shard_map/pallas_call | solution.py:183
  119.0 23.6 %collective-permute-done.10 = bf16[128,8192]{1,0:T(8,128)(2,1)} collective-permute-done((bf16[128,8192]{1,0:T(8,128)(2,1)S(1)}, bf16[128,8192]{1,0:T(8,128)(2,1)}, u32[]{:S(2)}, u32[]{:S(2)}) %collective-permute-start.10) | collective-permute-done | bytes 2097184 | tf_op jit(solution)/shard_map/ppermute | solution.py:24
  142.5 16.0 %all-to-all-done.1 = bf16[8,16,8192]{2,1,0:T(8,128)(2,1)S(1)} async-done(((bf16[8,16,8192]{2,1,0:T(8,128)(2,1)}), bf16[8,16,8192]{2,1,0:T(8,128)(2,1)S(1)}, u32[]{:S(2)}, u32[]{:S(2)}) %all-to-all-start.1) | async-done | bytes 2097184 | tf_op jit(solution)/shard_map/all_to_all | solution.py:35
  158.6 4.5 %all-to-all-start.2 = ((bf16[8,16,8192]{2,1,0:T(8,128)(2,1)}), bf16[8,16,8192]{2,1,0:T(8,128)(2,1)}, u32[]{:S(2)}, u32[]{:S(2)}) async-start(bf16[8,16,8192]{2,1,0:T(8,128)(2,1)} %bitcast.20), calls=%async_computation.2 | async-start | bytes 4194304 | tf_op jit(solution)/shard_map/all_to_all | solution.py:35
  163.1 1.5 shard_map.108
  164.6 14.2 %collective-permute-done.9.value_ref = bf16[64,8192]{1,0:T(8,128)(2,1)S(1)} collective-permute-done((bf16[64,8192]{1,0:T(8,128)(2,1)S(1)}, bf16[64,8192]{1,0:T(8,128)(2,1)S(1)}, u32[]{:S(2)}, u32[]{:S(2)}) %collective-permute-start.9) | collective-permute-done | bytes 1048608 | tf_op jit(solution)/shard_map/ppermute | solution.py:24
  179.8 2.0 shard_map.109
  181.9 29.0 %all-to-all-done.2 = bf16[8,16,8192]{2,1,0:T(8,128)(2,1)} async-done(((bf16[8,16,8192]{2,1,0:T(8,128)(2,1)}), bf16[8,16,8192]{2,1,0:T(8,128)(2,1)}, u32[]{:S(2)}, u32[]{:S(2)}) %all-to-all-start.2) | async-done | bytes 2097184 | tf_op jit(solution)/shard_map/all_to_all | solution.py:35
  210.9 3.2 %shard_map.111 = bf16[64,8192]{1,0:T(8,128)(2,1)} custom-call(s32[25]{0:T(128)S(1)} %copy-done.11, bf16[64,8192]{1,0:T(8,128)(2,1)S(1)} %copy-done.3, bf16[128,8192]{1,0:T(8,128)(2,1)} %bitcast.21.parts_ref), custom_call_target="tpu_custom_call" | custom-call | tf_op jit(solution)/shard_map/pallas_call | solution.py:83
  (46 shorter events, 14.4 us)
Async XLA Ops:
  3.1 9.9 %copy-start.13 = (bf16[1,64,8192]{2,1,0:T(8,128)(2,1)S(1)}, bf16[1,64,8192]{2,1,0:T(8,128)(2,1)}, u32[]{:S(2)}) copy-start(bf16[1,64,8192]{2,1,0:T(8,128)(2,1)} %param.10) | copy-start | bytes 3145732
  3.1 61.4 %copy-start.15 = (s32[1,32,8]{1,2,0:T(8,128)S(1)}, s32[1,32,8]{1,2,0:T(8,128)}, u32[]{:S(2)}) copy-start(s32[1,32,8]{1,2,0:T(8,128)} %param.17) | copy-start | bytes 3076
  3.1 66.0 %all-to-all-start = ((bf16[8,16,8192]{2,1,0:T(8,128)(2,1)}), bf16[8,16,8192]{2,1,0:T(8,128)(2,1)S(1)}, u32[]{:S(2)}, u32[]{:S(2)}) async-start(bf16[8,16,8192]{2,1,0:T(8,128)(2,1)} %bitcast.30), calls=%async_computation | async-start | bytes 4194304 | tf_op jit(solution)/shard_map/all_to_all | solution.py:35
  13.0 13.0 %collective-permute-start.1 = (bf16[64,8192]{1,0:T(8,128)(2,1)S(1)}, bf16[64,8192]{1,0:T(8,128)(2,1)S(1)}, u32[]{:S(2)}, u32[]{:S(2)}) collective-permute-start(bf16[64,8192]{1,0:T(8,128)(2,1)S(1)} %bitcast.39), channel_id=1, source_target_pairs={{0,24},{8,0},{16,8},{24,16},{1,25},{9,1},{17,9},{25,17},{2,26},{10... | collective-permute-start | bytes 3145736 | tf_op jit(solution)/shard_map/ppermute | solution.py:24
  27.1 18.0 %collective-permute-start.2 = (bf16[16,8192]{1,0:T(8,128)(2,1)}, bf16[16,8192]{1,0:T(8,128)(2,1)S(1)}, u32[]{:S(2)}, u32[]{:S(2)}) collective-permute-start(bf16[16,8192]{1,0:T(8,128)(2,1)} %get-tuple-element.34), channel_id=1, source_target_pairs={{0,1},{1,0},{2,3},{3,2},{4,5},{5,4},{6,7},{7,6},{8,9},{9,8},{10,11... | collective-permute-start | bytes 786440 | tf_op jit(solution)/shard_map/ppermute | solution.py:29
  28.8 23.6 %collective-permute-start.3 = (bf16[16,8192]{1,0:T(8,128)(2,1)}, bf16[16,8192]{1,0:T(8,128)(2,1)S(1)}, u32[]{:S(2)}, u32[]{:S(2)}) collective-permute-start(bf16[16,8192]{1,0:T(8,128)(2,1)} %get-tuple-element.36), channel_id=1, source_target_pairs={{0,2},{1,3},{2,0},{3,1},{4,6},{5,7},{6,4},{7,5},{8,10},{9,11},{10,... | collective-permute-start | bytes 786440 | tf_op jit(solution)/shard_map/ppermute | solution.py:29
  30.3 26.6 %collective-permute-start.4 = (bf16[16,8192]{1,0:T(8,128)(2,1)}, bf16[16,8192]{1,0:T(8,128)(2,1)S(1)}, u32[]{:S(2)}, u32[]{:S(2)}) collective-permute-start(bf16[16,8192]{1,0:T(8,128)(2,1)} %get-tuple-element.38), channel_id=1, source_target_pairs={{0,3},{1,2},{2,1},{3,0},{4,7},{5,6},{6,5},{7,4},{8,11},{9,10},{10,... | collective-permute-start | bytes 786440 | tf_op jit(solution)/shard_map/ppermute | solution.py:29
  56.9 12.2 %collective-permute-start.5 = (bf16[16,8192]{1,0:T(8,128)(2,1)}, bf16[16,8192]{1,0:T(8,128)(2,1)S(1)}, u32[]{:S(2)}, u32[]{:S(2)}) collective-permute-start(bf16[16,8192]{1,0:T(8,128)(2,1)} %get-tuple-element.39), channel_id=1, source_target_pairs={{0,7},{1,6},{2,5},{3,4},{4,3},{5,2},{6,1},{7,0},{8,15},{9,14},{10,... | collective-permute-start | bytes 786440 | tf_op jit(solution)/shard_map/ppermute | solution.py:29
  60.4 16.5 %collective-permute-start.6 = (bf16[16,8192]{1,0:T(8,128)(2,1)}, bf16[16,8192]{1,0:T(8,128)(2,1)S(1)}, u32[]{:S(2)}, u32[]{:S(2)}) collective-permute-start(bf16[16,8192]{1,0:T(8,128)(2,1)} %get-tuple-element.43), channel_id=1, source_target_pairs={{0,6},{1,7},{2,4},{3,5},{4,2},{5,3},{6,0},{7,1},{8,14},{9,15},{10,... | collective-permute-start | bytes 786440 | tf_op jit(solution)/shard_map/ppermute | solution.py:29
  61.6 39.2 %collective-permute-start.7 = (bf16[16,8192]{1,0:T(8,128)(2,1)}, bf16[16,8192]{1,0:T(8,128)(2,1)}, u32[]{:S(2)}, u32[]{:S(2)}) collective-permute-start(bf16[16,8192]{1,0:T(8,128)(2,1)} %get-tuple-element.45), channel_id=1, source_target_pairs={{0,5},{1,4},{2,7},{3,6},{4,1},{5,0},{6,3},{7,2},{8,13},{9,12},{10,... | collective-permute-start | bytes 786440 | tf_op jit(solution)/shard_map/ppermute | solution.py:29
  64.2 41.9 %collective-permute-start.8 = (bf16[16,8192]{1,0:T(8,128)(2,1)}, bf16[16,8192]{1,0:T(8,128)(2,1)}, u32[]{:S(2)}, u32[]{:S(2)}) collective-permute-start(bf16[16,8192]{1,0:T(8,128)(2,1)} %get-tuple-element.47), channel_id=1, source_target_pairs={{0,4},{1,5},{2,6},{3,7},{4,0},{5,1},{6,2},{7,3},{8,12},{9,13},{10,... | collective-permute-start | bytes 786440 | tf_op jit(solution)/shard_map/ppermute | solution.py:29
  64.5 1.3 collective-permute-start
  75.5 1.3 copy-start
  106.1 4.0 %copy-start.4 = (bf16[16,8192]{1,0:T(8,128)(2,1)S(1)}, bf16[16,8192]{1,0:T(8,128)(2,1)}, u32[]{:S(2)}) copy-start(bf16[16,8192]{1,0:T(8,128)(2,1)} %get-tuple-element.28.refs_7_) | copy-start | bytes 786436
  106.1 4.0 %copy-start.7 = (bf16[1,512,128]{2,1,0:T(8,128)(2,1)S(1)}, bf16[1,512,128]{2,1,0:T(8,128)(2,1)}, u32[]{:S(2)}) copy-start(bf16[1,512,128]{2,1,0:T(8,128)(2,1)} %param.14) | copy-start | bytes 393220
  106.1 4.1 %copy-start.12 = (s32[25]{0:T(128)S(1)}, s32[25]{0:T(128)}, u32[]{:S(2)}) copy-start(s32[25]{0:T(128)} %get-tuple-element.49.plan_ref) | copy-start | bytes 304
  106.1 52.5 %all-to-all-start.1 = ((bf16[8,16,8192]{2,1,0:T(8,128)(2,1)}), bf16[8,16,8192]{2,1,0:T(8,128)(2,1)S(1)}, u32[]{:S(2)}, u32[]{:S(2)}) async-start(bf16[8,16,8192]{2,1,0:T(8,128)(2,1)} %bitcast.25), calls=%async_computation.1 | async-start | bytes 4194304 | tf_op jit(solution)/shard_map/all_to_all | solution.py:35
  118.1 24.4 %collective-permute-start.10 = (bf16[128,8192]{1,0:T(8,128)(2,1)S(1)}, bf16[128,8192]{1,0:T(8,128)(2,1)}, u32[]{:S(2)}, u32[]{:S(2)}) collective-permute-start(bf16[128,8192]{1,0:T(8,128)(2,1)S(1)} %shard_map.110), channel_id=1, source_target_pairs={{0,24},{8,0},{16,8},{24,16},{1,25},{9,1},{17,9},{25,17},{2,26},{10... | collective-permute-start | bytes 6291464 | tf_op jit(solution)/shard_map/ppermute | solution.py:24
  158.6 4.5 %copy-start.1 = (bf16[1,64,8192]{2,1,0:T(8,128)(2,1)S(1)}, bf16[1,64,8192]{2,1,0:T(8,128)(2,1)}, u32[]{:S(2)}) copy-start(bf16[1,64,8192]{2,1,0:T(8,128)(2,1)} %param.9) | copy-start | bytes 3145732
  158.6 4.5 %copy-start.10 = (s32[25]{0:T(128)S(1)}, s32[25]{0:T(128)}, u32[]{:S(2)}) copy-start(s32[25]{0:T(128)} %get-tuple-element.30.plan_ref) | copy-start | bytes 304
  158.6 52.3 %all-to-all-start.2 = ((bf16[8,16,8192]{2,1,0:T(8,128)(2,1)}), bf16[8,16,8192]{2,1,0:T(8,128)(2,1)}, u32[]{:S(2)}, u32[]{:S(2)}) async-start(bf16[8,16,8192]{2,1,0:T(8,128)(2,1)} %bitcast.20), calls=%async_computation.2 | async-start | bytes 4194304 | tf_op jit(solution)/shard_map/all_to_all | solution.py:35
  164.6 46.3 %copy-start.3 = (bf16[64,8192]{1,0:T(8,128)(2,1)S(1)}, bf16[64,8192]{1,0:T(8,128)(2,1)}, u32[]{:S(2)}) copy-start(bf16[64,8192]{1,0:T(8,128)(2,1)} %copy-done.2) | copy-start | bytes 3145732
  164.6 46.3 %copy-start.11 = (s32[25]{0:T(128)S(1)}, s32[25]{0:T(128)}, u32[]{:S(2)}) copy-start(s32[25]{0:T(128)} %get-tuple-element.40.plan_ref) | copy-start | bytes 304
  164.6 14.3 %collective-permute-start.9 = (bf16[64,8192]{1,0:T(8,128)(2,1)S(1)}, bf16[64,8192]{1,0:T(8,128)(2,1)S(1)}, u32[]{:S(2)}, u32[]{:S(2)}) collective-permute-start(bf16[64,8192]{1,0:T(8,128)(2,1)S(1)} %shard_map.108), channel_id=1, source_target_pairs={{0,8},{8,16},{16,24},{24,0},{1,9},{9,17},{17,25},{25,1},{2,10},{10... | collective-permute-start | bytes 3145736 | tf_op jit(solution)/shard_map/ppermute | solution.py:24
  (7 other events, 5.8 us)

commit v5 on v4

--- a/solution.py
+++ b/solution.py
@@ -290,7 +290,7 @@
     )
 
     rows_b = {0: packed_b[0]} | {o: permute(after(packed_b[o], base_b), o) for o in near}
-    waits = [rows_b[o] for o in near]
+    waits = [rows_b[1]]
     rows_b |= {o: permute(after(packed_b[o], *waits), o) for o in far}
     rows_b = [rows_b[o] for o in order]
     rows_f = after(rows_f, rows_b[0], next_plan_b)

time: 215 us -> 212 us (0.986)
  waiting for transfers between devices: 152 us -> 125 us
  starting transfers between devices: 28.7 us -> 53.7 us
    ppermute x7, waiting for transfers between devices: 55.9 us -> 30.3 us  [permute(): lax.ppermute(piece, 'bundle', [(b, b ^ offset) for b in range(count)])]
    ppermute x7, starting transfers between devices: 11.1 us -> 35.4 us  [permute(): lax.ppermute(piece, 'bundle', [(b, b ^ offset) for b in range(count)])]
  transfers between devices with their start and end apart: 14 -> 14, of which waited for: 12 -> 9; matrix products, arithmetic and copies ran while one was open for 0% -> 0% of each run, Pallas kernels for 9% -> 9%
where the time goes in v5:
time: 212 us
  waiting for transfers between devices  125 us (59%)
  starting transfers between devices  53.7 us (25%)
  Pallas kernels  25.1 us (12%)
  local copies, waits for them, and re-layouts  6.54 us (3%)
    ppermute x4, waiting for transfers between devices, shifted(): lax.ppermute(value, 'pipe', [(p, (p + steps) % count) for p in range(coun...  50.1 us
    all_to_all x3, waiting for transfers between devices, swap(): lax.all_to_all(pieces, 'bundle', split_axis=0, concat_axis=0, tiled=True)  45 us
    ppermute x7, starting transfers between devices, permute(): lax.ppermute(piece, 'bundle', [(b, b ^ offset) for b in range(count)])  35.4 us
    ppermute x7, waiting for transfers between devices, permute(): lax.ppermute(piece, 'bundle', [(b, b ^ offset) for b in range(count)])  30.3 us
    all_to_all x3, starting transfers between devices, swap(): lax.all_to_all(pieces, 'bundle', split_axis=0, concat_axis=0, tiled=True)  15.6 us
    pallas_call x2, Pallas kernels, middle(): pl.pallas_call(kernel, out_shape=jax.ShapeDtypeStruct((height, width), jn...  11.8 us
    unnamed x34, local copies, waits for them, and re-layouts  6.54 us
    pallas_call x2, Pallas kernels, pack(): pl.pallas_call(kernel, out_shape=[jax.ShapeDtypeStruct((r, width), jnp.bf...  4.93 us
  transfers between devices with their start and end apart: 14, of which 9 were waited for; matrix products, arithmetic and copies ran while one was open for 0% of the time, Pallas kernels for 9%

profile of v5, /device:TPU:0, one launch (start us, length us, event | category | flops | bytes accessed | tf_op | source)
XLA Modules:
  0.0 211.6 jit_solution(13381815881208532725)
XLA Ops:
  0.6 2.5 %shard_map.104 = bf16[128,8192]{1,0:T(8,128)(2,1)} custom-call(s32[1]{0:T(128)} %bitcast.dev_ref, s32[8,32]{1,0:T(8,128)} %bitcast.41, bf16[64,8192]{1,0:T(8,128)(2,1)} %bitcast.26), custom_call_target="tpu_custom_call" | custom-call | tf_op jit(solution)/shard_map/pallas_call | solution.py:115
  3.1 7.4 %all-to-all-start = ((bf16[8,16,8192]{2,1,0:T(8,128)(2,1)}), bf16[8,16,8192]{2,1,0:T(8,128)(2,1)S(1)}, u32[]{:S(2)}, u32[]{:S(2)}) async-start(bf16[8,16,8192]{2,1,0:T(8,128)(2,1)} %bitcast.30), calls=%async_computation | async-start | bytes 4194304 | tf_op jit(solution)/shard_map/all_to_all | solution.py:35
  10.5 2.4 %shard_map.105 = (bf16[16,8192]{1,0:T(8,128)(2,1)}, bf16[16,8192]{1,0:T(8,128)(2,1)}, bf16[16,8192]{1,0:T(8,128)(2,1)}, bf16[16,8192]{1,0:T(8,128)(2,1)}, bf16[1...) custom-call(s32[1]{0:T(128)} %bitcast.dev_ref, ...), custom_call_target="tpu_custom_call" | custom-call | tf_op jit(solution)/shard_map/pallas_call | solution.py:115
  13.7 12.3 %collective-permute-done.1.base_ref = bf16[64,8192]{1,0:T(8,128)(2,1)S(1)} collective-permute-done((bf16[64,8192]{1,0:T(8,128)(2,1)S(1)}, bf16[64,8192]{1,0:T(8,128)(2,1)S(1)}, u32[]{:S(2)}, u32[]{:S(2)}) %collective-permute-start.1) | collective-permute-done | bytes 1048608 | tf_op jit(solution)/shard_map/ppermute | solution.py:24
  27.0 1.7 collective-permute-start.2
  28.8 16.2 %collective-permute-done.2.refs_6_ = bf16[16,8192]{1,0:T(8,128)(2,1)S(1)} collective-permute-done((bf16[16,8192]{1,0:T(8,128)(2,1)}, bf16[16,8192]{1,0:T(8,128)(2,1)S(1)}, u32[]{:S(2)}, u32[]{:S(2)}) %collective-permute-start.2) | collective-permute-done | bytes 262176 | tf_op jit(solution)/shard_map/ppermute | solution.py:29
  45.0 3.2 %collective-permute-start.3 = (bf16[16,8192]{1,0:T(8,128)(2,1)}, bf16[16,8192]{1,0:T(8,128)(2,1)S(1)}, u32[]{:S(2)}, u32[]{:S(2)}) collective-permute-start(bf16[16,8192]{1,0:T(8,128)(2,1)} %get-tuple-element.35), channel_id=1, source_target_pairs={{0,7},{1,6},{2,5},{3,4},{4,3},{5,2},{6,1},{7,0},{8,15},{9,14},{10,... | collective-permute-start | bytes 786440 | tf_op jit(solution)/shard_map/ppermute | solution.py:29
  49.3 3.7 %collective-permute-start.8 = (bf16[16,8192]{1,0:T(8,128)(2,1)}, bf16[16,8192]{1,0:T(8,128)(2,1)S(1)}, u32[]{:S(2)}, u32[]{:S(2)}) collective-permute-start(bf16[16,8192]{1,0:T(8,128)(2,1)} %get-tuple-element.47), channel_id=1, source_target_pairs={{0,2},{1,3},{2,0},{3,1},{4,6},{5,7},{6,4},{7,5},{8,10},{9,11},{10,... | collective-permute-start | bytes 786440 | tf_op jit(solution)/shard_map/ppermute | solution.py:29
  54.5 2.6 %collective-permute-done.3.refs_0_ = bf16[16,8192]{1,0:T(8,128)(2,1)S(1)} collective-permute-done((bf16[16,8192]{1,0:T(8,128)(2,1)}, bf16[16,8192]{1,0:T(8,128)(2,1)S(1)}, u32[]{:S(2)}, u32[]{:S(2)}) %collective-permute-start.3) | collective-permute-done | bytes 262176 | tf_op jit(solution)/shard_map/ppermute | solution.py:29
  57.1 25.2 %collective-permute-start.6 = (bf16[16,8192]{1,0:T(8,128)(2,1)}, bf16[16,8192]{1,0:T(8,128)(2,1)}, u32[]{:S(2)}, u32[]{:S(2)}) collective-permute-start(bf16[16,8192]{1,0:T(8,128)(2,1)} %get-tuple-element.43), channel_id=1, source_target_pairs={{0,4},{1,5},{2,6},{3,7},{4,0},{5,1},{6,2},{7,3},{8,12},{9,13},{10,... | collective-permute-start | bytes 786440 | tf_op jit(solution)/shard_map/ppermute | solution.py:29
  82.4 1.6 shard_map.106
  84.7 5.8 %shard_map.107 = bf16[128,8192]{1,0:T(8,128)(2,1)S(1)} custom-call(s32[25]{0:T(128)S(1)} %copy-done.9, bf16[128,8192]{1,0:T(8,128)(2,1)S(1)} %bitcast.24, bf16[8192,128]{1,0:T(8,128)(2,1)} %bitcast.31, bf16[8192,128]{1,0:T(8,128)(2,1)} %bitcast.33, bf16[128,8192]{1,0:T(8,128)(2,1)} %bitcast.35), custom_call_target="tpu_custom_call" | custom-call | tf_op jit(solution)/shard_map/pallas_call | solution.py:183
  92.5 7.9 %collective-permute-done.5.refs_2_ = bf16[16,8192]{1,0:T(8,128)(2,1)} collective-permute-done((bf16[16,8192]{1,0:T(8,128)(2,1)}, bf16[16,8192]{1,0:T(8,128)(2,1)}, u32[]{:S(2)}, u32[]{:S(2)}) %collective-permute-start.5) | collective-permute-done | bytes 262176 | tf_op jit(solution)/shard_map/ppermute | solution.py:29
  100.4 3.5 %collective-permute-done.6.refs_3_ = bf16[16,8192]{1,0:T(8,128)(2,1)} collective-permute-done((bf16[16,8192]{1,0:T(8,128)(2,1)}, bf16[16,8192]{1,0:T(8,128)(2,1)}, u32[]{:S(2)}, u32[]{:S(2)}) %collective-permute-start.6) | collective-permute-done | bytes 262176 | tf_op jit(solution)/shard_map/ppermute | solution.py:29
  103.9 3.7 %all-to-all-start.1 = ((bf16[8,16,8192]{2,1,0:T(8,128)(2,1)}), bf16[8,16,8192]{2,1,0:T(8,128)(2,1)S(1)}, u32[]{:S(2)}, u32[]{:S(2)}) async-start(bf16[8,16,8192]{2,1,0:T(8,128)(2,1)} %bitcast.25), calls=%async_computation.1 | async-start | bytes 4194304 | tf_op jit(solution)/shard_map/all_to_all | solution.py:35
  109.5 6.1 %shard_map.110 = bf16[128,8192]{1,0:T(8,128)(2,1)S(1)} custom-call(s32[25]{0:T(128)S(1)} %copy-done.12, bf16[16,8192]{1,0:T(8,128)(2,1)S(1)} %collective-permute-done.3.refs_0_, bf16[16,8192]{1,0:T(8,128)(2,1)S(1)} %copy-done.6, bf16[16,8192]{1,0:T(8,128)(2,1)} %collective-permute-done.5.refs_2_, bf16[16,8192]{1,0:T(8,128)(2,1)} %collective-permute-done.6.refs_3_, ...), custom_call_target="tpu_custom_call" | custom-call | tf_op jit(solution)/shard_map/pallas_call | solution.py:183
  116.5 23.6 %collective-permute-done.10 = bf16[128,8192]{1,0:T(8,128)(2,1)} collective-permute-done((bf16[128,8192]{1,0:T(8,128)(2,1)S(1)}, bf16[128,8192]{1,0:T(8,128)(2,1)}, u32[]{:S(2)}, u32[]{:S(2)}) %collective-permute-start.10) | collective-permute-done | bytes 2097184 | tf_op jit(solution)/shard_map/ppermute | solution.py:24
  140.0 16.0 %all-to-all-done.1 = bf16[8,16,8192]{2,1,0:T(8,128)(2,1)S(1)} async-done(((bf16[8,16,8192]{2,1,0:T(8,128)(2,1)}), bf16[8,16,8192]{2,1,0:T(8,128)(2,1)S(1)}, u32[]{:S(2)}, u32[]{:S(2)}) %all-to-all-start.1) | async-done | bytes 2097184 | tf_op jit(solution)/shard_map/all_to_all | solution.py:35
  156.0 4.5 %all-to-all-start.2 = ((bf16[8,16,8192]{2,1,0:T(8,128)(2,1)}), bf16[8,16,8192]{2,1,0:T(8,128)(2,1)}, u32[]{:S(2)}, u32[]{:S(2)}) async-start(bf16[8,16,8192]{2,1,0:T(8,128)(2,1)} %bitcast.20), calls=%async_computation.2 | async-start | bytes 4194304 | tf_op jit(solution)/shard_map/all_to_all | solution.py:35
  160.5 1.5 shard_map.108
  162.1 14.2 %collective-permute-done.9.value_ref = bf16[64,8192]{1,0:T(8,128)(2,1)S(1)} collective-permute-done((bf16[64,8192]{1,0:T(8,128)(2,1)S(1)}, bf16[64,8192]{1,0:T(8,128)(2,1)S(1)}, u32[]{:S(2)}, u32[]{:S(2)}) %collective-permute-start.9) | collective-permute-done | bytes 1048608 | tf_op jit(solution)/shard_map/ppermute | solution.py:24
  177.3 2.0 shard_map.109
  179.3 29.0 %all-to-all-done.2 = bf16[8,16,8192]{2,1,0:T(8,128)(2,1)} async-done(((bf16[8,16,8192]{2,1,0:T(8,128)(2,1)}), bf16[8,16,8192]{2,1,0:T(8,128)(2,1)}, u32[]{:S(2)}, u32[]{:S(2)}) %all-to-all-start.2) | async-done | bytes 2097184 | tf_op jit(solution)/shard_map/all_to_all | solution.py:35
  208.3 3.2 %shard_map.111 = bf16[64,8192]{1,0:T(8,128)(2,1)} custom-call(s32[25]{0:T(128)S(1)} %copy-done.11, bf16[64,8192]{1,0:T(8,128)(2,1)S(1)} %copy-done.3, bf16[128,8192]{1,0:T(8,128)(2,1)} %bitcast.21.parts_ref), custom_call_target="tpu_custom_call" | custom-call | tf_op jit(solution)/shard_map/pallas_call | solution.py:83
  (46 shorter events, 10.7 us)
Async XLA Ops:
  3.1 9.9 %copy-start.13 = (bf16[1,64,8192]{2,1,0:T(8,128)(2,1)S(1)}, bf16[1,64,8192]{2,1,0:T(8,128)(2,1)}, u32[]{:S(2)}) copy-start(bf16[1,64,8192]{2,1,0:T(8,128)(2,1)} %param.10) | copy-start | bytes 3145732
  3.1 45.1 %copy-start.15 = (s32[1,32,8]{1,2,0:T(8,128)S(1)}, s32[1,32,8]{1,2,0:T(8,128)}, u32[]{:S(2)}) copy-start(s32[1,32,8]{1,2,0:T(8,128)} %param.17) | copy-start | bytes 3076
  3.1 80.9 %all-to-all-start = ((bf16[8,16,8192]{2,1,0:T(8,128)(2,1)}), bf16[8,16,8192]{2,1,0:T(8,128)(2,1)S(1)}, u32[]{:S(2)}, u32[]{:S(2)}) async-start(bf16[8,16,8192]{2,1,0:T(8,128)(2,1)} %bitcast.30), calls=%async_computation | async-start | bytes 4194304 | tf_op jit(solution)/shard_map/all_to_all | solution.py:35
  13.0 13.0 %collective-permute-start.1 = (bf16[64,8192]{1,0:T(8,128)(2,1)S(1)}, bf16[64,8192]{1,0:T(8,128)(2,1)S(1)}, u32[]{:S(2)}, u32[]{:S(2)}) collective-permute-start(bf16[64,8192]{1,0:T(8,128)(2,1)S(1)} %bitcast.39), channel_id=1, source_target_pairs={{0,24},{8,0},{16,8},{24,16},{1,25},{9,1},{17,9},{25,17},{2,26},{10... | collective-permute-start | bytes 3145736 | tf_op jit(solution)/shard_map/ppermute | solution.py:24
  27.0 18.0 %collective-permute-start.2 = (bf16[16,8192]{1,0:T(8,128)(2,1)}, bf16[16,8192]{1,0:T(8,128)(2,1)S(1)}, u32[]{:S(2)}, u32[]{:S(2)}) collective-permute-start(bf16[16,8192]{1,0:T(8,128)(2,1)} %get-tuple-element.34), channel_id=1, source_target_pairs={{0,1},{1,0},{2,3},{3,2},{4,5},{5,4},{6,7},{7,6},{8,9},{9,8},{10,11... | collective-permute-start | bytes 786440 | tf_op jit(solution)/shard_map/ppermute | solution.py:29
  45.0 12.1 %collective-permute-start.3 = (bf16[16,8192]{1,0:T(8,128)(2,1)}, bf16[16,8192]{1,0:T(8,128)(2,1)S(1)}, u32[]{:S(2)}, u32[]{:S(2)}) collective-permute-start(bf16[16,8192]{1,0:T(8,128)(2,1)} %get-tuple-element.35), channel_id=1, source_target_pairs={{0,7},{1,6},{2,5},{3,4},{4,3},{5,2},{6,1},{7,0},{8,15},{9,14},{10,... | collective-permute-start | bytes 786440 | tf_op jit(solution)/shard_map/ppermute | solution.py:29
  48.2 4.8 %collective-permute-start = (s32[32,8]{0,1:T(8,128)S(1)}, s32[32,8]{0,1:T(8,128)S(1)}, u32[]{:S(2)}, u32[]{:S(2)}) collective-permute-start(s32[32,8]{0,1:T(8,128)S(1)} %bitcast.45), channel_id=1, source_target_pairs={{0,24},{8,0},{16,8},{24,16},{1,25},{9,1},{17,9},{25,17},{2,26},{10... | collective-permute-start | bytes 3080 | tf_op jit(solution)/shard_map/ppermute | solution.py:24
  49.3 42.5 %collective-permute-start.7 = (bf16[16,8192]{1,0:T(8,128)(2,1)}, bf16[16,8192]{1,0:T(8,128)(2,1)S(1)}, u32[]{:S(2)}, u32[]{:S(2)}) collective-permute-start(bf16[16,8192]{1,0:T(8,128)(2,1)} %get-tuple-element.45), channel_id=1, source_target_pairs={{0,3},{1,2},{2,1},{3,0},{4,7},{5,6},{6,5},{7,4},{8,11},{9,10},{10,... | collective-permute-start | bytes 786440 | tf_op jit(solution)/shard_map/ppermute | solution.py:29
  49.3 42.5 %collective-permute-start.8 = (bf16[16,8192]{1,0:T(8,128)(2,1)}, bf16[16,8192]{1,0:T(8,128)(2,1)S(1)}, u32[]{:S(2)}, u32[]{:S(2)}) collective-permute-start(bf16[16,8192]{1,0:T(8,128)(2,1)} %get-tuple-element.47), channel_id=1, source_target_pairs={{0,2},{1,3},{2,0},{3,1},{4,6},{5,7},{6,4},{7,5},{8,10},{9,11},{10,... | collective-permute-start | bytes 786440 | tf_op jit(solution)/shard_map/ppermute | solution.py:29
  53.0 38.7 %collective-permute-start.4 = (bf16[16,8192]{1,0:T(8,128)(2,1)}, bf16[16,8192]{1,0:T(8,128)(2,1)S(1)}, u32[]{:S(2)}, u32[]{:S(2)}) collective-permute-start(bf16[16,8192]{1,0:T(8,128)(2,1)} %get-tuple-element.39), channel_id=1, source_target_pairs={{0,6},{1,7},{2,4},{3,5},{4,2},{5,3},{6,0},{7,1},{8,14},{9,15},{10,... | collective-permute-start | bytes 786440 | tf_op jit(solution)/shard_map/ppermute | solution.py:29
  53.1 29.3 %copy-start.16 = (s32[32,8]{0,1:T(8,128)}, s32[32,8]{0,1:T(8,128)S(1)}, u32[]{:S(2)}) copy-start(s32[32,8]{0,1:T(8,128)S(1)} %collective-permute-done) | copy-start | bytes 3076
  53.1 47.3 %collective-permute-start.5 = (bf16[16,8192]{1,0:T(8,128)(2,1)}, bf16[16,8192]{1,0:T(8,128)(2,1)}, u32[]{:S(2)}, u32[]{:S(2)}) collective-permute-start(bf16[16,8192]{1,0:T(8,128)(2,1)} %get-tuple-element.41), channel_id=1, source_target_pairs={{0,5},{1,4},{2,7},{3,6},{4,1},{5,0},{6,3},{7,2},{8,13},{9,12},{10,... | collective-permute-start | bytes 786440 | tf_op jit(solution)/shard_map/ppermute | solution.py:29
  57.1 46.7 %collective-permute-start.6 = (bf16[16,8192]{1,0:T(8,128)(2,1)}, bf16[16,8192]{1,0:T(8,128)(2,1)}, u32[]{:S(2)}, u32[]{:S(2)}) collective-permute-start(bf16[16,8192]{1,0:T(8,128)(2,1)} %get-tuple-element.43), channel_id=1, source_target_pairs={{0,4},{1,5},{2,6},{3,7},{4,0},{5,1},{6,2},{7,3},{8,12},{9,13},{10,... | collective-permute-start | bytes 786440 | tf_op jit(solution)/shard_map/ppermute | solution.py:29
  103.9 3.8 %copy-start.4 = (bf16[16,8192]{1,0:T(8,128)(2,1)S(1)}, bf16[16,8192]{1,0:T(8,128)(2,1)}, u32[]{:S(2)}) copy-start(bf16[16,8192]{1,0:T(8,128)(2,1)} %get-tuple-element.28.refs_7_) | copy-start | bytes 786436
  103.9 3.8 %copy-start.7 = (bf16[1,512,128]{2,1,0:T(8,128)(2,1)S(1)}, bf16[1,512,128]{2,1,0:T(8,128)(2,1)}, u32[]{:S(2)}) copy-start(bf16[1,512,128]{2,1,0:T(8,128)(2,1)} %param.14) | copy-start | bytes 393220
  103.9 3.8 %copy-start.12 = (s32[25]{0:T(128)S(1)}, s32[25]{0:T(128)}, u32[]{:S(2)}) copy-start(s32[25]{0:T(128)} %get-tuple-element.49.plan_ref) | copy-start | bytes 304
  103.9 52.1 %all-to-all-start.1 = ((bf16[8,16,8192]{2,1,0:T(8,128)(2,1)}), bf16[8,16,8192]{2,1,0:T(8,128)(2,1)S(1)}, u32[]{:S(2)}, u32[]{:S(2)}) async-start(bf16[8,16,8192]{2,1,0:T(8,128)(2,1)} %bitcast.25), calls=%async_computation.1 | async-start | bytes 4194304 | tf_op jit(solution)/shard_map/all_to_all | solution.py:35
  115.6 24.4 %collective-permute-start.10 = (bf16[128,8192]{1,0:T(8,128)(2,1)S(1)}, bf16[128,8192]{1,0:T(8,128)(2,1)}, u32[]{:S(2)}, u32[]{:S(2)}) collective-permute-start(bf16[128,8192]{1,0:T(8,128)(2,1)S(1)} %shard_map.110), channel_id=1, source_target_pairs={{0,24},{8,0},{16,8},{24,16},{1,25},{9,1},{17,9},{25,17},{2,26},{10... | collective-permute-start | bytes 6291464 | tf_op jit(solution)/shard_map/ppermute | solution.py:24
  156.0 4.5 %copy-start.1 = (bf16[1,64,8192]{2,1,0:T(8,128)(2,1)S(1)}, bf16[1,64,8192]{2,1,0:T(8,128)(2,1)}, u32[]{:S(2)}) copy-start(bf16[1,64,8192]{2,1,0:T(8,128)(2,1)} %param.9) | copy-start | bytes 3145732
  156.0 4.5 %copy-start.10 = (s32[25]{0:T(128)S(1)}, s32[25]{0:T(128)}, u32[]{:S(2)}) copy-start(s32[25]{0:T(128)} %get-tuple-element.30.plan_ref) | copy-start | bytes 304
  156.0 52.3 %all-to-all-start.2 = ((bf16[8,16,8192]{2,1,0:T(8,128)(2,1)}), bf16[8,16,8192]{2,1,0:T(8,128)(2,1)}, u32[]{:S(2)}, u32[]{:S(2)}) async-start(bf16[8,16,8192]{2,1,0:T(8,128)(2,1)} %bitcast.20), calls=%async_computation.2 | async-start | bytes 4194304 | tf_op jit(solution)/shard_map/all_to_all | solution.py:35
  162.0 46.3 %copy-start.3 = (bf16[64,8192]{1,0:T(8,128)(2,1)S(1)}, bf16[64,8192]{1,0:T(8,128)(2,1)}, u32[]{:S(2)}) copy-start(bf16[64,8192]{1,0:T(8,128)(2,1)} %copy-done.2) | copy-start | bytes 3145732
  162.0 46.3 %copy-start.11 = (s32[25]{0:T(128)S(1)}, s32[25]{0:T(128)}, u32[]{:S(2)}) copy-start(s32[25]{0:T(128)} %get-tuple-element.36.plan_ref) | copy-start | bytes 304
  162.0 14.3 %collective-permute-start.9 = (bf16[64,8192]{1,0:T(8,128)(2,1)S(1)}, bf16[64,8192]{1,0:T(8,128)(2,1)S(1)}, u32[]{:S(2)}, u32[]{:S(2)}) collective-permute-start(bf16[64,8192]{1,0:T(8,128)(2,1)S(1)} %shard_map.108), channel_id=1, source_target_pairs={{0,8},{8,16},{16,24},{24,0},{1,9},{9,17},{17,25},{25,1},{2,10},{10... | collective-permute-start | bytes 3145736 | tf_op jit(solution)/shard_map/ppermute | solution.py:24
  (7 other events, 6.5 us)

commit v6 on v5

--- a/solution.py
+++ b/solution.py
@@ -8,7 +8,7 @@
 BLOCK = 16
 OUT, HAS, SAVED = range(3)
 FIELDS = 3
-VMEM_LIMIT = 48 * 1024 * 1024
+VMEM_LIMIT = 60 * 1024 * 1024
 VMEM_MOST = 60 * 1024 * 1024
 VMEM_LEAST = 16 * 1024 * 1024
 PLACE_CHUNK = 4096

time: 212 us -> 212 us (level)
  local copies, waits for them, and re-layouts: 6.54 us -> 3.29 us
  Pallas kernels: 25.1 us -> 28.1 us
    unnamed x34 -> x30, local copies, waits for them, and re-layouts: 6.54 us -> 3.29 us
    pallas_call x2, Pallas kernels: 11.8 us -> 14.8 us  [middle(): pl.pallas_call(kernel, out_shape=jax.ShapeDtypeStruct((height, width), jn...]
  transfers between devices with their start and end apart: 14 -> 14, of which waited for: 9 -> 9; matrix products, arithmetic and copies ran while one was open for 0% -> 0% of each run, Pallas kernels for 9% -> 11%
where the time goes in v6:
time: 212 us; the launch traced here: 211 us
  waiting for transfers between devices  125 us (59%)
  starting transfers between devices  53.9 us (25%)
  Pallas kernels  28.1 us (13%)
  local copies, waits for them, and re-layouts  3.29 us (2%)
    ppermute x4, waiting for transfers between devices, shifted(): lax.ppermute(value, 'pipe', [(p, (p + steps) % count) for p in range(coun...  50.4 us
    all_to_all x3, waiting for transfers between devices, swap(): lax.all_to_all(pieces, 'bundle', split_axis=0, concat_axis=0, tiled=True)  45.1 us
    ppermute x7, starting transfers between devices, permute(): lax.ppermute(piece, 'bundle', [(b, b ^ offset) for b in range(count)])  35.8 us
    ppermute x7, waiting for transfers between devices, permute(): lax.ppermute(piece, 'bundle', [(b, b ^ offset) for b in range(count)])  29.9 us
    all_to_all x3, starting transfers between devices, swap(): lax.all_to_all(pieces, 'bundle', split_axis=0, concat_axis=0, tiled=True)  15.5 us
    pallas_call x2, Pallas kernels, middle(): pl.pallas_call(kernel, out_shape=jax.ShapeDtypeStruct((height, width), jn...  14.8 us
    pallas_call x2, Pallas kernels, pack(): pl.pallas_call(kernel, out_shape=[jax.ShapeDtypeStruct((r, width), jnp.bf...  4.93 us
    pallas_call x2, Pallas kernels, chunked(): pl.pallas_call(kernel, out_shape=jax.ShapeDtypeStruct((out_rows, width),...  4.71 us
  transfers between devices with their start and end apart: 14, of which 9 were waited for; matrix products, arithmetic and copies ran while one was open for 0% of the time, Pallas kernels for 11%

profile of v6, /device:TPU:0, one launch (start us, length us, event | category | flops | bytes accessed | tf_op | source)
XLA Modules:
  0.0 211.5 jit_solution(17306758991929179994)
XLA Ops:
  0.6 2.5 %shard_map.104 = bf16[128,8192]{1,0:T(8,128)(2,1)} custom-call(s32[1]{0:T(128)} %bitcast.dev_ref, s32[8,32]{1,0:T(8,128)} %bitcast.41, bf16[64,8192]{1,0:T(8,128)(2,1)} %bitcast.24), custom_call_target="tpu_custom_call" | custom-call | tf_op jit(solution)/shard_map/pallas_call | solution.py:115
  3.1 7.4 %all-to-all-start = ((bf16[8,16,8192]{2,1,0:T(8,128)(2,1)}), bf16[8,16,8192]{2,1,0:T(8,128)(2,1)S(1)}, u32[]{:S(2)}, u32[]{:S(2)}) async-start(bf16[8,16,8192]{2,1,0:T(8,128)(2,1)} %bitcast.26), calls=%async_computation | async-start | bytes 4194304 | tf_op jit(solution)/shard_map/all_to_all | solution.py:35
  10.5 2.4 %shard_map.105 = (bf16[16,8192]{1,0:T(8,128)(2,1)}, bf16[16,8192]{1,0:T(8,128)(2,1)}, bf16[16,8192]{1,0:T(8,128)(2,1)}, bf16[16,8192]{1,0:T(8,128)(2,1)}, bf16[1...) custom-call(s32[1]{0:T(128)} %bitcast.dev_ref, ...), custom_call_target="tpu_custom_call" | custom-call | tf_op jit(solution)/shard_map/pallas_call | solution.py:115
  13.7 12.3 %collective-permute-done.1.base_ref = bf16[64,8192]{1,0:T(8,128)(2,1)S(1)} collective-permute-done((bf16[64,8192]{1,0:T(8,128)(2,1)S(1)}, bf16[64,8192]{1,0:T(8,128)(2,1)S(1)}, u32[]{:S(2)}, u32[]{:S(2)}) %collective-permute-start.1) | collective-permute-done | bytes 1048608 | tf_op jit(solution)/shard_map/ppermute | solution.py:24
  27.0 1.7 collective-permute-start.2
  28.7 16.1 %collective-permute-done.2.refs_6_ = bf16[16,8192]{1,0:T(8,128)(2,1)S(1)} collective-permute-done((bf16[16,8192]{1,0:T(8,128)(2,1)}, bf16[16,8192]{1,0:T(8,128)(2,1)S(1)}, u32[]{:S(2)}, u32[]{:S(2)}) %collective-permute-start.2) | collective-permute-done | bytes 262176 | tf_op jit(solution)/shard_map/ppermute | solution.py:29
  44.8 3.4 %collective-permute-start.3 = (bf16[16,8192]{1,0:T(8,128)(2,1)}, bf16[16,8192]{1,0:T(8,128)(2,1)S(1)}, u32[]{:S(2)}, u32[]{:S(2)}) collective-permute-start(bf16[16,8192]{1,0:T(8,128)(2,1)} %get-tuple-element.35), channel_id=1, source_target_pairs={{0,7},{1,6},{2,5},{3,4},{4,3},{5,2},{6,1},{7,0},{8,15},{9,14},{10,... | collective-permute-start | bytes 786440 | tf_op jit(solution)/shard_map/ppermute | solution.py:29
  49.3 3.7 %collective-permute-start.8 = (bf16[16,8192]{1,0:T(8,128)(2,1)}, bf16[16,8192]{1,0:T(8,128)(2,1)S(1)}, u32[]{:S(2)}, u32[]{:S(2)}) collective-permute-start(bf16[16,8192]{1,0:T(8,128)(2,1)} %get-tuple-element.47), channel_id=1, source_target_pairs={{0,2},{1,3},{2,0},{3,1},{4,6},{5,7},{6,4},{7,5},{8,10},{9,11},{10,... | collective-permute-start | bytes 786440 | tf_op jit(solution)/shard_map/ppermute | solution.py:29
  54.5 2.5 %collective-permute-done.3.refs_0_ = bf16[16,8192]{1,0:T(8,128)(2,1)S(1)} collective-permute-done((bf16[16,8192]{1,0:T(8,128)(2,1)}, bf16[16,8192]{1,0:T(8,128)(2,1)S(1)}, u32[]{:S(2)}, u32[]{:S(2)}) %collective-permute-start.3) | collective-permute-done | bytes 262176 | tf_op jit(solution)/shard_map/ppermute | solution.py:29
  57.0 25.4 %collective-permute-start.6 = (bf16[16,8192]{1,0:T(8,128)(2,1)}, bf16[16,8192]{1,0:T(8,128)(2,1)}, u32[]{:S(2)}, u32[]{:S(2)}) collective-permute-start(bf16[16,8192]{1,0:T(8,128)(2,1)} %get-tuple-element.43), channel_id=1, source_target_pairs={{0,4},{1,5},{2,6},{3,7},{4,0},{5,1},{6,2},{7,3},{8,12},{9,13},{10,... | collective-permute-start | bytes 786440 | tf_op jit(solution)/shard_map/ppermute | solution.py:29
  82.4 1.6 shard_map.106
  85.3 7.2 %shard_map.107 = bf16[128,8192]{1,0:T(8,128)(2,1)} custom-call(s32[25]{0:T(128)} %get-tuple-element.30.plan_ref, bf16[128,8192]{1,0:T(8,128)(2,1)} %bitcast.27, bf16[8192,128]{1,0:T(8,128)(2,1)} %bitcast.29, bf16[8192,128]{1,0:T(8,128)(2,1)} %bitcast.31, bf16[128,8192]{1,0:T(8,128)(2,1)} %bitcast.33), custom_call_target="tpu_custom_call" | custom-call | tf_op jit(solution)/shard_map/pallas_call | solution.py:183
  92.6 7.8 %collective-permute-done.5.refs_2_ = bf16[16,8192]{1,0:T(8,128)(2,1)} collective-permute-done((bf16[16,8192]{1,0:T(8,128)(2,1)}, bf16[16,8192]{1,0:T(8,128)(2,1)}, u32[]{:S(2)}, u32[]{:S(2)}) %collective-permute-start.5) | collective-permute-done | bytes 262176 | tf_op jit(solution)/shard_map/ppermute | solution.py:29
  100.4 3.5 %collective-permute-done.6.refs_3_ = bf16[16,8192]{1,0:T(8,128)(2,1)} collective-permute-done((bf16[16,8192]{1,0:T(8,128)(2,1)}, bf16[16,8192]{1,0:T(8,128)(2,1)}, u32[]{:S(2)}, u32[]{:S(2)}) %collective-permute-start.6) | collective-permute-done | bytes 262176 | tf_op jit(solution)/shard_map/ppermute | solution.py:29
  103.9 3.6 %all-to-all-start.1 = ((bf16[8,16,8192]{2,1,0:T(8,128)(2,1)}), bf16[8,16,8192]{2,1,0:T(8,128)(2,1)S(1)}, u32[]{:S(2)}, u32[]{:S(2)}) async-start(bf16[8,16,8192]{2,1,0:T(8,128)(2,1)} %bitcast.28), calls=%async_computation.1 | async-start | bytes 4194304 | tf_op jit(solution)/shard_map/all_to_all | solution.py:35
  107.5 7.6 %shard_map.110 = bf16[128,8192]{1,0:T(8,128)(2,1)} custom-call(s32[25]{0:T(128)} %get-tuple-element.49.plan_ref, bf16[16,8192]{1,0:T(8,128)(2,1)} %copy-done.9, bf16[16,8192]{1,0:T(8,128)(2,1)} %copy-done.12, bf16[16,8192]{1,0:T(8,128)(2,1)} %collective-permute-done.5.refs_2_, bf16[16,8192]{1,0:T(8,128)(2,1)} %collective-permute-done.6.refs_3_, ...), custom_call_target="tpu_custom_call" | custom-call | tf_op jit(solution)/shard_map/pallas_call | solution.py:183
  116.0 23.9 %collective-permute-done.10 = bf16[128,8192]{1,0:T(8,128)(2,1)} collective-permute-done((bf16[128,8192]{1,0:T(8,128)(2,1)}, bf16[128,8192]{1,0:T(8,128)(2,1)}, u32[]{:S(2)}, u32[]{:S(2)}) %collective-permute-start.10) | collective-permute-done | bytes 2097184 | tf_op jit(solution)/shard_map/ppermute | solution.py:24
  139.8 16.1 %all-to-all-done.1 = bf16[8,16,8192]{2,1,0:T(8,128)(2,1)S(1)} async-done(((bf16[8,16,8192]{2,1,0:T(8,128)(2,1)}), bf16[8,16,8192]{2,1,0:T(8,128)(2,1)S(1)}, u32[]{:S(2)}, u32[]{:S(2)}) %all-to-all-start.1) | async-done | bytes 2097184 | tf_op jit(solution)/shard_map/all_to_all | solution.py:35
  155.9 4.5 %all-to-all-start.2 = ((bf16[8,16,8192]{2,1,0:T(8,128)(2,1)}), bf16[8,16,8192]{2,1,0:T(8,128)(2,1)}, u32[]{:S(2)}, u32[]{:S(2)}) async-start(bf16[8,16,8192]{2,1,0:T(8,128)(2,1)} %bitcast.20), calls=%async_computation.2 | async-start | bytes 4194304 | tf_op jit(solution)/shard_map/all_to_all | solution.py:35
  160.4 1.5 shard_map.108
  162.0 14.2 %collective-permute-done.9.value_ref = bf16[64,8192]{1,0:T(8,128)(2,1)S(1)} collective-permute-done((bf16[64,8192]{1,0:T(8,128)(2,1)S(1)}, bf16[64,8192]{1,0:T(8,128)(2,1)S(1)}, u32[]{:S(2)}, u32[]{:S(2)}) %collective-permute-start.9) | collective-permute-done | bytes 1048608 | tf_op jit(solution)/shard_map/ppermute | solution.py:24
  177.2 2.0 shard_map.109
  179.2 29.0 %all-to-all-done.2 = bf16[8,16,8192]{2,1,0:T(8,128)(2,1)} async-done(((bf16[8,16,8192]{2,1,0:T(8,128)(2,1)}), bf16[8,16,8192]{2,1,0:T(8,128)(2,1)}, u32[]{:S(2)}, u32[]{:S(2)}) %all-to-all-start.2) | async-done | bytes 2097184 | tf_op jit(solution)/shard_map/all_to_all | solution.py:35
  208.2 3.2 %shard_map.111 = bf16[64,8192]{1,0:T(8,128)(2,1)} custom-call(s32[25]{0:T(128)S(1)} %copy-done.4, bf16[64,8192]{1,0:T(8,128)(2,1)S(1)} %copy-done.2, bf16[128,8192]{1,0:T(8,128)(2,1)} %bitcast.21.parts_ref), custom_call_target="tpu_custom_call" | custom-call | tf_op jit(solution)/shard_map/pallas_call | solution.py:83
  (42 shorter events, 7.4 us)
Async XLA Ops:
  3.1 9.9 %copy-start.6 = (bf16[1,64,8192]{2,1,0:T(8,128)(2,1)S(1)}, bf16[1,64,8192]{2,1,0:T(8,128)(2,1)}, u32[]{:S(2)}) copy-start(bf16[1,64,8192]{2,1,0:T(8,128)(2,1)} %param.10) | copy-start | bytes 3145732
  3.1 45.1 %copy-start.13 = (s32[1,32,8]{1,2,0:T(8,128)S(1)}, s32[1,32,8]{1,2,0:T(8,128)}, u32[]{:S(2)}) copy-start(s32[1,32,8]{1,2,0:T(8,128)} %param.17) | copy-start | bytes 3076
  3.1 80.9 %all-to-all-start = ((bf16[8,16,8192]{2,1,0:T(8,128)(2,1)}), bf16[8,16,8192]{2,1,0:T(8,128)(2,1)S(1)}, u32[]{:S(2)}, u32[]{:S(2)}) async-start(bf16[8,16,8192]{2,1,0:T(8,128)(2,1)} %bitcast.26), calls=%async_computation | async-start | bytes 4194304 | tf_op jit(solution)/shard_map/all_to_all | solution.py:35
  13.0 13.0 %collective-permute-start.1 = (bf16[64,8192]{1,0:T(8,128)(2,1)S(1)}, bf16[64,8192]{1,0:T(8,128)(2,1)S(1)}, u32[]{:S(2)}, u32[]{:S(2)}) collective-permute-start(bf16[64,8192]{1,0:T(8,128)(2,1)S(1)} %bitcast.37), channel_id=1, source_target_pairs={{0,24},{8,0},{16,8},{24,16},{1,25},{9,1},{17,9},{25,17},{2,26},{10... | collective-permute-start | bytes 3145736 | tf_op jit(solution)/shard_map/ppermute | solution.py:24
  27.0 17.8 %collective-permute-start.2 = (bf16[16,8192]{1,0:T(8,128)(2,1)}, bf16[16,8192]{1,0:T(8,128)(2,1)S(1)}, u32[]{:S(2)}, u32[]{:S(2)}) collective-permute-start(bf16[16,8192]{1,0:T(8,128)(2,1)} %get-tuple-element.34), channel_id=1, source_target_pairs={{0,1},{1,0},{2,3},{3,2},{4,5},{5,4},{6,7},{7,6},{8,9},{9,8},{10,11... | collective-permute-start | bytes 786440 | tf_op jit(solution)/shard_map/ppermute | solution.py:29
  44.8 59.1 %copy-start.8 = (bf16[16,8192]{1,0:T(8,128)(2,1)}, bf16[16,8192]{1,0:T(8,128)(2,1)S(1)}, u32[]{:S(2)}) copy-start(bf16[16,8192]{1,0:T(8,128)(2,1)S(1)} %collective-permute-done.2.refs_6_) | copy-start | bytes 786436
  44.8 12.2 %collective-permute-start.3 = (bf16[16,8192]{1,0:T(8,128)(2,1)}, bf16[16,8192]{1,0:T(8,128)(2,1)S(1)}, u32[]{:S(2)}, u32[]{:S(2)}) collective-permute-start(bf16[16,8192]{1,0:T(8,128)(2,1)} %get-tuple-element.35), channel_id=1, source_target_pairs={{0,7},{1,6},{2,5},{3,4},{4,3},{5,2},{6,1},{7,0},{8,15},{9,14},{10,... | collective-permute-start | bytes 786440 | tf_op jit(solution)/shard_map/ppermute | solution.py:29
  48.2 4.8 %collective-permute-start = (s32[32,8]{0,1:T(8,128)S(1)}, s32[32,8]{0,1:T(8,128)S(1)}, u32[]{:S(2)}, u32[]{:S(2)}) collective-permute-start(s32[32,8]{0,1:T(8,128)S(1)} %bitcast.45), channel_id=1, source_target_pairs={{0,24},{8,0},{16,8},{24,16},{1,25},{9,1},{17,9},{25,17},{2,26},{10... | collective-permute-start | bytes 3080 | tf_op jit(solution)/shard_map/ppermute | solution.py:24
  49.3 43.2 %collective-permute-start.7 = (bf16[16,8192]{1,0:T(8,128)(2,1)}, bf16[16,8192]{1,0:T(8,128)(2,1)S(1)}, u32[]{:S(2)}, u32[]{:S(2)}) collective-permute-start(bf16[16,8192]{1,0:T(8,128)(2,1)} %get-tuple-element.45), channel_id=1, source_target_pairs={{0,3},{1,2},{2,1},{3,0},{4,7},{5,6},{6,5},{7,4},{8,11},{9,10},{10,... | collective-permute-start | bytes 786440 | tf_op jit(solution)/shard_map/ppermute | solution.py:29
  49.3 43.2 %collective-permute-start.8 = (bf16[16,8192]{1,0:T(8,128)(2,1)}, bf16[16,8192]{1,0:T(8,128)(2,1)S(1)}, u32[]{:S(2)}, u32[]{:S(2)}) collective-permute-start(bf16[16,8192]{1,0:T(8,128)(2,1)} %get-tuple-element.47), channel_id=1, source_target_pairs={{0,2},{1,3},{2,0},{3,1},{4,6},{5,7},{6,4},{7,5},{8,10},{9,11},{10,... | collective-permute-start | bytes 786440 | tf_op jit(solution)/shard_map/ppermute | solution.py:29
  53.0 39.5 %collective-permute-start.4 = (bf16[16,8192]{1,0:T(8,128)(2,1)}, bf16[16,8192]{1,0:T(8,128)(2,1)S(1)}, u32[]{:S(2)}, u32[]{:S(2)}) collective-permute-start(bf16[16,8192]{1,0:T(8,128)(2,1)} %get-tuple-element.39), channel_id=1, source_target_pairs={{0,6},{1,7},{2,4},{3,5},{4,2},{5,3},{6,0},{7,1},{8,14},{9,15},{10,... | collective-permute-start | bytes 786440 | tf_op jit(solution)/shard_map/ppermute | solution.py:29
  53.0 29.3 %copy-start.14 = (s32[32,8]{0,1:T(8,128)}, s32[32,8]{0,1:T(8,128)S(1)}, u32[]{:S(2)}) copy-start(s32[32,8]{0,1:T(8,128)S(1)} %collective-permute-done) | copy-start | bytes 3076
  53.0 47.3 %collective-permute-start.5 = (bf16[16,8192]{1,0:T(8,128)(2,1)}, bf16[16,8192]{1,0:T(8,128)(2,1)}, u32[]{:S(2)}, u32[]{:S(2)}) collective-permute-start(bf16[16,8192]{1,0:T(8,128)(2,1)} %get-tuple-element.41), channel_id=1, source_target_pairs={{0,5},{1,4},{2,7},{3,6},{4,1},{5,0},{6,3},{7,2},{8,13},{9,12},{10,... | collective-permute-start | bytes 786440 | tf_op jit(solution)/shard_map/ppermute | solution.py:29
  57.0 46.9 %copy-start.9 = (bf16[16,8192]{1,0:T(8,128)(2,1)}, bf16[16,8192]{1,0:T(8,128)(2,1)S(1)}, u32[]{:S(2)}) copy-start(bf16[16,8192]{1,0:T(8,128)(2,1)S(1)} %collective-permute-done.3.refs_0_) | copy-start | bytes 786436
  57.0 46.9 %collective-permute-start.6 = (bf16[16,8192]{1,0:T(8,128)(2,1)}, bf16[16,8192]{1,0:T(8,128)(2,1)}, u32[]{:S(2)}, u32[]{:S(2)}) collective-permute-start(bf16[16,8192]{1,0:T(8,128)(2,1)} %get-tuple-element.43), channel_id=1, source_target_pairs={{0,4},{1,5},{2,6},{3,7},{4,0},{5,1},{6,2},{7,3},{8,12},{9,13},{10,... | collective-permute-start | bytes 786440 | tf_op jit(solution)/shard_map/ppermute | solution.py:29
  92.5 11.4 %copy-start.10 = (bf16[16,8192]{1,0:T(8,128)(2,1)}, bf16[16,8192]{1,0:T(8,128)(2,1)S(1)}, u32[]{:S(2)}) copy-start(bf16[16,8192]{1,0:T(8,128)(2,1)S(1)} %collective-permute-done.7.refs_4_) | copy-start | bytes 786436
  92.5 11.3 %copy-start.11 = (bf16[16,8192]{1,0:T(8,128)(2,1)}, bf16[16,8192]{1,0:T(8,128)(2,1)S(1)}, u32[]{:S(2)}) copy-start(bf16[16,8192]{1,0:T(8,128)(2,1)S(1)} %collective-permute-done.8.refs_5_) | copy-start | bytes 786436
  92.5 11.3 %copy-start.12 = (bf16[16,8192]{1,0:T(8,128)(2,1)}, bf16[16,8192]{1,0:T(8,128)(2,1)S(1)}, u32[]{:S(2)}) copy-start(bf16[16,8192]{1,0:T(8,128)(2,1)S(1)} %collective-permute-done.4.refs_1_) | copy-start | bytes 786436
  103.9 52.0 %all-to-all-start.1 = ((bf16[8,16,8192]{2,1,0:T(8,128)(2,1)}), bf16[8,16,8192]{2,1,0:T(8,128)(2,1)S(1)}, u32[]{:S(2)}, u32[]{:S(2)}) async-start(bf16[8,16,8192]{2,1,0:T(8,128)(2,1)} %bitcast.28), calls=%async_computation.1 | async-start | bytes 4194304 | tf_op jit(solution)/shard_map/all_to_all | solution.py:35
  115.1 24.7 %collective-permute-start.10 = (bf16[128,8192]{1,0:T(8,128)(2,1)}, bf16[128,8192]{1,0:T(8,128)(2,1)}, u32[]{:S(2)}, u32[]{:S(2)}) collective-permute-start(bf16[128,8192]{1,0:T(8,128)(2,1)} %shard_map.110), channel_id=1, source_target_pairs={{0,24},{8,0},{16,8},{24,16},{1,25},{9,1},{17,9},{25,17},{2,26},{10... | collective-permute-start | bytes 6291464 | tf_op jit(solution)/shard_map/ppermute | solution.py:24
  155.9 52.3 %all-to-all-start.2 = ((bf16[8,16,8192]{2,1,0:T(8,128)(2,1)}), bf16[8,16,8192]{2,1,0:T(8,128)(2,1)}, u32[]{:S(2)}, u32[]{:S(2)}) async-start(bf16[8,16,8192]{2,1,0:T(8,128)(2,1)} %bitcast.20), calls=%async_computation.2 | async-start | bytes 4194304 | tf_op jit(solution)/shard_map/all_to_all | solution.py:35
  161.9 46.3 %copy-start.2 = (bf16[64,8192]{1,0:T(8,128)(2,1)S(1)}, bf16[64,8192]{1,0:T(8,128)(2,1)}, u32[]{:S(2)}) copy-start(bf16[64,8192]{1,0:T(8,128)(2,1)} %copy-done.1) | copy-start | bytes 3145732
  161.9 46.3 %copy-start.4 = (s32[25]{0:T(128)S(1)}, s32[25]{0:T(128)}, u32[]{:S(2)}) copy-start(s32[25]{0:T(128)} %get-tuple-element.36.plan_ref) | copy-start | bytes 304
  161.9 14.3 %collective-permute-start.9 = (bf16[64,8192]{1,0:T(8,128)(2,1)S(1)}, bf16[64,8192]{1,0:T(8,128)(2,1)S(1)}, u32[]{:S(2)}, u32[]{:S(2)}) collective-permute-start(bf16[64,8192]{1,0:T(8,128)(2,1)S(1)} %shard_map.108), channel_id=1, source_target_pairs={{0,8},{8,16},{16,24},{24,0},{1,9},{9,17},{17,25},{25,1},{2,10},{10... | collective-permute-start | bytes 3145736 | tf_op jit(solution)/shard_map/ppermute | solution.py:24
  (5 other events, 12.2 us)

commit v7 on v6

--- a/solution.py
+++ b/solution.py
@@ -10,7 +10,7 @@
 FIELDS = 3
 VMEM_LIMIT = 60 * 1024 * 1024
 VMEM_MOST = 60 * 1024 * 1024
-VMEM_LEAST = 16 * 1024 * 1024
+VMEM_LEAST = 10 * 1024 * 1024
 PLACE_CHUNK = 4096
 ACROSS = ((1,), (1,))
 

time: 212 us -> 212 us (level)
  no operation moved by 1% of the time
where the time goes in v7:
time: 212 us; the launch traced here: 211 us
  waiting for transfers between devices  125 us (59%)
  starting transfers between devices  53.9 us (25%)
  Pallas kernels  28.1 us (13%)
  local copies, waits for them, and re-layouts  3.29 us (2%)
    ppermute x4, waiting for transfers between devices, shifted(): lax.ppermute(value, 'pipe', [(p, (p + steps) % count) for p in range(coun...  50.4 us
    all_to_all x3, waiting for transfers between devices, swap(): lax.all_to_all(pieces, 'bundle', split_axis=0, concat_axis=0, tiled=True)  45.1 us
    ppermute x7, starting transfers between devices, permute(): lax.ppermute(piece, 'bundle', [(b, b ^ offset) for b in range(count)])  35.8 us
    ppermute x7, waiting for transfers between devices, permute(): lax.ppermute(piece, 'bundle', [(b, b ^ offset) for b in range(count)])  29.9 us
    all_to_all x3, starting transfers between devices, swap(): lax.all_to_all(pieces, 'bundle', split_axis=0, concat_axis=0, tiled=True)  15.5 us
    pallas_call x2, Pallas kernels, middle(): pl.pallas_call(kernel, out_shape=jax.ShapeDtypeStruct((height, width), jn...  14.8 us
    pallas_call x2, Pallas kernels, pack(): pl.pallas_call(kernel, out_shape=[jax.ShapeDtypeStruct((r, width), jnp.bf...  4.93 us
    pallas_call x2, Pallas kernels, chunked(): pl.pallas_call(kernel, out_shape=jax.ShapeDtypeStruct((out_rows, width),...  4.71 us
  transfers between devices with their start and end apart: 14, of which 9 were waited for; matrix products, arithmetic and copies ran while one was open for 0% of the time, Pallas kernels for 11%

profile of v7, /device:TPU:0, one launch (start us, length us, event | category | flops | bytes accessed | tf_op | source)
XLA Modules:
  0.0 211.5 jit_solution(5786221740751715284)
XLA Ops:
  0.6 2.5 %shard_map.104 = bf16[128,8192]{1,0:T(8,128)(2,1)} custom-call(s32[1]{0:T(128)} %bitcast.dev_ref, s32[8,32]{1,0:T(8,128)} %bitcast.41, bf16[64,8192]{1,0:T(8,128)(2,1)} %bitcast.24), custom_call_target="tpu_custom_call" | custom-call | tf_op jit(solution)/shard_map/pallas_call | solution.py:115
  3.1 7.4 %all-to-all-start = ((bf16[8,16,8192]{2,1,0:T(8,128)(2,1)}), bf16[8,16,8192]{2,1,0:T(8,128)(2,1)S(1)}, u32[]{:S(2)}, u32[]{:S(2)}) async-start(bf16[8,16,8192]{2,1,0:T(8,128)(2,1)} %bitcast.26), calls=%async_computation | async-start | bytes 4194304 | tf_op jit(solution)/shard_map/all_to_all | solution.py:35
  10.5 2.4 %shard_map.105 = (bf16[16,8192]{1,0:T(8,128)(2,1)}, bf16[16,8192]{1,0:T(8,128)(2,1)}, bf16[16,8192]{1,0:T(8,128)(2,1)}, bf16[16,8192]{1,0:T(8,128)(2,1)}, bf16[1...) custom-call(s32[1]{0:T(128)} %bitcast.dev_ref, ...), custom_call_target="tpu_custom_call" | custom-call | tf_op jit(solution)/shard_map/pallas_call | solution.py:115
  13.7 12.3 %collective-permute-done.1.base_ref = bf16[64,8192]{1,0:T(8,128)(2,1)S(1)} collective-permute-done((bf16[64,8192]{1,0:T(8,128)(2,1)S(1)}, bf16[64,8192]{1,0:T(8,128)(2,1)S(1)}, u32[]{:S(2)}, u32[]{:S(2)}) %collective-permute-start.1) | collective-permute-done | bytes 1048608 | tf_op jit(solution)/shard_map/ppermute | solution.py:24
  27.0 1.7 collective-permute-start.2
  28.7 16.1 %collective-permute-done.2.refs_6_ = bf16[16,8192]{1,0:T(8,128)(2,1)S(1)} collective-permute-done((bf16[16,8192]{1,0:T(8,128)(2,1)}, bf16[16,8192]{1,0:T(8,128)(2,1)S(1)}, u32[]{:S(2)}, u32[]{:S(2)}) %collective-permute-start.2) | collective-permute-done | bytes 262176 | tf_op jit(solution)/shard_map/ppermute | solution.py:29
  44.8 3.4 %collective-permute-start.3 = (bf16[16,8192]{1,0:T(8,128)(2,1)}, bf16[16,8192]{1,0:T(8,128)(2,1)S(1)}, u32[]{:S(2)}, u32[]{:S(2)}) collective-permute-start(bf16[16,8192]{1,0:T(8,128)(2,1)} %get-tuple-element.35), channel_id=1, source_target_pairs={{0,7},{1,6},{2,5},{3,4},{4,3},{5,2},{6,1},{7,0},{8,15},{9,14},{10,... | collective-permute-start | bytes 786440 | tf_op jit(solution)/shard_map/ppermute | solution.py:29
  49.3 3.7 %collective-permute-start.8 = (bf16[16,8192]{1,0:T(8,128)(2,1)}, bf16[16,8192]{1,0:T(8,128)(2,1)S(1)}, u32[]{:S(2)}, u32[]{:S(2)}) collective-permute-start(bf16[16,8192]{1,0:T(8,128)(2,1)} %get-tuple-element.47), channel_id=1, source_target_pairs={{0,2},{1,3},{2,0},{3,1},{4,6},{5,7},{6,4},{7,5},{8,10},{9,11},{10,... | collective-permute-start | bytes 786440 | tf_op jit(solution)/shard_map/ppermute | solution.py:29
  54.5 2.5 %collective-permute-done.3.refs_0_ = bf16[16,8192]{1,0:T(8,128)(2,1)S(1)} collective-permute-done((bf16[16,8192]{1,0:T(8,128)(2,1)}, bf16[16,8192]{1,0:T(8,128)(2,1)S(1)}, u32[]{:S(2)}, u32[]{:S(2)}) %collective-permute-start.3) | collective-permute-done | bytes 262176 | tf_op jit(solution)/shard_map/ppermute | solution.py:29
  57.0 25.4 %collective-permute-start.6 = (bf16[16,8192]{1,0:T(8,128)(2,1)}, bf16[16,8192]{1,0:T(8,128)(2,1)}, u32[]{:S(2)}, u32[]{:S(2)}) collective-permute-start(bf16[16,8192]{1,0:T(8,128)(2,1)} %get-tuple-element.43), channel_id=1, source_target_pairs={{0,4},{1,5},{2,6},{3,7},{4,0},{5,1},{6,2},{7,3},{8,12},{9,13},{10,... | collective-permute-start | bytes 786440 | tf_op jit(solution)/shard_map/ppermute | solution.py:29
  82.4 1.6 shard_map.106
  85.3 7.2 %shard_map.107 = bf16[128,8192]{1,0:T(8,128)(2,1)} custom-call(s32[25]{0:T(128)} %get-tuple-element.30.plan_ref, bf16[128,8192]{1,0:T(8,128)(2,1)} %bitcast.27, bf16[8192,128]{1,0:T(8,128)(2,1)} %bitcast.29, bf16[8192,128]{1,0:T(8,128)(2,1)} %bitcast.31, bf16[128,8192]{1,0:T(8,128)(2,1)} %bitcast.33), custom_call_target="tpu_custom_call" | custom-call | tf_op jit(solution)/shard_map/pallas_call | solution.py:183
  92.6 7.8 %collective-permute-done.5.refs_2_ = bf16[16,8192]{1,0:T(8,128)(2,1)} collective-permute-done((bf16[16,8192]{1,0:T(8,128)(2,1)}, bf16[16,8192]{1,0:T(8,128)(2,1)}, u32[]{:S(2)}, u32[]{:S(2)}) %collective-permute-start.5) | collective-permute-done | bytes 262176 | tf_op jit(solution)/shard_map/ppermute | solution.py:29
  100.4 3.5 %collective-permute-done.6.refs_3_ = bf16[16,8192]{1,0:T(8,128)(2,1)} collective-permute-done((bf16[16,8192]{1,0:T(8,128)(2,1)}, bf16[16,8192]{1,0:T(8,128)(2,1)}, u32[]{:S(2)}, u32[]{:S(2)}) %collective-permute-start.6) | collective-permute-done | bytes 262176 | tf_op jit(solution)/shard_map/ppermute | solution.py:29
  103.9 3.6 %all-to-all-start.1 = ((bf16[8,16,8192]{2,1,0:T(8,128)(2,1)}), bf16[8,16,8192]{2,1,0:T(8,128)(2,1)S(1)}, u32[]{:S(2)}, u32[]{:S(2)}) async-start(bf16[8,16,8192]{2,1,0:T(8,128)(2,1)} %bitcast.28), calls=%async_computation.1 | async-start | bytes 4194304 | tf_op jit(solution)/shard_map/all_to_all | solution.py:35
  107.5 7.6 %shard_map.110 = bf16[128,8192]{1,0:T(8,128)(2,1)} custom-call(s32[25]{0:T(128)} %get-tuple-element.49.plan_ref, bf16[16,8192]{1,0:T(8,128)(2,1)} %copy-done.9, bf16[16,8192]{1,0:T(8,128)(2,1)} %copy-done.12, bf16[16,8192]{1,0:T(8,128)(2,1)} %collective-permute-done.5.refs_2_, bf16[16,8192]{1,0:T(8,128)(2,1)} %collective-permute-done.6.refs_3_, ...), custom_call_target="tpu_custom_call" | custom-call | tf_op jit(solution)/shard_map/pallas_call | solution.py:183
  116.0 23.9 %collective-permute-done.10 = bf16[128,8192]{1,0:T(8,128)(2,1)} collective-permute-done((bf16[128,8192]{1,0:T(8,128)(2,1)}, bf16[128,8192]{1,0:T(8,128)(2,1)}, u32[]{:S(2)}, u32[]{:S(2)}) %collective-permute-start.10) | collective-permute-done | bytes 2097184 | tf_op jit(solution)/shard_map/ppermute | solution.py:24
  139.8 16.1 %all-to-all-done.1 = bf16[8,16,8192]{2,1,0:T(8,128)(2,1)S(1)} async-done(((bf16[8,16,8192]{2,1,0:T(8,128)(2,1)}), bf16[8,16,8192]{2,1,0:T(8,128)(2,1)S(1)}, u32[]{:S(2)}, u32[]{:S(2)}) %all-to-all-start.1) | async-done | bytes 2097184 | tf_op jit(solution)/shard_map/all_to_all | solution.py:35
  155.9 4.5 %all-to-all-start.2 = ((bf16[8,16,8192]{2,1,0:T(8,128)(2,1)}), bf16[8,16,8192]{2,1,0:T(8,128)(2,1)}, u32[]{:S(2)}, u32[]{:S(2)}) async-start(bf16[8,16,8192]{2,1,0:T(8,128)(2,1)} %bitcast.20), calls=%async_computation.2 | async-start | bytes 4194304 | tf_op jit(solution)/shard_map/all_to_all | solution.py:35
  160.4 1.5 shard_map.108
  162.0 14.2 %collective-permute-done.9.value_ref = bf16[64,8192]{1,0:T(8,128)(2,1)S(1)} collective-permute-done((bf16[64,8192]{1,0:T(8,128)(2,1)S(1)}, bf16[64,8192]{1,0:T(8,128)(2,1)S(1)}, u32[]{:S(2)}, u32[]{:S(2)}) %collective-permute-start.9) | collective-permute-done | bytes 1048608 | tf_op jit(solution)/shard_map/ppermute | solution.py:24
  177.2 2.0 shard_map.109
  179.2 29.0 %all-to-all-done.2 = bf16[8,16,8192]{2,1,0:T(8,128)(2,1)} async-done(((bf16[8,16,8192]{2,1,0:T(8,128)(2,1)}), bf16[8,16,8192]{2,1,0:T(8,128)(2,1)}, u32[]{:S(2)}, u32[]{:S(2)}) %all-to-all-start.2) | async-done | bytes 2097184 | tf_op jit(solution)/shard_map/all_to_all | solution.py:35
  208.2 3.2 %shard_map.111 = bf16[64,8192]{1,0:T(8,128)(2,1)} custom-call(s32[25]{0:T(128)S(1)} %copy-done.4, bf16[64,8192]{1,0:T(8,128)(2,1)S(1)} %copy-done.2, bf16[128,8192]{1,0:T(8,128)(2,1)} %bitcast.21.parts_ref), custom_call_target="tpu_custom_call" | custom-call | tf_op jit(solution)/shard_map/pallas_call | solution.py:83
  (42 shorter events, 7.4 us)
Async XLA Ops:
  3.1 9.9 %copy-start.6 = (bf16[1,64,8192]{2,1,0:T(8,128)(2,1)S(1)}, bf16[1,64,8192]{2,1,0:T(8,128)(2,1)}, u32[]{:S(2)}) copy-start(bf16[1,64,8192]{2,1,0:T(8,128)(2,1)} %param.10) | copy-start | bytes 3145732
  3.1 45.1 %copy-start.13 = (s32[1,32,8]{1,2,0:T(8,128)S(1)}, s32[1,32,8]{1,2,0:T(8,128)}, u32[]{:S(2)}) copy-start(s32[1,32,8]{1,2,0:T(8,128)} %param.17) | copy-start | bytes 3076
  3.1 80.9 %all-to-all-start = ((bf16[8,16,8192]{2,1,0:T(8,128)(2,1)}), bf16[8,16,8192]{2,1,0:T(8,128)(2,1)S(1)}, u32[]{:S(2)}, u32[]{:S(2)}) async-start(bf16[8,16,8192]{2,1,0:T(8,128)(2,1)} %bitcast.26), calls=%async_computation | async-start | bytes 4194304 | tf_op jit(solution)/shard_map/all_to_all | solution.py:35
  13.0 13.0 %collective-permute-start.1 = (bf16[64,8192]{1,0:T(8,128)(2,1)S(1)}, bf16[64,8192]{1,0:T(8,128)(2,1)S(1)}, u32[]{:S(2)}, u32[]{:S(2)}) collective-permute-start(bf16[64,8192]{1,0:T(8,128)(2,1)S(1)} %bitcast.37), channel_id=1, source_target_pairs={{0,24},{8,0},{16,8},{24,16},{1,25},{9,1},{17,9},{25,17},{2,26},{10... | collective-permute-start | bytes 3145736 | tf_op jit(solution)/shard_map/ppermute | solution.py:24
  27.0 17.8 %collective-permute-start.2 = (bf16[16,8192]{1,0:T(8,128)(2,1)}, bf16[16,8192]{1,0:T(8,128)(2,1)S(1)}, u32[]{:S(2)}, u32[]{:S(2)}) collective-permute-start(bf16[16,8192]{1,0:T(8,128)(2,1)} %get-tuple-element.34), channel_id=1, source_target_pairs={{0,1},{1,0},{2,3},{3,2},{4,5},{5,4},{6,7},{7,6},{8,9},{9,8},{10,11... | collective-permute-start | bytes 786440 | tf_op jit(solution)/shard_map/ppermute | solution.py:29
  44.8 59.1 %copy-start.8 = (bf16[16,8192]{1,0:T(8,128)(2,1)}, bf16[16,8192]{1,0:T(8,128)(2,1)S(1)}, u32[]{:S(2)}) copy-start(bf16[16,8192]{1,0:T(8,128)(2,1)S(1)} %collective-permute-done.2.refs_6_) | copy-start | bytes 786436
  44.8 12.2 %collective-permute-start.3 = (bf16[16,8192]{1,0:T(8,128)(2,1)}, bf16[16,8192]{1,0:T(8,128)(2,1)S(1)}, u32[]{:S(2)}, u32[]{:S(2)}) collective-permute-start(bf16[16,8192]{1,0:T(8,128)(2,1)} %get-tuple-element.35), channel_id=1, source_target_pairs={{0,7},{1,6},{2,5},{3,4},{4,3},{5,2},{6,1},{7,0},{8,15},{9,14},{10,... | collective-permute-start | bytes 786440 | tf_op jit(solution)/shard_map/ppermute | solution.py:29
  48.2 4.8 %collective-permute-start = (s32[32,8]{0,1:T(8,128)S(1)}, s32[32,8]{0,1:T(8,128)S(1)}, u32[]{:S(2)}, u32[]{:S(2)}) collective-permute-start(s32[32,8]{0,1:T(8,128)S(1)} %bitcast.45), channel_id=1, source_target_pairs={{0,24},{8,0},{16,8},{24,16},{1,25},{9,1},{17,9},{25,17},{2,26},{10... | collective-permute-start | bytes 3080 | tf_op jit(solution)/shard_map/ppermute | solution.py:24
  49.3 43.2 %collective-permute-start.7 = (bf16[16,8192]{1,0:T(8,128)(2,1)}, bf16[16,8192]{1,0:T(8,128)(2,1)S(1)}, u32[]{:S(2)}, u32[]{:S(2)}) collective-permute-start(bf16[16,8192]{1,0:T(8,128)(2,1)} %get-tuple-element.45), channel_id=1, source_target_pairs={{0,3},{1,2},{2,1},{3,0},{4,7},{5,6},{6,5},{7,4},{8,11},{9,10},{10,... | collective-permute-start | bytes 786440 | tf_op jit(solution)/shard_map/ppermute | solution.py:29
  49.3 43.2 %collective-permute-start.8 = (bf16[16,8192]{1,0:T(8,128)(2,1)}, bf16[16,8192]{1,0:T(8,128)(2,1)S(1)}, u32[]{:S(2)}, u32[]{:S(2)}) collective-permute-start(bf16[16,8192]{1,0:T(8,128)(2,1)} %get-tuple-element.47), channel_id=1, source_target_pairs={{0,2},{1,3},{2,0},{3,1},{4,6},{5,7},{6,4},{7,5},{8,10},{9,11},{10,... | collective-permute-start | bytes 786440 | tf_op jit(solution)/shard_map/ppermute | solution.py:29
  53.0 39.5 %collective-permute-start.4 = (bf16[16,8192]{1,0:T(8,128)(2,1)}, bf16[16,8192]{1,0:T(8,128)(2,1)S(1)}, u32[]{:S(2)}, u32[]{:S(2)}) collective-permute-start(bf16[16,8192]{1,0:T(8,128)(2,1)} %get-tuple-element.39), channel_id=1, source_target_pairs={{0,6},{1,7},{2,4},{3,5},{4,2},{5,3},{6,0},{7,1},{8,14},{9,15},{10,... | collective-permute-start | bytes 786440 | tf_op jit(solution)/shard_map/ppermute | solution.py:29
  53.0 29.3 %copy-start.14 = (s32[32,8]{0,1:T(8,128)}, s32[32,8]{0,1:T(8,128)S(1)}, u32[]{:S(2)}) copy-start(s32[32,8]{0,1:T(8,128)S(1)} %collective-permute-done) | copy-start | bytes 3076
  53.0 47.3 %collective-permute-start.5 = (bf16[16,8192]{1,0:T(8,128)(2,1)}, bf16[16,8192]{1,0:T(8,128)(2,1)}, u32[]{:S(2)}, u32[]{:S(2)}) collective-permute-start(bf16[16,8192]{1,0:T(8,128)(2,1)} %get-tuple-element.41), channel_id=1, source_target_pairs={{0,5},{1,4},{2,7},{3,6},{4,1},{5,0},{6,3},{7,2},{8,13},{9,12},{10,... | collective-permute-start | bytes 786440 | tf_op jit(solution)/shard_map/ppermute | solution.py:29
  57.0 46.9 %copy-start.9 = (bf16[16,8192]{1,0:T(8,128)(2,1)}, bf16[16,8192]{1,0:T(8,128)(2,1)S(1)}, u32[]{:S(2)}) copy-start(bf16[16,8192]{1,0:T(8,128)(2,1)S(1)} %collective-permute-done.3.refs_0_) | copy-start | bytes 786436
  57.0 46.9 %collective-permute-start.6 = (bf16[16,8192]{1,0:T(8,128)(2,1)}, bf16[16,8192]{1,0:T(8,128)(2,1)}, u32[]{:S(2)}, u32[]{:S(2)}) collective-permute-start(bf16[16,8192]{1,0:T(8,128)(2,1)} %get-tuple-element.43), channel_id=1, source_target_pairs={{0,4},{1,5},{2,6},{3,7},{4,0},{5,1},{6,2},{7,3},{8,12},{9,13},{10,... | collective-permute-start | bytes 786440 | tf_op jit(solution)/shard_map/ppermute | solution.py:29
  92.5 11.4 %copy-start.10 = (bf16[16,8192]{1,0:T(8,128)(2,1)}, bf16[16,8192]{1,0:T(8,128)(2,1)S(1)}, u32[]{:S(2)}) copy-start(bf16[16,8192]{1,0:T(8,128)(2,1)S(1)} %collective-permute-done.7.refs_4_) | copy-start | bytes 786436
  92.5 11.3 %copy-start.11 = (bf16[16,8192]{1,0:T(8,128)(2,1)}, bf16[16,8192]{1,0:T(8,128)(2,1)S(1)}, u32[]{:S(2)}) copy-start(bf16[16,8192]{1,0:T(8,128)(2,1)S(1)} %collective-permute-done.8.refs_5_) | copy-start | bytes 786436
  92.5 11.3 %copy-start.12 = (bf16[16,8192]{1,0:T(8,128)(2,1)}, bf16[16,8192]{1,0:T(8,128)(2,1)S(1)}, u32[]{:S(2)}) copy-start(bf16[16,8192]{1,0:T(8,128)(2,1)S(1)} %collective-permute-done.4.refs_1_) | copy-start | bytes 786436
  103.9 52.0 %all-to-all-start.1 = ((bf16[8,16,8192]{2,1,0:T(8,128)(2,1)}), bf16[8,16,8192]{2,1,0:T(8,128)(2,1)S(1)}, u32[]{:S(2)}, u32[]{:S(2)}) async-start(bf16[8,16,8192]{2,1,0:T(8,128)(2,1)} %bitcast.28), calls=%async_computation.1 | async-start | bytes 4194304 | tf_op jit(solution)/shard_map/all_to_all | solution.py:35
  115.1 24.7 %collective-permute-start.10 = (bf16[128,8192]{1,0:T(8,128)(2,1)}, bf16[128,8192]{1,0:T(8,128)(2,1)}, u32[]{:S(2)}, u32[]{:S(2)}) collective-permute-start(bf16[128,8192]{1,0:T(8,128)(2,1)} %shard_map.110), channel_id=1, source_target_pairs={{0,24},{8,0},{16,8},{24,16},{1,25},{9,1},{17,9},{25,17},{2,26},{10... | collective-permute-start | bytes 6291464 | tf_op jit(solution)/shard_map/ppermute | solution.py:24
  155.9 52.3 %all-to-all-start.2 = ((bf16[8,16,8192]{2,1,0:T(8,128)(2,1)}), bf16[8,16,8192]{2,1,0:T(8,128)(2,1)}, u32[]{:S(2)}, u32[]{:S(2)}) async-start(bf16[8,16,8192]{2,1,0:T(8,128)(2,1)} %bitcast.20), calls=%async_computation.2 | async-start | bytes 4194304 | tf_op jit(solution)/shard_map/all_to_all | solution.py:35
  161.9 46.3 %copy-start.2 = (bf16[64,8192]{1,0:T(8,128)(2,1)S(1)}, bf16[64,8192]{1,0:T(8,128)(2,1)}, u32[]{:S(2)}) copy-start(bf16[64,8192]{1,0:T(8,128)(2,1)} %copy-done.1) | copy-start | bytes 3145732
  161.9 46.3 %copy-start.4 = (s32[25]{0:T(128)S(1)}, s32[25]{0:T(128)}, u32[]{:S(2)}) copy-start(s32[25]{0:T(128)} %get-tuple-element.36.plan_ref) | copy-start | bytes 304
  161.9 14.3 %collective-permute-start.9 = (bf16[64,8192]{1,0:T(8,128)(2,1)S(1)}, bf16[64,8192]{1,0:T(8,128)(2,1)S(1)}, u32[]{:S(2)}, u32[]{:S(2)}) collective-permute-start(bf16[64,8192]{1,0:T(8,128)(2,1)S(1)} %shard_map.108), channel_id=1, source_target_pairs={{0,8},{8,16},{16,24},{24,0},{1,9},{9,17},{17,25},{25,1},{2,10},{10... | collective-permute-start | bytes 3145736 | tf_op jit(solution)/shard_map/ppermute | solution.py:24
  (5 other events, 12.2 us)
